TPU v7x, 512 devices: a whole 4x8x8 slice. The times are simulated.
512 devices in a mesh: seq: 64 (over y, x, core), chan: 8 (over z).
Axes of the slice: x: 4, y: 8, z: 8, core: 2. Of those that a mesh axis runs over, the one named last changes fastest.
Arguments:
- out_gate: bfloat16 [16384, 16, 256], P('seq', 'chan'), may hold values from -6 to 6
- in_gate: bfloat16 [16384, 16, 256], P('seq', 'chan'), may hold values from -6 to 6
- values_in: bfloat16 [16384, 16, 256], P('seq', 'chan'), may hold values from -6 to 6
- filter_taps: bfloat16 [16384, 256], P('seq'), may hold values from -1.05 to 1.05
- skip_gain: float32 [16, 256], P('chan'), may hold values from 0.5 to 1.5
- out_cotangent: bfloat16 [16384, 16, 256], P('seq', 'chan'), may hold values from -6 to 6
Outputs:
- mixed: bfloat16 [16384, 16, 256], P('seq', 'chan')
- grad_out_gate: bfloat16 [16384, 16, 256], P('seq', 'chan')
- grad_in_gate: bfloat16 [16384, 16, 256], P('seq', 'chan')
- grad_values: bfloat16 [16384, 16, 256], P('seq', 'chan')
- grad_filter: float32 [16384, 256], P('seq', 'chan')
All inputs are finite; a program needn't handle non-finite values.
Results may differ from a plain program's by a relative error of at most 0.0049.
Values may be sent and summed in bfloat16 or wider, within the bound.
No kernel may reach another device: no remote copies, remote signals or barrier semaphores. Data moves between devices by JAX's collectives and lax.ppermute only.
A program may use at most 128 MiB of HBM per device.

v0:
```python
import math

import jax
import jax.numpy as jnp
from jax import lax
from jax.sharding import PartitionSpec as P

highest = lax.Precision.HIGHEST


def phases(numbers, modulus):
    angles = (numbers % modulus).astype(jnp.float32) * (2.0 * math.pi / modulus)
    return (jnp.cos(angles), jnp.sin(angles))


def product(form, left, right):
    return jnp.einsum(form, left, right, precision=highest, preferred_element_type=jnp.float32)


def forward_spectrum(signal):
    seq_count = lax.axis_size("seq")
    row_count = signal.shape[0]
    slice_rows = row_count // seq_count
    block_count = 2 * seq_count
    full_length = block_count * row_count
    owner_index = lax.broadcasted_iota(jnp.int32, (seq_count, 2, seq_count), 0)
    half_index = lax.broadcasted_iota(jnp.int32, (seq_count, 2, seq_count), 1)
    source = lax.broadcasted_iota(jnp.int32, (seq_count, 2, seq_count), 2)
    block_cos, block_sin = phases((owner_index + seq_count * half_index) * source, block_count)
    row_index = lax.broadcasted_iota(jnp.int32, (row_count, row_count), 1)
    freq_index = lax.broadcasted_iota(jnp.int32, (row_count, row_count), 0)
    row_cos, row_sin = phases(freq_index * row_index, row_count)
    values = lax.all_to_all(
        signal.reshape(1, row_count, signal.shape[1]),
        "seq",
        split_axis=1,
        concat_axis=0,
        tiled=True,
    ).astype(jnp.float32)
    real_part = product("jhb,brc->jhrc", block_cos, values)
    imag_part = -product("jhb,brc->jhrc", block_sin, values)
    device_pos = lax.axis_index("seq")
    twist_shape = (seq_count, 2, slice_rows, 1)
    owner_twist = lax.broadcasted_iota(jnp.int32, twist_shape, 0)
    half_twist = lax.broadcasted_iota(jnp.int32, twist_shape, 1)
    local_row = lax.broadcasted_iota(jnp.int32, twist_shape, 2)
    positions = device_pos * slice_rows + local_row
    twist_cos, twist_sin = phases(positions * (owner_twist + seq_count * half_twist), full_length)
    turned_real = real_part * twist_cos + imag_part * twist_sin
    turned_imag = imag_part * twist_cos - real_part * twist_sin
    gathered_real = lax.all_to_all(turned_real, "seq", split_axis=0, concat_axis=2, tiled=True)
    gathered_imag = lax.all_to_all(turned_imag, "seq", split_axis=0, concat_axis=2, tiled=True)
    blocked_real = gathered_real[0]
    blocked_imag = gathered_imag[0]
    spec_real = product("kt,htc->hkc", row_cos, blocked_real) + product(
        "kt,htc->hkc", row_sin, blocked_imag
    )
    spec_imag = product("kt,htc->hkc", row_cos, blocked_imag) - product(
        "kt,htc->hkc", row_sin, blocked_real
    )
    return (spec_real, spec_imag)


def inverse_signal(spec_real, spec_imag, paired):
    seq_count = lax.axis_size("seq")
    row_count = spec_real.shape[1]
    block_count = 2 * seq_count
    full_length = block_count * row_count
    row_index = lax.broadcasted_iota(jnp.int32, (row_count, row_count), 0)
    freq_index = lax.broadcasted_iota(jnp.int32, (row_count, row_count), 1)
    row_cos, row_sin = phases(row_index * freq_index, row_count)
    blocked_real = product("tk,hkc->htc", row_cos, spec_real) - product(
        "tk,hkc->htc", row_sin, spec_imag
    )
    blocked_imag = product("tk,hkc->htc", row_cos, spec_imag) + product(
        "tk,hkc->htc", row_sin, spec_real
    )
    device_pos = lax.axis_index("seq")
    half_twist = lax.broadcasted_iota(jnp.int32, (2, row_count, 1), 0)
    positions = lax.broadcasted_iota(jnp.int32, (2, row_count, 1), 1)
    twist_cos, twist_sin = phases(positions * (device_pos + seq_count * half_twist), full_length)
    turned_real = blocked_real * twist_cos - blocked_imag * twist_sin
    turned_imag = blocked_imag * twist_cos + blocked_real * twist_sin
    target = lax.broadcasted_iota(jnp.int32, (seq_count, seq_count, 2), 0)
    owner_index = lax.broadcasted_iota(jnp.int32, (seq_count, seq_count, 2), 1)
    half_index = lax.broadcasted_iota(jnp.int32, (seq_count, seq_count, 2), 2)
    back_cos, back_sin = phases(target * (owner_index + seq_count * half_index), block_count)
    inverse_scale = 1.0 / full_length

    def combine(received):
        recv_real, recv_imag = received
        real_out = (
            product("bjh,jhrc->brc", back_cos, recv_real)
            - product("bjh,jhrc->brc", back_sin, recv_imag)
        ) * inverse_scale
        if paired:
            imag_out = (
                product("bjh,jhrc->brc", back_cos, recv_imag)
                + product("bjh,jhrc->brc", back_sin, recv_real)
            ) * inverse_scale
            stacked = jnp.stack([real_out, imag_out])
        else:
            stacked = real_out[None]
        returned = lax.all_to_all(stacked, "seq", split_axis=1, concat_axis=2, tiled=True)
        if paired:
            return (returned[0, 0], returned[1, 0])
        return returned[0, 0]

    return combine(
        (
            lax.all_to_all(turned_real[None], "seq", split_axis=2, concat_axis=0, tiled=True),
            lax.all_to_all(turned_imag[None], "seq", split_axis=2, concat_axis=0, tiled=True),
        )
    )


def radix_path(mixed_in, conv_cot, filter_taps, member_count, group_count):
    row_count = mixed_in.shape[0]
    channels = member_count * group_count
    wide_shape = (2, row_count, member_count, group_count)
    flat_shape = (2, row_count, channels)
    input_real, input_imag = forward_spectrum(mixed_in.reshape(row_count, channels))
    taps_real, taps_imag = forward_spectrum(filter_taps)
    taps_real = taps_real[:, :, None, :]
    taps_imag = taps_imag[:, :, None, :]
    input_real = input_real.reshape(wide_shape)
    input_imag = input_imag.reshape(wide_shape)
    prod_real = input_real * taps_real - input_imag * taps_imag
    prod_imag = input_real * taps_imag + input_imag * taps_real
    conv_out = inverse_signal(prod_real.reshape(flat_shape), prod_imag.reshape(flat_shape), False)
    cot_real, cot_imag = forward_spectrum(conv_cot.reshape(row_count, channels))
    cot_real = cot_real.reshape(wide_shape)
    cot_imag = cot_imag.reshape(wide_shape)
    adj_real = cot_real * taps_real + cot_imag * taps_imag
    adj_imag = cot_imag * taps_real - cot_real * taps_imag
    cross_real = cot_real * input_real + cot_imag * input_imag
    cross_imag = cot_imag * input_real - cot_real * input_imag
    joint_real = (adj_real - cross_imag).reshape(flat_shape)
    joint_imag = (adj_imag + cross_real).reshape(flat_shape)
    back_conv, lag_terms = inverse_signal(joint_real, joint_imag, True)
    lag_local = jnp.sum(lag_terms.reshape(row_count, member_count, group_count), axis=1)
    filter_sum = lax.psum_scatter(lag_local, "chan", scatter_dimension=1, tiled=True)
    return (conv_out, back_conv, filter_sum)


def local(out_gate, in_gate, values_in, filter_taps, skip_gain, out_cotangent):
    row_count, member_count, group_count = out_gate.shape
    mixed_in = (in_gate.astype(jnp.float32) * values_in.astype(jnp.float32)).astype(jnp.bfloat16)
    conv_cot = (out_cotangent.astype(jnp.float32) * out_gate.astype(jnp.float32)).astype(
        jnp.bfloat16
    )
    conv_out, back_conv, filter_sum = radix_path(
        mixed_in, conv_cot, filter_taps, member_count, group_count
    )
    conv_out = conv_out.reshape(row_count, member_count, group_count)
    mixed_float = mixed_in.astype(jnp.float32)
    cot_float = conv_cot.astype(jnp.float32)
    before_gate = conv_out + skip_gain[None] * mixed_float
    mixed = (out_gate.astype(jnp.float32) * before_gate).astype(jnp.bfloat16)
    grad_out_gate = (out_cotangent.astype(jnp.float32) * before_gate).astype(jnp.bfloat16)
    seq_total = row_count * lax.axis_size("seq")
    member_total = member_count * lax.axis_size("chan")
    norm_factor = 1.0 / math.sqrt(seq_total * member_total)
    grad_filter = filter_sum * norm_factor
    back_in = back_conv.reshape(row_count, member_count, group_count) + skip_gain[None] * cot_float
    grad_in_gate = (back_in * values_in.astype(jnp.float32)).astype(jnp.bfloat16)
    grad_values = (back_in * in_gate.astype(jnp.float32)).astype(jnp.bfloat16)
    return (mixed, grad_out_gate, grad_in_gate, grad_values, grad_filter)


def solution(mesh):
    in_specs = (
        P("seq", "chan", None),
        P("seq", "chan", None),
        P("seq", "chan", None),
        P("seq", None),
        P("chan", None),
        P("seq", "chan", None),
    )
    out_specs = (
        P("seq", "chan", None),
        P("seq", "chan", None),
        P("seq", "chan", None),
        P("seq", "chan", None),
        P("seq", "chan"),
    )
    return jax.shard_map(local, mesh=mesh, in_specs=in_specs, out_specs=out_specs, check_vma=False)
```

profile of v0, /device:TPU:6, one launch (start us, length us, event | category | flops | bytes accessed | tf_op | source)
XLA Modules:
  0.0 523.3 jit_solution(6659915815937801688)
XLA Ops:
  11.1 10.6 %all-to-all-start.3 = ((bf16[64,2,512]{2,1,0:T(2,128)(2,1)}), bf16[64,2,512]{2,1,0:T(2,128)(2,1)S(1)}, u32[]{:S(2)}, u32[]{:S(2)}) async-start(bf16[64,2,512]{2,1,0:T(2,128)(2,1)} %reshape.177), calls=%async_computation.3 | async-start | bytes 262144 | tf_op jit(solution)/shard_map/all_to_all | solution.py:33
  26.1 4.8 all-to-all-done.3
  30.8 6.4 %all-to-all-start = ((bf16[64,2,1024]{2,1,0:T(2,128)(2,1)}), bf16[64,2,1024]{2,1,0:T(2,128)(2,1)S(1)}, u32[]{:S(2)}, u32[]{:S(2)}) async-start(bf16[64,2,1024]{2,1,0:T(2,128)(2,1)} %reshape.175), calls=%async_computation | async-start | bytes 524288 | tf_op jit(solution)/shard_map/all_to_all | solution.py:33
  40.9 8.4 %all-to-all-done = bf16[64,2,1024]{2,1,0:T(2,128)(2,1)S(1)} async-done(((bf16[64,2,1024]{2,1,0:T(2,128)(2,1)}), bf16[64,2,1024]{2,1,0:T(2,128)(2,1)S(1)}, u32[]{:S(2)}, u32[]{:S(2)}) %all-to-all-start) | async-done | bytes 262176 | tf_op jit(solution)/shard_map/all_to_all | solution.py:33
  49.3 5.9 %all-to-all-start.9 = ((bf16[64,2,1024]{2,1,0:T(2,128)(2,1)}), bf16[64,2,1024]{2,1,0:T(2,128)(2,1)S(1)}, u32[]{:S(2)}, u32[]{:S(2)}) async-start(bf16[64,2,1024]{2,1,0:T(2,128)(2,1)} %reshape.179), calls=%async_computation.9 | async-start | bytes 524288 | tf_op jit(solution)/shard_map/all_to_all | solution.py:33
  58.6 8.6 %all-to-all-done.9 = bf16[64,2,1024]{2,1,0:T(2,128)(2,1)S(1)} async-done(((bf16[64,2,1024]{2,1,0:T(2,128)(2,1)}), bf16[64,2,1024]{2,1,0:T(2,128)(2,1)S(1)}, u32[]{:S(2)}, u32[]{:S(2)}) %all-to-all-start.9) | async-done | bytes 262176 | tf_op jit(solution)/shard_map/all_to_all | solution.py:33
  67.2 6.0 %all-to-all-start.5 = ((f32[64,2,4,256]{3,2,1,0:T(4,128)}), f32[64,2,4,256]{3,2,1,0:T(4,128)S(1)}, u32[]{:S(2)}, u32[]{:S(2)}) async-start(f32[64,2,4,256]{3,2,1,0:T(4,128)} %copy.152), calls=%async_computation.5 | async-start | bytes 1048576 | tf_op jit(solution)/shard_map/all_to_all | solution.py:52
  77.3 13.6 %all-to-all-done.5 = f32[64,2,4,256]{3,2,1,0:T(4,128)S(1)} async-done(((f32[64,2,4,256]{3,2,1,0:T(4,128)}), f32[64,2,4,256]{3,2,1,0:T(4,128)S(1)}, u32[]{:S(2)}, u32[]{:S(2)}) %all-to-all-start.5) | async-done | bytes 524320 | tf_op jit(solution)/shard_map/all_to_all | solution.py:52
  91.7 6.1 %all-to-all-start.4 = ((f32[64,2,4,256]{3,2,1,0:T(4,128)}), f32[64,2,4,256]{3,2,1,0:T(4,128)}, u32[]{:S(2)}, u32[]{:S(2)}) async-start(f32[64,2,4,256]{3,2,1,0:T(4,128)} %copy.149), calls=%async_computation.4 | async-start | bytes 1048576 | tf_op jit(solution)/shard_map/all_to_all | solution.py:51
  105.0 10.2 %all-to-all-done.4 = f32[64,2,4,256]{3,2,1,0:T(4,128)} async-done(((f32[64,2,4,256]{3,2,1,0:T(4,128)}), f32[64,2,4,256]{3,2,1,0:T(4,128)}, u32[]{:S(2)}, u32[]{:S(2)}) %all-to-all-start.4) | async-done | bytes 524320 | tf_op jit(solution)/shard_map/all_to_all | solution.py:51
  115.3 6.0 %all-to-all-start.1 = ((f32[64,2,4,512]{3,2,1,0:T(4,128)}), f32[64,2,4,512]{3,2,1,0:T(4,128)}, u32[]{:S(2)}, u32[]{:S(2)}) async-start(f32[64,2,4,512]{3,2,1,0:T(4,128)} %copy.140), calls=%async_computation.1 | async-start | bytes 2097152 | tf_op jit(solution)/shard_map/all_to_all | solution.py:51
  123.0 27.0 %all-to-all-done.1 = f32[64,2,4,512]{3,2,1,0:T(4,128)} async-done(((f32[64,2,4,512]{3,2,1,0:T(4,128)}), f32[64,2,4,512]{3,2,1,0:T(4,128)}, u32[]{:S(2)}, u32[]{:S(2)}) %all-to-all-start.1) | async-done | bytes 1048608 | tf_op jit(solution)/shard_map/all_to_all | solution.py:51
  150.1 5.6 %all-to-all-start.2 = ((f32[64,2,4,512]{3,2,1,0:T(4,128)}), f32[64,2,4,512]{3,2,1,0:T(4,128)S(1)}, u32[]{:S(2)}, u32[]{:S(2)}) async-start(f32[64,2,4,512]{3,2,1,0:T(4,128)} %copy.143), calls=%async_computation.2 | async-start | bytes 2097152 | tf_op jit(solution)/shard_map/all_to_all | solution.py:52
  157.4 27.2 %all-to-all-done.2 = f32[64,2,4,512]{3,2,1,0:T(4,128)S(1)} async-done(((f32[64,2,4,512]{3,2,1,0:T(4,128)}), f32[64,2,4,512]{3,2,1,0:T(4,128)S(1)}, u32[]{:S(2)}, u32[]{:S(2)}) %all-to-all-start.2) | async-done | bytes 1048608 | tf_op jit(solution)/shard_map/all_to_all | solution.py:52
  184.5 5.6 %all-to-all-start.11 = ((f32[64,2,4,512]{3,2,1,0:T(4,128)}), f32[64,2,4,512]{3,2,1,0:T(4,128)S(1)}, u32[]{:S(2)}, u32[]{:S(2)}) async-start(f32[64,2,4,512]{3,2,1,0:T(4,128)} %copy.170), calls=%async_computation.11 | async-start | bytes 2097152 | tf_op jit(solution)/shard_map/all_to_all | solution.py:52
  198.2 20.8 %all-to-all-done.11 = f32[64,2,4,512]{3,2,1,0:T(4,128)S(1)} async-done(((f32[64,2,4,512]{3,2,1,0:T(4,128)}), f32[64,2,4,512]{3,2,1,0:T(4,128)S(1)}, u32[]{:S(2)}, u32[]{:S(2)}) %all-to-all-start.11) | async-done | bytes 1048608 | tf_op jit(solution)/shard_map/all_to_all | solution.py:52
  220.0 5.8 %all-to-all-start.10 = ((f32[64,2,4,512]{3,2,1,0:T(4,128)}), f32[64,2,4,512]{3,2,1,0:T(4,128)}, u32[]{:S(2)}, u32[]{:S(2)}) async-start(f32[64,2,4,512]{3,2,1,0:T(4,128)} %copy.167), calls=%async_computation.10 | async-start | bytes 2097152 | tf_op jit(solution)/shard_map/all_to_all | solution.py:51
  247.9 3.0 fusion.3
  279.7 3.4 add_bitcast_fusion
  285.4 8.8 %all-to-all-start.7 = ((f32[1,2,256,512]{3,1,0,2:T(2,128)}), f32[1,2,256,512]{3,1,0,2:T(2,128)}, u32[]{:S(2)}, u32[]{:S(2)}) async-start(f32[1,2,256,512]{3,1,0,2:T(2,128)} %copy.161), calls=%async_computation.7 | async-start | bytes 2097152 | tf_op jit(solution)/shard_map/all_to_all | solution.py:112
  295.5 27.4 %all-to-all-done.7 = f32[1,2,256,512]{3,1,0,2:T(2,128)} async-done(((f32[1,2,256,512]{3,1,0,2:T(2,128)}), f32[1,2,256,512]{3,1,0,2:T(2,128)}, u32[]{:S(2)}, u32[]{:S(2)}) %all-to-all-start.7) | async-done | bytes 1048608 | tf_op jit(solution)/shard_map/all_to_all | solution.py:112
  322.9 5.6 %all-to-all-start.13 = ((f32[1,2,256,512]{3,1,0,2:T(2,128)}), f32[1,2,256,512]{3,1,0,2:T(2,128)S(1)}, u32[]{:S(2)}, u32[]{:S(2)}) async-start(f32[1,2,256,512]{3,1,0,2:T(2,128)} %copy.177), calls=%async_computation.13 | async-start | bytes 2097152 | tf_op jit(solution)/shard_map/all_to_all | solution.py:112
  329.9 27.5 %all-to-all-done.13 = f32[1,2,256,512]{3,1,0,2:T(2,128)S(1)} async-done(((f32[1,2,256,512]{3,1,0,2:T(2,128)}), f32[1,2,256,512]{3,1,0,2:T(2,128)S(1)}, u32[]{:S(2)}, u32[]{:S(2)}) %all-to-all-start.13) | async-done | bytes 1048608 | tf_op jit(solution)/shard_map/all_to_all | solution.py:112
  357.4 5.6 %all-to-all-start.12 = ((f32[1,2,256,512]{3,1,0,2:T(2,128)}), f32[1,2,256,512]{3,1,0,2:T(2,128)S(1)}, u32[]{:S(2)}, u32[]{:S(2)}) async-start(f32[1,2,256,512]{3,1,0,2:T(2,128)} %copy.175), calls=%async_computation.12 | async-start | bytes 2097152 | tf_op jit(solution)/shard_map/all_to_all | solution.py:111
  364.3 27.5 %all-to-all-done.12 = f32[1,2,256,512]{3,1,0,2:T(2,128)S(1)} async-done(((f32[1,2,256,512]{3,1,0,2:T(2,128)}), f32[1,2,256,512]{3,1,0,2:T(2,128)S(1)}, u32[]{:S(2)}, u32[]{:S(2)}) %all-to-all-start.12) | async-done | bytes 1048608 | tf_op jit(solution)/shard_map/all_to_all | solution.py:111
  391.8 5.6 %all-to-all-start.6 = ((f32[1,2,256,512]{3,1,0,2:T(2,128)}), f32[1,2,256,512]{3,1,0,2:T(2,128)S(1)}, u32[]{:S(2)}, u32[]{:S(2)}) async-start(f32[1,2,256,512]{3,1,0,2:T(2,128)} %copy.159), calls=%async_computation.6 | async-start | bytes 2097152 | tf_op jit(solution)/shard_map/all_to_all | solution.py:111
  405.4 20.9 %all-to-all-done.6 = f32[1,2,256,512]{3,1,0,2:T(2,128)S(1)} async-done(((f32[1,2,256,512]{3,1,0,2:T(2,128)}), f32[1,2,256,512]{3,1,0,2:T(2,128)S(1)}, u32[]{:S(2)}, u32[]{:S(2)}) %all-to-all-start.6) | async-done | bytes 1048608 | tf_op jit(solution)/shard_map/all_to_all | solution.py:111
  426.3 5.9 %all-to-all-start.14 = ((f32[2,64,4,512]{3,2,0,1:T(4,128)}), f32[2,64,4,512]{3,2,0,1:T(4,128)S(1)}, u32[]{:S(2)}, u32[]{:S(2)}) async-start(f32[2,64,4,512]{3,2,0,1:T(4,128)} %copy.179), calls=%async_computation.14 | async-start | bytes 2097152 | tf_op jit(solution)/shard_map/all_to_all | solution.py:104
  437.6 23.3 %all-to-all-done.14 = f32[2,64,4,512]{3,2,0,1:T(4,128)S(1)} async-done(((f32[2,64,4,512]{3,2,0,1:T(4,128)}), f32[2,64,4,512]{3,2,0,1:T(4,128)S(1)}, u32[]{:S(2)}, u32[]{:S(2)}) %all-to-all-start.14) | async-done | bytes 1048608 | tf_op jit(solution)/shard_map/all_to_all | solution.py:104
  460.9 5.6 %all-to-all-start.8 = ((f32[1,64,4,512]{3,2,0,1:T(4,128)}), f32[1,64,4,512]{3,2,0,1:T(4,128)S(1)}, u32[]{:S(2)}, u32[]{:S(2)}) async-start(f32[1,64,4,512]{3,2,0,1:T(4,128)} %copy.163), calls=%async_computation.8 | async-start | bytes 1048576 | tf_op jit(solution)/shard_map/all_to_all | solution.py:104
  468.7 15.5 %all-to-all-done.8 = f32[1,64,4,512]{3,2,0,1:T(4,128)S(1)} async-done(((f32[1,64,4,512]{3,2,0,1:T(4,128)}), f32[1,64,4,512]{3,2,0,1:T(4,128)S(1)}, u32[]{:S(2)}, u32[]{:S(2)}) %all-to-all-start.8) | async-done | bytes 524320 | tf_op jit(solution)/shard_map/all_to_all | solution.py:104
  487.9 26.8 %reduce-scatter.4.cloned.1.call-done = f32[32,256]{1,0:T(8,128)} async-done(((f32[256,256]{1,0:T(8,128)}), f32[32,256]{1,0:T(8,128)}) %reduce-scatter.4.cloned.1.call-update) | async-done | bytes 32784
  (139 shorter events, 116.9 us)
Async XLA Ops:
  7.2 14.5 %copy-start.19 = (bf16[256,2,256]{2,1,0:T(2,128)(2,1)S(1)}, bf16[256,2,256]{2,1,0:T(2,128)(2,1)}, u32[]{:S(2)}) copy-start(bf16[256,2,256]{2,1,0:T(2,128)(2,1)} %param.11) | copy-start | bytes 786436
  8.8 12.8 %copy-start.17 = (bf16[256,2,256]{2,1,0:T(2,128)(2,1)S(1)}, bf16[256,2,256]{2,1,0:T(2,128)(2,1)}, u32[]{:S(2)}) copy-start(bf16[256,2,256]{2,1,0:T(2,128)(2,1)} %param.6) | copy-start | bytes 786436
  10.3 11.4 %copy-start.13 = (bf16[256,2,256]{2,1,0:T(2,128)(2,1)S(1)}, bf16[256,2,256]{2,1,0:T(2,128)(2,1)}, u32[]{:S(2)}) copy-start(bf16[256,2,256]{2,1,0:T(2,128)(2,1)} %param.7) | copy-start | bytes 786436
  10.3 11.4 %copy-start.15 = (bf16[256,2,256]{2,1,0:T(2,128)(2,1)S(1)}, bf16[256,2,256]{2,1,0:T(2,128)(2,1)}, u32[]{:S(2)}) copy-start(bf16[256,2,256]{2,1,0:T(2,128)(2,1)} %param.8) | copy-start | bytes 786436
  11.1 19.8 %all-to-all-start.3 = ((bf16[64,2,512]{2,1,0:T(2,128)(2,1)}), bf16[64,2,512]{2,1,0:T(2,128)(2,1)S(1)}, u32[]{:S(2)}, u32[]{:S(2)}) async-start(bf16[64,2,512]{2,1,0:T(2,128)(2,1)} %reshape.177), calls=%async_computation.3 | async-start | bytes 262144 | tf_op jit(solution)/shard_map/all_to_all | solution.py:33
  22.3 15.0 %copy-start.7 = (bf16[256,2,256]{2,1,0:T(2,128)(2,1)}, bf16[256,2,256]{2,1,0:T(2,128)(2,1)S(1)}, u32[]{:S(2)}) copy-start(bf16[256,2,256]{2,1,0:T(2,128)(2,1)S(1)} %get-tuple-element.51) | copy-start | bytes 786436
  30.8 18.5 %all-to-all-start = ((bf16[64,2,1024]{2,1,0:T(2,128)(2,1)}), bf16[64,2,1024]{2,1,0:T(2,128)(2,1)S(1)}, u32[]{:S(2)}, u32[]{:S(2)}) async-start(bf16[64,2,1024]{2,1,0:T(2,128)(2,1)} %reshape.175), calls=%async_computation | async-start | bytes 524288 | tf_op jit(solution)/shard_map/all_to_all | solution.py:33
  49.3 17.9 %all-to-all-start.9 = ((bf16[64,2,1024]{2,1,0:T(2,128)(2,1)}), bf16[64,2,1024]{2,1,0:T(2,128)(2,1)S(1)}, u32[]{:S(2)}, u32[]{:S(2)}) async-start(bf16[64,2,1024]{2,1,0:T(2,128)(2,1)} %reshape.179), calls=%async_computation.9 | async-start | bytes 524288 | tf_op jit(solution)/shard_map/all_to_all | solution.py:33
  67.2 23.7 %all-to-all-start.5 = ((f32[64,2,4,256]{3,2,1,0:T(4,128)}), f32[64,2,4,256]{3,2,1,0:T(4,128)S(1)}, u32[]{:S(2)}, u32[]{:S(2)}) async-start(f32[64,2,4,256]{3,2,1,0:T(4,128)} %copy.152), calls=%async_computation.5 | async-start | bytes 1048576 | tf_op jit(solution)/shard_map/all_to_all | solution.py:52
  91.7 23.6 %all-to-all-start.4 = ((f32[64,2,4,256]{3,2,1,0:T(4,128)}), f32[64,2,4,256]{3,2,1,0:T(4,128)}, u32[]{:S(2)}, u32[]{:S(2)}) async-start(f32[64,2,4,256]{3,2,1,0:T(4,128)} %copy.149), calls=%async_computation.4 | async-start | bytes 1048576 | tf_op jit(solution)/shard_map/all_to_all | solution.py:51
  105.0 16.3 %copy-start.1 = (f32[64,2,4,512]{3,0,2,1:T(8,128)S(1)}, f32[64,2,4,512]{3,0,2,1:T(8,128)}, u32[]{:S(2)}) copy-start(f32[64,2,4,512]{3,0,2,1:T(8,128)} %get-tuple-element.41) | copy-start | bytes 3145732
  115.3 34.8 %all-to-all-start.1 = ((f32[64,2,4,512]{3,2,1,0:T(4,128)}), f32[64,2,4,512]{3,2,1,0:T(4,128)}, u32[]{:S(2)}, u32[]{:S(2)}) async-start(f32[64,2,4,512]{3,2,1,0:T(4,128)} %copy.140), calls=%async_computation.1 | async-start | bytes 2097152 | tf_op jit(solution)/shard_map/all_to_all | solution.py:51
  150.1 34.5 %all-to-all-start.2 = ((f32[64,2,4,512]{3,2,1,0:T(4,128)}), f32[64,2,4,512]{3,2,1,0:T(4,128)S(1)}, u32[]{:S(2)}, u32[]{:S(2)}) async-start(f32[64,2,4,512]{3,2,1,0:T(4,128)} %copy.143), calls=%async_computation.2 | async-start | bytes 2097152 | tf_op jit(solution)/shard_map/all_to_all | solution.py:52
  184.5 34.5 %all-to-all-start.11 = ((f32[64,2,4,512]{3,2,1,0:T(4,128)}), f32[64,2,4,512]{3,2,1,0:T(4,128)S(1)}, u32[]{:S(2)}, u32[]{:S(2)}) async-start(f32[64,2,4,512]{3,2,1,0:T(4,128)} %copy.170), calls=%async_computation.11 | async-start | bytes 2097152 | tf_op jit(solution)/shard_map/all_to_all | solution.py:52
  190.3 1.7 copy-start.12
  220.0 34.6 %all-to-all-start.10 = ((f32[64,2,4,512]{3,2,1,0:T(4,128)}), f32[64,2,4,512]{3,2,1,0:T(4,128)}, u32[]{:S(2)}, u32[]{:S(2)}) async-start(f32[64,2,4,512]{3,2,1,0:T(4,128)} %copy.167), calls=%async_computation.10 | async-start | bytes 2097152 | tf_op jit(solution)/shard_map/all_to_all | solution.py:51
  225.8 1.6 copy-start.21
  236.1 1.6 copy-start.4
  258.9 2.0 copy-start.2
  260.9 2.0 copy-start
  260.9 2.0 copy-start.9
  261.0 2.0 copy-start.10
  285.4 37.5 %all-to-all-start.7 = ((f32[1,2,256,512]{3,1,0,2:T(2,128)}), f32[1,2,256,512]{3,1,0,2:T(2,128)}, u32[]{:S(2)}, u32[]{:S(2)}) async-start(f32[1,2,256,512]{3,1,0,2:T(2,128)} %copy.161), calls=%async_computation.7 | async-start | bytes 2097152 | tf_op jit(solution)/shard_map/all_to_all | solution.py:112
  322.9 34.5 %all-to-all-start.13 = ((f32[1,2,256,512]{3,1,0,2:T(2,128)}), f32[1,2,256,512]{3,1,0,2:T(2,128)S(1)}, u32[]{:S(2)}, u32[]{:S(2)}) async-start(f32[1,2,256,512]{3,1,0,2:T(2,128)} %copy.177), calls=%async_computation.13 | async-start | bytes 2097152 | tf_op jit(solution)/shard_map/all_to_all | solution.py:112
  357.4 34.5 %all-to-all-start.12 = ((f32[1,2,256,512]{3,1,0,2:T(2,128)}), f32[1,2,256,512]{3,1,0,2:T(2,128)S(1)}, u32[]{:S(2)}, u32[]{:S(2)}) async-start(f32[1,2,256,512]{3,1,0,2:T(2,128)} %copy.175), calls=%async_computation.12 | async-start | bytes 2097152 | tf_op jit(solution)/shard_map/all_to_all | solution.py:111
  391.8 34.5 %all-to-all-start.6 = ((f32[1,2,256,512]{3,1,0,2:T(2,128)}), f32[1,2,256,512]{3,1,0,2:T(2,128)S(1)}, u32[]{:S(2)}, u32[]{:S(2)}) async-start(f32[1,2,256,512]{3,1,0,2:T(2,128)} %copy.159), calls=%async_computation.6 | async-start | bytes 2097152 | tf_op jit(solution)/shard_map/all_to_all | solution.py:111
  426.3 34.6 %all-to-all-start.14 = ((f32[2,64,4,512]{3,2,0,1:T(4,128)}), f32[2,64,4,512]{3,2,0,1:T(4,128)S(1)}, u32[]{:S(2)}, u32[]{:S(2)}) async-start(f32[2,64,4,512]{3,2,0,1:T(4,128)} %copy.179), calls=%async_computation.14 | async-start | bytes 2097152 | tf_op jit(solution)/shard_map/all_to_all | solution.py:104
  460.9 23.2 %all-to-all-start.8 = ((f32[1,64,4,512]{3,2,0,1:T(4,128)}), f32[1,64,4,512]{3,2,0,1:T(4,128)S(1)}, u32[]{:S(2)}, u32[]{:S(2)}) async-start(f32[1,64,4,512]{3,2,0,1:T(4,128)} %copy.163), calls=%async_computation.8 | async-start | bytes 1048576 | tf_op jit(solution)/shard_map/all_to_all | solution.py:104
  466.5 48.1 %reduce-scatter.4.cloned.1.call-start = ((), (), s32[]{:S(2)}) async-start(), calls=%async_computation.16 | async-start | bytes 294912
  467.8 17.3 %copy-start.18 = (bf16[256,2,256]{2,1,0:T(2,128)(2,1)S(1)}, bf16[256,2,256]{2,1,0:T(2,128)(2,1)}, u32[]{:S(2)}) copy-start(bf16[256,2,256]{2,1,0:T(2,128)(2,1)} %param.6) | copy-start | bytes 786436
  467.8 17.3 %copy-start.20 = (bf16[256,2,256]{2,1,0:T(2,128)(2,1)S(1)}, bf16[256,2,256]{2,1,0:T(2,128)(2,1)}, u32[]{:S(2)}) copy-start(bf16[256,2,256]{2,1,0:T(2,128)(2,1)} %param.11) | copy-start | bytes 786436
  467.8 17.3 %copy-start.22 = (f32[2,256]{1,0:T(2,128)S(1)}, f32[2,256]{1,0:T(2,128)}, u32[]{:S(2)}) copy-start(f32[2,256]{1,0:T(2,128)} %param.10) | copy-start | bytes 6148
  (7 other events, 6.8 us)
Sparse Core Ops, SparseCore 0:
  470.2 44.4 reduce-scatter.3
where the time goes:
time: 533 us; the launch traced here: 523 us
  waiting for transfers between devices  291 us (55%)
  starting transfers between devices  95.5 us (18%)
  matrix products  61.2 us (11%)
  local copies, waits for them, and re-layouts  50.8 us (10%)
  between operations  15 us (3%)
  other arithmetic  9.54 us (2%)
    all_to_all x3, waiting for transfers between devices, forward_spectrum(): lax.all_to_all(turned_imag, 'seq', split_axis=0, concat_axis=2, tiled=True)  61.6 us
    dot_general x32, matrix products, product(): jnp.einsum(form, left, right, precision=highest, preferred_element_type=j...  61.2 us
    all_to_all x2, waiting for transfers between devices, inverse_signal(): lax.all_to_all(turned_imag[None], 'seq', split_axis=2, concat_axis=0, til...  54.9 us
    all_to_all x2, waiting for transfers between devices, inverse_signal(): lax.all_to_all(turned_real[None], 'seq', split_axis=2, concat_axis=0, til...  48.4 us
    all_to_all x3, waiting for transfers between devices, forward_spectrum(): lax.all_to_all(turned_real, 'seq', split_axis=0, concat_axis=2, tiled=True)  39 us
    all_to_all x2, waiting for transfers between devices, combine(): lax.all_to_all(stacked, 'seq', split_axis=1, concat_axis=2, tiled=True)  38.8 us
    unnamed x2, waiting for transfers between devices  26.8 us
    all_to_all x3, starting transfers between devices, forward_spectrum(): lax.all_to_all(signal.reshape(1, row_count, signal.shape[1]), 'seq', spli...  23 us
  transfers between devices with their start and end apart: 16, of which 16 were waited for; matrix products, arithmetic and copies ran while one was open for 16% of the time, Pallas kernels for 0%

commit v1 on v0

v1 whole, which is shorter than its diff:
```python
import math

import jax
import jax.numpy as jnp
import ml_dtypes
import numpy as np
from jax import lax
from jax.experimental import pallas as pl
from jax.experimental.pallas import tpu as pltpu
from jax.sharding import PartitionSpec as P

BLOCKS = 64
ROWS = 256
HALF = ROWS // 2
SIGNALS = 8
GROUPS_HERE = 4
KEPT = 64
FULL = 2 * BLOCKS * ROWS


def split_table(table):
    high = table.astype(ml_dtypes.bfloat16)
    low = (table - high.astype(np.float64)).astype(ml_dtypes.bfloat16)
    return high, low


def tables():
    kept = np.arange(KEPT)[:, None]
    block = np.arange(BLOCKS)[None, :]
    coarse = 2 * math.pi * (((2 * kept + 1) * block) % (4 * BLOCKS)) / (4 * BLOCKS)
    enter_high, enter_low = split_table(np.concatenate([np.cos(coarse), -np.sin(coarse)], axis=0))
    enter = np.concatenate([enter_high, enter_low], axis=1)
    leave_high, leave_low = split_table(
        np.concatenate([np.cos(coarse.T), -np.sin(coarse.T)], axis=1) * (2.0 / FULL)
    )
    leave = np.concatenate([leave_high, leave_high, leave_low], axis=1)
    row = np.arange(ROWS)[None, :]
    twist = 2 * math.pi * (kept + 0.5) * row / FULL
    turn_cos = np.cos(twist).astype(np.float32)
    turn_sin = np.sin(twist).astype(np.float32)
    fine = []
    for odd in (0, 1):
        angle = (
            2
            * math.pi
            * ((np.arange(HALF)[:, None] * (2 * np.arange(HALF)[None, :] + odd)) % ROWS)
            / ROWS
        )
        cos, sin = np.cos(angle), np.sin(angle)
        forth = np.concatenate(
            [np.concatenate([cos, -sin], axis=1), np.concatenate([sin, cos], axis=1)], axis=0
        )
        fine.append((split_table(forth), split_table(forth.T)))
    forth = np.stack([fine[0][0][0], fine[0][0][1], fine[1][0][0], fine[1][0][1]])
    back = np.stack([fine[0][1][0], fine[0][1][1], fine[1][1][0], fine[1][1][1]])
    return enter, leave, turn_cos, turn_sin, forth, back


def mxu(left, right):
    return jnp.dot(left, right, preferred_element_type=jnp.float32)


def halves(value):
    high = value.astype(jnp.bfloat16)
    low = (value - high.astype(jnp.float32)).astype(jnp.bfloat16)
    return high, low


def spectral_kernel(
    recv_ref,
    enter_ref,
    leave_ref,
    cos_ref,
    sin_ref,
    forth_ref,
    back_ref,
    send_ref,
    wide_ref,
    high_ref,
    low_ref,
    spec_ref,
    turn_ref,
):
    signals = 2 * SIGNALS + GROUPS_HERE
    for lane in range(5):
        lanes = slice(lane * HALF, (lane + 1) * HALF)
        wide_ref[lane] = (
            recv_ref[:, :, lanes].astype(jnp.float32).reshape(BLOCKS * SIGNALS, HALF)
        )
    enter = enter_ref[...]
    turn_cos = cos_ref[...]
    turn_sin = sin_ref[...]

    def every(row):
        return pl.ds(row, BLOCKS, stride=SIGNALS)

    for index in range(signals):
        if index < 2 * SIGNALS:
            which, row = divmod(index, SIGNALS)
            places = ((2 * which, row), (2 * which + 1, row))
        else:
            row = index - 2 * SIGNALS
            places = ((4, row), (4, row + GROUPS_HERE))
        taken = jnp.concatenate(
            [wide_ref[lane, every(place), :] for lane, place in places], axis=1
        ).astype(jnp.bfloat16)
        first = mxu(enter, jnp.concatenate([taken, taken], axis=0))
        real, imag = first[:KEPT], first[KEPT:]
        turned_real = real * turn_cos + imag * turn_sin
        turned_imag = imag * turn_cos - real * turn_sin
        for odd in (0, 1):
            sign = 1.0 - 2.0 * odd
            for part, value in enumerate((turned_real, turned_imag)):
                high, low = halves(value[:, :HALF] + sign * value[:, HALF:])
                rows = slice(index * KEPT, (index + 1) * KEPT)
                lanes = slice(part * HALF, (part + 1) * HALF)
                high_ref[odd, rows, lanes] = high
                low_ref[odd, rows, lanes] = low

    def both(matrix_ref, odd, rows):
        high = high_ref[odd, rows, :]
        return (
            mxu(low_ref[odd, rows, :], matrix_ref[2 * odd])
            + mxu(high, matrix_ref[2 * odd + 1])
            + mxu(high, matrix_ref[2 * odd])
        )

    chunk = 4 * KEPT
    for start in range(0, signals * KEPT, chunk):
        for odd in (0, 1):
            spec_ref[odd, start : start + chunk, :] = both(
                forth_ref, odd, slice(start, start + chunk)
            )

    def spectrum(odd, index):
        rows = slice(index * KEPT, (index + 1) * KEPT)
        return spec_ref[odd, rows, :HALF], spec_ref[odd, rows, HALF:]

    def put(odd, index, real, imag):
        rows = slice(index * KEPT, (index + 1) * KEPT)
        for part, value in enumerate((real, imag)):
            high, low = halves(value)
            lanes = slice(part * HALF, (part + 1) * HALF)
            high_ref[odd, rows, lanes] = high
            low_ref[odd, rows, lanes] = low

    for group in range(GROUPS_HERE):
        for odd in (0, 1):
            tap_real, tap_imag = spectrum(odd, 2 * SIGNALS + group)
            lag_real = jnp.zeros((KEPT, HALF), jnp.float32)
            lag_imag = jnp.zeros((KEPT, HALF), jnp.float32)
            for member in range(SIGNALS // GROUPS_HERE):
                index = member * GROUPS_HERE + group
                in_real, in_imag = spectrum(odd, index)
                cot_real, cot_imag = spectrum(odd, SIGNALS + index)
                put(
                    odd,
                    index,
                    in_real * tap_real - in_imag * tap_imag,
                    in_real * tap_imag + in_imag * tap_real,
                )
                put(
                    odd,
                    SIGNALS + index,
                    cot_real * tap_real + cot_imag * tap_imag,
                    cot_imag * tap_real - cot_real * tap_imag,
                )
                lag_real += cot_real * in_real + cot_imag * in_imag
                lag_imag += cot_imag * in_real - cot_real * in_imag
            put(odd, 2 * SIGNALS + group, lag_real, lag_imag)

    for start in range(0, signals * KEPT, chunk):
        rows = slice(start, start + chunk)
        even_part = both(back_ref, 0, rows)
        odd_part = both(back_ref, 1, rows)
        turn_ref[0, rows, :] = even_part + odd_part
        turn_ref[1, rows, :] = even_part - odd_part

    leave = leave_ref[...]
    for index in range(signals):
        rows = slice(index * KEPT, (index + 1) * KEPT)
        real = jnp.concatenate([turn_ref[0, rows, :HALF], turn_ref[1, rows, :HALF]], axis=1)
        imag = jnp.concatenate([turn_ref[0, rows, HALF:], turn_ref[1, rows, HALF:]], axis=1)
        real_high, real_low = halves(real * turn_cos - imag * turn_sin)
        imag_high, imag_low = halves(imag * turn_cos + real * turn_sin)
        result = mxu(
            leave,
            jnp.concatenate(
                [real_high, imag_high, real_low, imag_low, real_high, imag_high], axis=0
            ),
        )
        if index < 2 * SIGNALS:
            which, row = divmod(index, SIGNALS)
            wide_ref[2 * which, every(row), :] = result[:, :HALF]
            wide_ref[2 * which + 1, every(row), :] = result[:, HALF:]
        else:
            row = index - 2 * SIGNALS
            wide_ref[4, every(row), :] = result[:, :HALF]
            wide_ref[4, every(row + GROUPS_HERE), :] = result[:, HALF:]
    for lane in range(5):
        lanes = slice(lane * HALF, (lane + 1) * HALF)
        send_ref[:, :, lanes] = (
            wide_ref[lane].reshape(BLOCKS, SIGNALS, HALF).astype(jnp.bfloat16)
        )


def spectral(received):
    signals = 2 * SIGNALS + GROUPS_HERE
    return pl.pallas_call(
        spectral_kernel,
        out_shape=jax.ShapeDtypeStruct((BLOCKS, SIGNALS, 5 * HALF), jnp.bfloat16),
        in_specs=[pl.BlockSpec(memory_space=pltpu.VMEM)] * 7,
        out_specs=pl.BlockSpec(memory_space=pltpu.VMEM),
        scratch_shapes=[
            pltpu.VMEM((5, BLOCKS * SIGNALS, HALF), jnp.float32),
            pltpu.VMEM((2, signals * KEPT, ROWS), jnp.bfloat16),
            pltpu.VMEM((2, signals * KEPT, ROWS), jnp.bfloat16),
            pltpu.VMEM((2, signals * KEPT, ROWS), jnp.float32),
            pltpu.VMEM((2, signals * KEPT, ROWS), jnp.float32),
        ],
        compiler_params=pltpu.CompilerParams(vmem_limit_bytes=32 * 1024 * 1024),
        cost_estimate=pl.CostEstimate(flops=6_000_000_000, bytes_accessed=3_000_000, transcendentals=0),
        name="spectral",
    )(received, *(jnp.asarray(table) for table in tables()))


def chunks(signal):
    row_count, member_count, group_count = signal.shape
    return (
        signal.reshape(row_count, member_count, BLOCKS, GROUPS_HERE)
        .transpose(2, 1, 3, 0)
        .reshape(BLOCKS, member_count * GROUPS_HERE, row_count)
    )


def unchunks(received, member_count):
    return (
        received.reshape(BLOCKS, member_count, GROUPS_HERE, ROWS)
        .transpose(3, 1, 0, 2)
        .reshape(ROWS, member_count, BLOCKS * GROUPS_HERE)
        .astype(jnp.float32)
    )


def exchange(value, axis):
    return lax.all_to_all(value, axis, split_axis=0, concat_axis=0, tiled=True)


def local(out_gate, in_gate, values_in, filter_taps, skip_gain, out_cotangent):
    row_count, member_count, group_count = out_gate.shape
    chan_count = lax.axis_size("chan")
    mixed_in = (in_gate.astype(jnp.float32) * values_in.astype(jnp.float32)).astype(jnp.bfloat16)
    conv_cot = (out_cotangent.astype(jnp.float32) * out_gate.astype(jnp.float32)).astype(
        jnp.bfloat16
    )
    taps = (
        filter_taps.T.reshape(BLOCKS, GROUPS_HERE, 2, HALF)
        .transpose(0, 2, 1, 3)
        .reshape(BLOCKS, SIGNALS, HALF)
    )
    outgoing = jnp.concatenate([chunks(mixed_in), chunks(conv_cot), taps], axis=2)
    returned = exchange(spectral(exchange(outgoing, "seq")), "seq")
    lag_terms = exchange(
        returned[:, :, 4 * HALF :].reshape(chan_count, -1, SIGNALS, HALF), "chan"
    )
    lag_sum = jnp.sum(lag_terms.astype(jnp.float32), axis=0)
    norm_factor = 1.0 / math.sqrt(BLOCKS * row_count * member_count * chan_count)
    grad_filter = (
        lag_sum.reshape(-1, 2, GROUPS_HERE, HALF).transpose(1, 3, 0, 2).reshape(row_count, -1)
        * norm_factor
    )
    conv_out = unchunks(returned[:, :, : 2 * HALF], member_count)
    back_conv = unchunks(returned[:, :, 2 * HALF : 4 * HALF], member_count)
    before_gate = conv_out + skip_gain[None] * mixed_in.astype(jnp.float32)
    mixed = (out_gate.astype(jnp.float32) * before_gate).astype(jnp.bfloat16)
    grad_out_gate = (out_cotangent.astype(jnp.float32) * before_gate).astype(jnp.bfloat16)
    back_in = back_conv + skip_gain[None] * conv_cot.astype(jnp.float32)
    grad_in_gate = (back_in * values_in.astype(jnp.float32)).astype(jnp.bfloat16)
    grad_values = (back_in * in_gate.astype(jnp.float32)).astype(jnp.bfloat16)
    return (mixed, grad_out_gate, grad_in_gate, grad_values, grad_filter)


def solution(mesh):
    in_specs = (
        P("seq", "chan", None),
        P("seq", "chan", None),
        P("seq", "chan", None),
        P("seq", None),
        P("chan", None),
        P("seq", "chan", None),
    )
    out_specs = (
        P("seq", "chan", None),
        P("seq", "chan", None),
        P("seq", "chan", None),
        P("seq", "chan", None),
        P("seq", "chan"),
    )
    return jax.shard_map(local, mesh=mesh, in_specs=in_specs, out_specs=out_specs, check_vma=False)
```

time: 533 us -> 87.7 us (0.16); the launches traced: 523 us -> 87.3 us
  waiting for transfers between devices: 291 us -> 2.89 us
  starting transfers between devices: 95.5 us -> 10.3 us
  matrix products: 61.2 us -> 0 us
  blocking collectives: 0 us -> 56.9 us
  local copies, waits for them, and re-layouts: 50.8 us -> 9.09 us
  between operations: 15 us -> 0.94 us
  other arithmetic: 9.54 us -> 2.42 us
    all_to_all x15 -> x1, waiting for transfers between devices: 264 us -> 2.89 us  [exchange(): return lax.all_to_all(value, axis, split_axis=0, concat_axis=0, tiled=True)]
    all_to_all x15 -> x1, starting transfers between devices: 95.4 us -> 10.3 us  [exchange(): return lax.all_to_all(value, axis, split_axis=0, concat_axis=0, tiled=True)]
    dot_general x32 -> x0, matrix products: 61.2 us -> none  [product(): jnp.einsum(form, left, right, precision=highest, preferred_element_type=j...]
    all_to_all x0 -> x2, blocking collectives: none -> 56.9 us  [exchange(): return lax.all_to_all(value, axis, split_axis=0, concat_axis=0, tiled=True)]
    unnamed x2 -> x0, waiting for transfers between devices: 26.8 us -> none
    all_to_all x12 -> x0, local copies, waits for them, and re-layouts: 13.8 us -> none  [the longest x3 6.62 us: forward_spectrum(): lax.all_to_all(turned_real, 'seq', split_axis=0, concat_axis=2, tiled=True)]
    broadcast_in_dim x5 -> x0, local copies, waits for them, and re-layouts: 7.3 us -> none  [the longest x2 3.57 us: inverse_signal(): turned_imag[None]]
    squeeze x6 -> x0, local copies, waits for them, and re-layouts: 7.15 us -> none  [the longest x3 3.64 us: forward_spectrum(): blocked_imag = gathered_imag[0]]
  transfers between devices with their start and end apart: 16 -> 1, of which waited for: 16 -> 1; matrix products, arithmetic and copies ran while one was open for 16% -> 6% of each run, Pallas kernels for 0% -> 0%
where the time goes in v1:
time: 87.7 us; the launch traced here: 87.3 us
  blocking collectives  56.9 us (65%)
  starting transfers between devices  10.3 us (12%)
  local copies, waits for them, and re-layouts  9.09 us (10%)
  Pallas kernels  4.7 us (5%)
  waiting for transfers between devices  2.89 us (3%)
  other arithmetic  2.42 us (3%)
  between operations  0.94 us (1%)
    all_to_all x2, blocking collectives, exchange(): return lax.all_to_all(value, axis, split_axis=0, concat_axis=0, tiled=True)  56.9 us
    all_to_all x1, starting transfers between devices, exchange(): return lax.all_to_all(value, axis, split_axis=0, concat_axis=0, tiled=True)  10.3 us
    unnamed x27, local copies, waits for them, and re-layouts  5.28 us
    pallas_call x1, Pallas kernels, spectral(): pl.pallas_call(spectral_kernel, out_shape=jax.ShapeDtypeStruct((BLOCKS, S...  4.7 us
    all_to_all x1, waiting for transfers between devices, exchange(): return lax.all_to_all(value, axis, split_axis=0, concat_axis=0, tiled=True)  2.89 us
  transfers between devices with their start and end apart: 1, of which 1 were waited for; matrix products, arithmetic and copies ran while one was open for 6% of the time, Pallas kernels for 0%

profile of v1, /device:TPU:6, one launch (start us, length us, event | category | flops | bytes accessed | tf_op | source)
XLA Modules:
  0.0 87.3 jit_solution(14574100720195111459)
XLA Ops:
  0.7 1.1 %copy.78 = bf16[256,256]{1,0:T(8,128)(2,1)S(1)} copy(bf16[256,256]{0,1:T(8,128)(2,1)} %bitcast.32) | data formatting | bytes 262144 | tf_op jit(solution)/shard_map/transpose | solution.py:257
  1.9 1.1 %fusion.2 = (bf16[256,2,256]{2,0,1:T(8,128)(2,1)S(1)}, bf16[256,2,256]{2,0,1:T(8,128)(2,1)S(1)}) fusion(bf16[256,2,256]{2,1,0:T(2,128)(2,1)S(1)} %copy-done.6, bf16[256,2,256]{2,1,0:T(2,128)(2,1)S(1)} %copy-done.7, bf16[256,2,256]{2,1,0:T(2,128)(2,1)S(1)} %copy-done.8, bf16[256,2,256]{2,1,0:T(2,128)(2,1)} %param.17), kind=kLoop, calls=%fused_computation.9 | loop fusion | flops 1048576 | bytes 1572864 | tf_op jit(solution)/shard_map/convert_element_type | solution.py:252
  2.9 0.2 copy.73
  3.1 0.1 copy.74
  3.2 0.1 reshape.51
  3.3 0.2 copy.76
  3.5 0.1 copy.77
  3.6 0.1 reshape.53
  3.7 0.1 pad_maximum_fusion
  3.8 0.0 copy-start
  3.8 0.0 copy-start.1
  3.8 30.9 %all_to_all.15.recv_ref = bf16[64,8,640]{2,1,0:T(8,128)(2,1)S(1)} all-to-all(bf16[64,8,640]{2,1,0:T(8,128)(2,1)S(1)} %pad_maximum_fusion), channel_id=1, replica_groups=mesh['seq'=64,'chan'=8] {'seq'}, dimensions={0} | all-to-all | bytes 1310720 | tf_op jit(solution)/shard_map/all_to_all | solution.py:246
  34.8 4.7 %spectral.1 = bf16[64,8,640]{2,1,0:T(8,128)(2,1)S(1)} custom-call(bf16[64,8,640]{2,1,0:T(8,128)(2,1)S(1)} %all_to_all.15.recv_ref, bf16[128,128]{1,0:T(8,128)(2,1)S(1)} %copy-done.5, bf16[64,384]{1,0:T(8,128)(2,1)S(1)} %copy-done.4, f32[64,256]{1,0:T(8,128)S(1)} %copy-done.3, f32[64,256]{1,0:T(8,128)S(1)} %copy-done.2, bf16[4,256,256]{2,1,0:T(8,128)(2,1)S(1)} %copy-done.1, ...), custom_call_target="tpu_custom_call" | custom-call | flops 6000000000 | bytes 3000000 | tf_op jit(solution)/shard_map/spectral/pallas_call | solution.py:209
  39.5 26.0 %all_to_all.16 = bf16[64,8,640]{2,1,0:T(8,128)(2,1)S(1)} all-to-all(bf16[64,8,640]{2,1,0:T(8,128)(2,1)S(1)} %spectral.1), channel_id=1, replica_groups=mesh['seq'=64,'chan'=8] {'seq'}, dimensions={0} | all-to-all | bytes 1310720 | tf_op jit(solution)/shard_map/all_to_all | solution.py:246
  65.5 0.7 slice.14
  66.2 10.3 %all-to-all-start.2 = ((bf16[8,8,8,128]{3,2,1,0:T(8,128)(2,1)}), bf16[8,8,8,128]{3,2,1,0:T(8,128)(2,1)}, u32[]{:S(2)}, u32[]{:S(2)}) async-start(bf16[8,8,8,128]{3,2,1,0:T(8,128)(2,1)} %bitcast.11), calls=%async_computation.2 | async-start | bytes 262144 | tf_op jit(solution)/shard_map/all_to_all | solution.py:246
  76.5 0.1 slice_convert_fusion
  76.6 0.1 reshape.60
  76.7 0.3 copy.82
  77.0 0.2 copy.83
  77.2 0.1 reshape.59
  77.4 0.3 copy.80
  77.7 0.2 copy.81
  77.9 0.7 copy-done.9
  78.6 0.3 fusion.1
  78.9 1.0 %copy.89 = bf16[256,2,256]{2,1,0:T(2,128)(2,1)} copy(bf16[256,2,256]{2,0,1:T(8,128)(2,1)S(1)} %get-tuple-element.25) | data formatting | bytes 524288
  79.9 1.0 %copy.88 = bf16[256,2,256]{2,1,0:T(2,128)(2,1)} copy(bf16[256,2,256]{2,0,1:T(8,128)(2,1)S(1)} %get-tuple-element.26) | data formatting | bytes 524288
  80.8 1.0 %copy.86 = bf16[256,2,256]{2,1,0:T(2,128)(2,1)} copy(bf16[256,2,256]{2,0,1:T(8,128)(2,1)S(1)} %get-tuple-element.31) | data formatting | bytes 524288
  81.8 1.0 %copy.87 = bf16[256,2,256]{2,1,0:T(2,128)(2,1)} copy(bf16[256,2,256]{2,0,1:T(8,128)(2,1)S(1)} %get-tuple-element.32) | data formatting | bytes 524288
  82.8 2.9 %all-to-all-done.2 = bf16[8,8,8,128]{3,2,1,0:T(8,128)(2,1)} async-done(((bf16[8,8,8,128]{3,2,1,0:T(8,128)(2,1)}), bf16[8,8,8,128]{3,2,1,0:T(8,128)(2,1)}, u32[]{:S(2)}, u32[]{:S(2)}) %all-to-all-start.2) | async-done | bytes 131104 | tf_op jit(solution)/shard_map/all_to_all | solution.py:246
  85.7 0.9 %convert_reduce_fusion = f32[8,8,128]{2,1,0:T(8,128)S(1)} fusion(bf16[8,8,8,128]{3,2,1,0:T(8,128)(2,1)} %all-to-all-done.2), kind=kLoop, calls=%fused_computation.17 | loop fusion | flops 122880 | bytes 163840 | tf_op jit(solution)/shard_map/reduce_sum | solution.py:266
  86.7 0.6 copy.100
  (24 shorter events, 0.2 us)
Async XLA Ops:
  0.6 1.2 %copy-start.6 = (bf16[256,2,256]{2,1,0:T(2,128)(2,1)S(1)}, bf16[256,2,256]{2,1,0:T(2,128)(2,1)}, u32[]{:S(2)}) copy-start(bf16[256,2,256]{2,1,0:T(2,128)(2,1)} %param.14) | copy-start | bytes 786436
  0.6 1.2 %copy-start.7 = (bf16[256,2,256]{2,1,0:T(2,128)(2,1)S(1)}, bf16[256,2,256]{2,1,0:T(2,128)(2,1)}, u32[]{:S(2)}) copy-start(bf16[256,2,256]{2,1,0:T(2,128)(2,1)} %param.13) | copy-start | bytes 786436
  0.7 1.2 %copy-start.8 = (bf16[256,2,256]{2,1,0:T(2,128)(2,1)S(1)}, bf16[256,2,256]{2,1,0:T(2,128)(2,1)}, u32[]{:S(2)}) copy-start(bf16[256,2,256]{2,1,0:T(2,128)(2,1)} %param.12) | copy-start | bytes 786436
  3.8 31.0 %copy-start = (bf16[4,256,256]{2,1,0:T(8,128)(2,1)S(1)}, bf16[4,256,256]{2,1,0:T(8,128)(2,1)}, u32[]{:S(2)}) copy-start(bf16[4,256,256]{2,1,0:T(8,128)(2,1)} %constant.21.clone.back_ref) | copy-start | bytes 1572868
  3.8 31.0 %copy-start.1 = (bf16[4,256,256]{2,1,0:T(8,128)(2,1)S(1)}, bf16[4,256,256]{2,1,0:T(8,128)(2,1)}, u32[]{:S(2)}) copy-start(bf16[4,256,256]{2,1,0:T(8,128)(2,1)} %constant.20.clone.forth_ref) | copy-start | bytes 1572868
  3.8 31.0 %copy-start.2 = (f32[64,256]{1,0:T(8,128)S(1)}, f32[64,256]{1,0:T(8,128)}, u32[]{:S(2)}) copy-start(f32[64,256]{1,0:T(8,128)} %constant.19.clone.sin_ref) | copy-start | bytes 196612
  3.8 31.0 %copy-start.3 = (f32[64,256]{1,0:T(8,128)S(1)}, f32[64,256]{1,0:T(8,128)}, u32[]{:S(2)}) copy-start(f32[64,256]{1,0:T(8,128)} %constant.18.clone.cos_ref) | copy-start | bytes 196612
  3.8 31.0 %copy-start.4 = (bf16[64,384]{1,0:T(8,128)(2,1)S(1)}, bf16[64,384]{1,0:T(8,128)(2,1)}, u32[]{:S(2)}) copy-start(bf16[64,384]{1,0:T(8,128)(2,1)} %constant.17.clone.leave_ref) | copy-start | bytes 147460
  3.8 31.0 %copy-start.5 = (bf16[128,128]{1,0:T(8,128)(2,1)S(1)}, bf16[128,128]{1,0:T(8,128)(2,1)}, u32[]{:S(2)}) copy-start(bf16[128,128]{1,0:T(8,128)(2,1)} %constant.16.clone.enter_ref) | copy-start | bytes 98308
  66.2 19.5 %all-to-all-start.2 = ((bf16[8,8,8,128]{3,2,1,0:T(8,128)(2,1)}), bf16[8,8,8,128]{3,2,1,0:T(8,128)(2,1)}, u32[]{:S(2)}, u32[]{:S(2)}) async-start(bf16[8,8,8,128]{3,2,1,0:T(8,128)(2,1)} %bitcast.11), calls=%async_computation.2 | async-start | bytes 262144 | tf_op jit(solution)/shard_map/all_to_all | solution.py:246
  77.7 1.0 %copy-start.9 = (bf16[256,2,256]{2,1,0:T(2,128)(2,1)S(1)}, bf16[256,2,256]{2,1,0:T(2,128)(2,1)}, u32[]{:S(2)}) copy-start(bf16[256,2,256]{2,1,0:T(2,128)(2,1)} %param.17) | copy-start | bytes 786436
  77.7 0.9 %copy-start.10 = (f32[2,256]{1,0:T(2,128)S(1)}, f32[2,256]{1,0:T(2,128)}, u32[]{:S(2)}) copy-start(f32[2,256]{1,0:T(2,128)} %param.16) | copy-start | bytes 6148

commit v2 on v1

v2 whole, which is shorter than its diff:
```python
import math

import jax
import jax.numpy as jnp
import ml_dtypes
import numpy as np
from jax import lax
from jax.experimental import pallas as pl
from jax.experimental.pallas import tpu as pltpu
from jax.sharding import PartitionSpec as P

BLOCKS = 64
ROWS = 256
HALF = ROWS // 2
SIGNALS = 8
GROUPS_HERE = 4
KEPT = 64
FULL = 2 * BLOCKS * ROWS


def split_table(table):
    high = table.astype(ml_dtypes.bfloat16)
    low = (table - high.astype(np.float64)).astype(ml_dtypes.bfloat16)
    return high, low


def tables():
    kept = np.arange(KEPT)[:, None]
    block = np.arange(BLOCKS)[None, :]
    coarse = 2 * math.pi * (((2 * kept + 1) * block) % (4 * BLOCKS)) / (4 * BLOCKS)
    enter_high, enter_low = split_table(np.concatenate([np.cos(coarse), -np.sin(coarse)], axis=0))
    enter = np.concatenate([enter_high, enter_low], axis=1)
    leave_high, leave_low = split_table(
        np.concatenate([np.cos(coarse.T), -np.sin(coarse.T)], axis=1) * (2.0 / FULL)
    )
    leave = np.concatenate(
        [
            np.concatenate([leave_high, leave_high], axis=1),
            np.concatenate([leave_low, np.zeros_like(leave_low)], axis=1),
        ]
    )
    row = np.arange(ROWS)[None, :]
    twist = 2 * math.pi * (kept + 0.5) * row / FULL
    turn_cos = np.cos(twist).astype(np.float32)
    turn_sin = np.sin(twist).astype(np.float32)
    fine = []
    for odd in (0, 1):
        angle = (
            2
            * math.pi
            * ((np.arange(HALF)[:, None] * (2 * np.arange(HALF)[None, :] + odd)) % ROWS)
            / ROWS
        )
        cos, sin = np.cos(angle), np.sin(angle)
        forth = np.concatenate(
            [np.concatenate([cos, -sin], axis=1), np.concatenate([sin, cos], axis=1)], axis=0
        )
        fine.append((split_table(forth), split_table(forth.T)))
    forth, back = (
        np.stack([np.concatenate([high, low, high]) for high, low in (pair[way] for pair in fine)])
        for way in (0, 1)
    )
    return enter, leave, turn_cos, turn_sin, forth, back


def mxu(left, right):
    return jnp.dot(left, right, preferred_element_type=jnp.float32)


def halves(value):
    high = value.astype(jnp.bfloat16)
    low = (value - high.astype(jnp.float32)).astype(jnp.bfloat16)
    return high, low


def spectral_kernel(
    recv_ref,
    enter_ref,
    leave_ref,
    cos_ref,
    sin_ref,
    forth_ref,
    back_ref,
    send_ref,
    wide_ref,
    high_ref,
    low_ref,
    spec_ref,
    turn_ref,
):
    signals = 2 * SIGNALS + GROUPS_HERE
    for lane in range(5):
        lanes = slice(lane * HALF, (lane + 1) * HALF)
        wide_ref[lane] = (
            recv_ref[:, :, lanes].astype(jnp.float32).reshape(BLOCKS * SIGNALS, HALF)
        )
    enter = enter_ref[...]
    turn_cos = cos_ref[...]
    turn_sin = sin_ref[...]

    def every(row):
        return pl.ds(row, BLOCKS, stride=SIGNALS)

    leave = leave_ref[...]
    members = SIGNALS // GROUPS_HERE
    count = 2 * members + 1

    def places(group, item):
        if item == 2 * members:
            return ((4, group), (4, group + GROUPS_HERE))
        which, member = divmod(item, members)
        row = member * GROUPS_HERE + group
        return ((2 * which, row), (2 * which + 1, row))

    def spot(group, item):
        start = (group * count + item) * KEPT
        return slice(start, start + KEPT)

    def put(odd, rows, real, imag):
        for part, value in enumerate((real, imag)):
            high, low = halves(value)
            lanes = slice(part * HALF, (part + 1) * HALF)
            high_ref[odd, rows, lanes] = high
            low_ref[odd, rows, lanes] = low

    def both(matrix_ref, odd, rows):
        high = high_ref[odd, rows, :]
        return mxu(
            jnp.concatenate([low_ref[odd, rows, :], high, high], axis=1), matrix_ref[odd]
        )

    def enter_group(group):
        for item in range(count):
            taken = jnp.concatenate(
                [wide_ref[lane, every(row), :] for lane, row in places(group, item)], axis=1
            ).astype(jnp.bfloat16)
            first = mxu(enter, jnp.concatenate([taken, taken], axis=0))
            real, imag = first[:KEPT], first[KEPT:]
            turned_real = real * turn_cos + imag * turn_sin
            turned_imag = imag * turn_cos - real * turn_sin
            for odd in (0, 1):
                sign = 1.0 - 2.0 * odd
                put(
                    odd,
                    spot(group, item),
                    turned_real[:, :HALF] + sign * turned_real[:, HALF:],
                    turned_imag[:, :HALF] + sign * turned_imag[:, HALF:],
                )

    def forth_group(group):
        rows = slice(group * count * KEPT, (group + 1) * count * KEPT)
        for odd in (0, 1):
            spec_ref[odd, rows, :] = both(forth_ref, odd, rows)

    def multiply_group(group):
        for odd in (0, 1):

            def spectrum(item):
                rows = spot(group, item)
                return spec_ref[odd, rows, :HALF], spec_ref[odd, rows, HALF:]

            tap_real, tap_imag = spectrum(2 * members)
            lag_real = lag_imag = None
            for member in range(members):
                in_real, in_imag = spectrum(member)
                cot_real, cot_imag = spectrum(members + member)
                put(
                    odd,
                    spot(group, member),
                    in_real * tap_real - in_imag * tap_imag,
                    in_real * tap_imag + in_imag * tap_real,
                )
                put(
                    odd,
                    spot(group, members + member),
                    cot_real * tap_real + cot_imag * tap_imag,
                    cot_imag * tap_real - cot_real * tap_imag,
                )
                more_real = cot_real * in_real + cot_imag * in_imag
                more_imag = cot_imag * in_real - cot_real * in_imag
                lag_real = more_real if member == 0 else lag_real + more_real
                lag_imag = more_imag if member == 0 else lag_imag + more_imag
            put(odd, spot(group, 2 * members), lag_real, lag_imag)

    def back_group(group):
        rows = slice(group * count * KEPT, (group + 1) * count * KEPT)
        even_part = both(back_ref, 0, rows)
        odd_part = both(back_ref, 1, rows)
        turn_ref[0, rows, :] = even_part + odd_part
        turn_ref[1, rows, :] = even_part - odd_part

    def leave_group(group):
        for item in range(count):
            rows = spot(group, item)
            real = jnp.concatenate([turn_ref[0, rows, :HALF], turn_ref[1, rows, :HALF]], axis=1)
            imag = jnp.concatenate([turn_ref[0, rows, HALF:], turn_ref[1, rows, HALF:]], axis=1)
            real_high, real_low = halves(real * turn_cos - imag * turn_sin)
            imag_high, imag_low = halves(imag * turn_cos + real * turn_sin)
            result = mxu(
                leave,
                jnp.concatenate([real_high, imag_high, real_low, imag_low], axis=0),
            )
            result = result[:BLOCKS] + result[BLOCKS:]
            for part, (lane, row) in enumerate(places(group, item)):
                wide_ref[lane, every(row), :] = result[:, part * HALF : (part + 1) * HALF]

    for step in range(GROUPS_HERE + 4):
        for lag, stage in enumerate(
            (enter_group, forth_group, multiply_group, back_group, leave_group)
        ):
            if 0 <= step - lag < GROUPS_HERE:
                stage(step - lag)
    for lane in range(5):
        lanes = slice(lane * HALF, (lane + 1) * HALF)
        send_ref[:, :, lanes] = (
            wide_ref[lane].reshape(BLOCKS, SIGNALS, HALF).astype(jnp.bfloat16)
        )


def spectral(received):
    signals = 2 * SIGNALS + GROUPS_HERE
    return pl.pallas_call(
        spectral_kernel,
        out_shape=jax.ShapeDtypeStruct((BLOCKS, SIGNALS, 5 * HALF), jnp.bfloat16),
        in_specs=[pl.BlockSpec(memory_space=pltpu.VMEM)] * 7,
        out_specs=pl.BlockSpec(memory_space=pltpu.VMEM),
        scratch_shapes=[
            pltpu.VMEM((5, BLOCKS * SIGNALS, HALF), jnp.float32),
            pltpu.VMEM((2, signals * KEPT, ROWS), jnp.bfloat16),
            pltpu.VMEM((2, signals * KEPT, ROWS), jnp.bfloat16),
            pltpu.VMEM((2, signals * KEPT, ROWS), jnp.float32),
            pltpu.VMEM((2, signals * KEPT, ROWS), jnp.float32),
        ],
        compiler_params=pltpu.CompilerParams(vmem_limit_bytes=32 * 1024 * 1024),
        cost_estimate=pl.CostEstimate(flops=6_000_000_000, bytes_accessed=3_000_000, transcendentals=0),
        name="spectral",
    )(received, *(jnp.asarray(table) for table in tables()))


def gate_kernel(
    out_gate_ref,
    in_gate_ref,
    values_ref,
    taps_ref,
    cot_ref,
    send_ref,
    gates_ref,
    held_taps_ref,
    arrived,
):
    sources = (in_gate_ref, values_ref, cot_ref, out_gate_ref)
    copies = [
        pltpu.make_async_copy(source, gates_ref.at[slot], arrived.at[slot])
        for slot, source in enumerate(sources)
    ]
    copies.append(pltpu.make_async_copy(taps_ref, held_taps_ref, arrived.at[len(sources)]))
    for copy in copies:
        copy.start()

    row = lax.broadcasted_iota(jnp.int32, (2 * ROWS, 2 * ROWS), 0)
    column = lax.broadcasted_iota(jnp.int32, (2 * ROWS, 2 * ROWS), 1)
    parted = (row == column % ROWS * 2 + column // ROWS).astype(jnp.float32)
    parted = parted.astype(jnp.bfloat16)
    plain = (row == column)[:ROWS, :ROWS].astype(jnp.float32).astype(jnp.bfloat16)

    def turned(value, order):
        return lax.dot_general(
            value, order, (((0,), (0,)), ((), ())), preferred_element_type=jnp.float32
        ).astype(jnp.bfloat16)

    def send(part, lanes, value):
        rows = slice(part * GROUPS_HERE, (part + 1) * GROUPS_HERE)
        send_ref[:, rows, lanes] = value.reshape(BLOCKS, GROUPS_HERE, -1)

    for which in range(2):
        left, right = 2 * which, 2 * which + 1
        copies[left].wait()
        copies[right].wait()
        product = gates_ref[left].reshape(2 * ROWS, ROWS).astype(jnp.float32) * gates_ref[
            right
        ].reshape(2 * ROWS, ROWS).astype(jnp.float32)
        signal = turned(product.astype(jnp.bfloat16), parted)
        for member in range(2):
            send(
                member,
                slice(which * ROWS, (which + 1) * ROWS),
                signal[:, member * ROWS : (member + 1) * ROWS],
            )
    copies[-1].wait()
    taps = turned(held_taps_ref[...], plain)
    for half in range(2):
        send(half, slice(2 * ROWS, None), taps[:, half * HALF : (half + 1) * HALF])


def gated_chunks(out_gate, in_gate, values_in, filter_taps, out_cotangent):
    return pl.pallas_call(
        gate_kernel,
        out_shape=jax.ShapeDtypeStruct((BLOCKS, SIGNALS, 5 * HALF), jnp.bfloat16),
        in_specs=[pl.BlockSpec(memory_space=pl.ANY)] * 5,
        out_specs=pl.BlockSpec(memory_space=pltpu.VMEM),
        scratch_shapes=[
            pltpu.VMEM((4, ROWS, 2, ROWS), jnp.bfloat16),
            pltpu.VMEM((ROWS, ROWS), jnp.bfloat16),
            pltpu.SemaphoreType.DMA((5,)),
        ],
        cost_estimate=pl.CostEstimate(
            flops=400_000_000, bytes_accessed=2_000_000, transcendentals=0
        ),
        name="gates",
    )(out_gate, in_gate, values_in, filter_taps, out_cotangent)


def unchunks(received, member_count):
    return (
        received.reshape(BLOCKS, member_count, GROUPS_HERE, ROWS)
        .transpose(3, 1, 0, 2)
        .reshape(ROWS, member_count, BLOCKS * GROUPS_HERE)
        .astype(jnp.float32)
    )


def exchange(value, axis):
    return lax.all_to_all(value, axis, split_axis=0, concat_axis=0, tiled=True)


def local(out_gate, in_gate, values_in, filter_taps, skip_gain, out_cotangent):
    row_count, member_count, group_count = out_gate.shape
    chan_count = lax.axis_size("chan")
    outgoing = gated_chunks(out_gate, in_gate, values_in, filter_taps, out_cotangent)
    returned = exchange(spectral(exchange(outgoing, "seq")), "seq")
    lag_terms = exchange(
        returned[:, :, 4 * HALF :].reshape(chan_count, -1, SIGNALS, HALF), "chan"
    )
    norm_factor = 1.0 / math.sqrt(BLOCKS * row_count * member_count * chan_count)
    lag_sum = jnp.sum(lag_terms.astype(jnp.float32), axis=0)
    grad_filter = (
        lag_sum.reshape(-1, 2, GROUPS_HERE, HALF).transpose(1, 3, 0, 2).reshape(row_count, -1)
        * norm_factor
    )
    mixed_in = (in_gate.astype(jnp.float32) * values_in.astype(jnp.float32)).astype(jnp.bfloat16)
    conv_cot = (out_cotangent.astype(jnp.float32) * out_gate.astype(jnp.float32)).astype(
        jnp.bfloat16
    )
    conv_out = unchunks(returned[:, :, : 2 * HALF], member_count)
    back_conv = unchunks(returned[:, :, 2 * HALF : 4 * HALF], member_count)
    before_gate = conv_out + skip_gain[None] * mixed_in.astype(jnp.float32)
    mixed = (out_gate.astype(jnp.float32) * before_gate).astype(jnp.bfloat16)
    grad_out_gate = (out_cotangent.astype(jnp.float32) * before_gate).astype(jnp.bfloat16)
    back_in = back_conv + skip_gain[None] * conv_cot.astype(jnp.float32)
    grad_in_gate = (back_in * values_in.astype(jnp.float32)).astype(jnp.bfloat16)
    grad_values = (back_in * in_gate.astype(jnp.float32)).astype(jnp.bfloat16)
    return (mixed, grad_out_gate, grad_in_gate, grad_values, grad_filter)


def solution(mesh):
    in_specs = (
        P("seq", "chan", None),
        P("seq", "chan", None),
        P("seq", "chan", None),
        P("seq", None),
        P("chan", None),
        P("seq", "chan", None),
    )
    out_specs = (
        P("seq", "chan", None),
        P("seq", "chan", None),
        P("seq", "chan", None),
        P("seq", "chan", None),
        P("seq", "chan"),
    )
    return jax.shard_map(local, mesh=mesh, in_specs=in_specs, out_specs=out_specs, check_vma=False)
```

time: 87.7 us -> 86.3 us (0.984)
  Pallas kernels: 4.7 us -> 7.14 us
  other arithmetic: 2.42 us -> 0.38 us
  local copies, waits for them, and re-layouts: 9.09 us -> 7.46 us
    pallas_call x0 -> x1, Pallas kernels: none -> 3.12 us  [gated_chunks(): pl.pallas_call(gate_kernel, out_shape=jax.ShapeDtypeStruct((BLOCKS, SIGNA...]
    transpose x4 -> x0, local copies, waits for them, and re-layouts: 1.32 us -> none  [the longest x1 1.07 us: local(): filter_taps.T.reshape(BLOCKS, GROUPS_HERE, 2, HALF).transpose(0, 2, 1, 3)]
    convert_element_type x2 -> x1, other arithmetic: 1.36 us -> 0.29 us  [local(): (out_cotangent.astype(jnp.float32) * before_gate).astype(jnp.bfloat16)]
    reduce_sum x1, other arithmetic: 0.93 us -> 0.02 us  [local(): lag_sum = jnp.sum(lag_terms.astype(jnp.float32), axis=0)]
where the time goes in v2:
time: 86.3 us; the launch traced here: 85.8 us
  blocking collectives  57.1 us (66%)
  starting transfers between devices  10.3 us (12%)
  local copies, waits for them, and re-layouts  7.46 us (9%)
  Pallas kernels  7.14 us (8%)
  waiting for transfers between devices  2.51 us (3%)
    all_to_all x2, blocking collectives, exchange(): return lax.all_to_all(value, axis, split_axis=0, concat_axis=0, tiled=True)  57.1 us
    all_to_all x1, starting transfers between devices, exchange(): return lax.all_to_all(value, axis, split_axis=0, concat_axis=0, tiled=True)  10.3 us
    unnamed x27, local copies, waits for them, and re-layouts  5.49 us
    pallas_call x1, Pallas kernels, spectral(): pl.pallas_call(spectral_kernel, out_shape=jax.ShapeDtypeStruct((BLOCKS, S...  4.02 us
    pallas_call x1, Pallas kernels, gated_chunks(): pl.pallas_call(gate_kernel, out_shape=jax.ShapeDtypeStruct((BLOCKS, SIGNA...  3.12 us
    all_to_all x1, waiting for transfers between devices, exchange(): return lax.all_to_all(value, axis, split_axis=0, concat_axis=0, tiled=True)  2.51 us
  transfers between devices with their start and end apart: 1, of which 1 were waited for; matrix products, arithmetic and copies ran while one was open for 6% of the time, Pallas kernels for 0%

profile of v2, /device:TPU:6, one launch (start us, length us, event | category | flops | bytes accessed | tf_op | source)
XLA Modules:
  0.0 85.8 jit_solution(17541014564033787883)
XLA Ops:
  0.6 0.0 copy-start.1
  0.6 3.1 %gates.1 = bf16[64,8,640]{2,1,0:T(8,128)(2,1)} custom-call(bf16[256,2,256]{2,1,0:T(2,128)(2,1)} %out_gate_ref.1, bf16[256,2,256]{2,1,0:T(2,128)(2,1)} %in_gate_ref.1, bf16[256,2,256]{2,1,0:T(2,128)(2,1)} %values_ref.1, bf16[256,256]{1,0:T(8,128)(2,1)} %taps_ref.1, bf16[256,2,256]{2,1,0:T(2,128)(2,1)} %cot_ref.1), custom_call_target="tpu_custom_call" | custom-call | flops 400000000 | bytes 2000000 | tf_op jit(solution)/shard_map/gates/pallas_call | solution.py:296
  3.8 0.0 copy-start
  3.8 0.0 copy-start.2
  3.8 0.0 copy-start.3
  3.8 0.0 copy-start.4
  3.8 0.0 copy-start.5
  3.8 31.1 %all_to_all.15.recv_ref = bf16[64,8,640]{2,1,0:T(8,128)(2,1)S(1)} all-to-all(bf16[64,8,640]{2,1,0:T(8,128)(2,1)} %gates.1), channel_id=1, replica_groups=mesh['seq'=64,'chan'=8] {'seq'}, dimensions={0} | all-to-all | bytes 1310720 | tf_op jit(solution)/shard_map/all_to_all | solution.py:323
  35.0 4.0 %spectral.1 = bf16[64,8,640]{2,1,0:T(8,128)(2,1)S(1)} custom-call(bf16[64,8,640]{2,1,0:T(8,128)(2,1)S(1)} %all_to_all.15.recv_ref, bf16[128,128]{1,0:T(8,128)(2,1)S(1)} %copy-done.5, bf16[128,256]{1,0:T(8,128)(2,1)S(1)} %copy-done.4, f32[64,256]{1,0:T(8,128)S(1)} %copy-done.3, f32[64,256]{1,0:T(8,128)S(1)} %copy-done.2, bf16[2,768,256]{2,1,0:T(8,128)(2,1)S(1)} %copy-done.1, ...), custom_call_target="tpu_custom_call" | custom-call | flops 6000000000 | bytes 3000000 | tf_op jit(solution)/shard_map/spectral/pallas_call | solution.py:222
  39.0 26.0 %all_to_all.16 = bf16[64,8,640]{2,1,0:T(8,128)(2,1)S(1)} all-to-all(bf16[64,8,640]{2,1,0:T(8,128)(2,1)S(1)} %spectral.1), channel_id=1, replica_groups=mesh['seq'=64,'chan'=8] {'seq'}, dimensions={0} | all-to-all | bytes 1310720 | tf_op jit(solution)/shard_map/all_to_all | solution.py:323
  65.0 0.7 slice.14
  65.7 10.3 %all-to-all-start.2 = ((bf16[8,8,8,128]{3,2,1,0:T(8,128)(2,1)}), bf16[8,8,8,128]{3,2,1,0:T(8,128)(2,1)S(1)}, u32[]{:S(2)}, u32[]{:S(2)}) async-start(bf16[8,8,8,128]{3,2,1,0:T(8,128)(2,1)} %bitcast.4), calls=%async_computation.2 | async-start | bytes 262144 | tf_op jit(solution)/shard_map/all_to_all | solution.py:323
  76.0 0.1 slice_convert_fusion
  76.1 0.1 reshape.36
  76.2 0.3 copy.61
  76.5 0.2 copy.62
  76.7 0.1 reshape.35
  76.9 0.0 copy-start.10
  76.9 0.3 copy.56
  77.2 0.2 copy.59
  77.5 0.1 copy-done.10
  77.6 0.6 copy-done.6
  78.1 0.1 copy-done.7
  78.2 0.1 copy-done.8
  78.3 0.1 copy-done.9
  78.4 0.3 fusion.4
  78.7 1.0 %copy.66 = bf16[256,2,256]{2,1,0:T(2,128)(2,1)} copy(bf16[256,2,256]{2,0,1:T(8,128)(2,1)S(1)} %get-tuple-element.27) | data formatting | bytes 524288
  79.7 1.0 %copy.65 = bf16[256,2,256]{2,1,0:T(2,128)(2,1)} copy(bf16[256,2,256]{2,0,1:T(8,128)(2,1)S(1)} %get-tuple-element.28) | data formatting | bytes 524288
  80.6 1.0 %copy.67 = bf16[256,2,256]{2,1,0:T(2,128)(2,1)} copy(bf16[256,2,256]{2,0,1:T(8,128)(2,1)S(1)} %get-tuple-element.29) | data formatting | bytes 524288
  81.6 1.0 %copy.68 = bf16[256,2,256]{2,1,0:T(2,128)(2,1)} copy(bf16[256,2,256]{2,0,1:T(8,128)(2,1)S(1)} %get-tuple-element.30) | data formatting | bytes 524288
  82.6 2.5 %all-to-all-done.2 = bf16[8,8,8,128]{3,2,1,0:T(8,128)(2,1)S(1)} async-done(((bf16[8,8,8,128]{3,2,1,0:T(8,128)(2,1)}), bf16[8,8,8,128]{3,2,1,0:T(8,128)(2,1)S(1)}, u32[]{:S(2)}, u32[]{:S(2)}) %all-to-all-start.2) | async-done | bytes 131104 | tf_op jit(solution)/shard_map/all_to_all | solution.py:323
  85.2 0.6 copy.95
  (14 shorter events, 0.1 us)
Async XLA Ops:
  0.6 34.3 %copy-start.1 = (bf16[2,768,256]{2,1,0:T(8,128)(2,1)S(1)}, bf16[2,768,256]{2,1,0:T(8,128)(2,1)}, u32[]{:S(2)}) copy-start(bf16[2,768,256]{2,1,0:T(8,128)(2,1)} %constant.20.clone.forth_ref) | copy-start | bytes 2359300
  3.8 31.2 %copy-start = (bf16[2,768,256]{2,1,0:T(8,128)(2,1)S(1)}, bf16[2,768,256]{2,1,0:T(8,128)(2,1)}, u32[]{:S(2)}) copy-start(bf16[2,768,256]{2,1,0:T(8,128)(2,1)} %constant.21.clone.back_ref) | copy-start | bytes 2359300
  3.8 31.2 %copy-start.2 = (f32[64,256]{1,0:T(8,128)S(1)}, f32[64,256]{1,0:T(8,128)}, u32[]{:S(2)}) copy-start(f32[64,256]{1,0:T(8,128)} %constant.19.clone.sin_ref) | copy-start | bytes 196612
  3.8 31.2 %copy-start.3 = (f32[64,256]{1,0:T(8,128)S(1)}, f32[64,256]{1,0:T(8,128)}, u32[]{:S(2)}) copy-start(f32[64,256]{1,0:T(8,128)} %constant.18.clone.cos_ref) | copy-start | bytes 196612
  3.8 31.2 %copy-start.4 = (bf16[128,256]{1,0:T(8,128)(2,1)S(1)}, bf16[128,256]{1,0:T(8,128)(2,1)}, u32[]{:S(2)}) copy-start(bf16[128,256]{1,0:T(8,128)(2,1)} %constant.17.clone.leave_ref) | copy-start | bytes 196612
  3.8 31.2 %copy-start.5 = (bf16[128,128]{1,0:T(8,128)(2,1)S(1)}, bf16[128,128]{1,0:T(8,128)(2,1)}, u32[]{:S(2)}) copy-start(bf16[128,128]{1,0:T(8,128)(2,1)} %constant.16.clone.enter_ref) | copy-start | bytes 98308
  65.7 19.4 %all-to-all-start.2 = ((bf16[8,8,8,128]{3,2,1,0:T(8,128)(2,1)}), bf16[8,8,8,128]{3,2,1,0:T(8,128)(2,1)S(1)}, u32[]{:S(2)}, u32[]{:S(2)}) async-start(bf16[8,8,8,128]{3,2,1,0:T(8,128)(2,1)} %bitcast.4), calls=%async_computation.2 | async-start | bytes 262144 | tf_op jit(solution)/shard_map/all_to_all | solution.py:323
  76.9 0.7 copy-start.10
  77.2 1.0 %copy-start.6 = (bf16[256,2,256]{2,1,0:T(2,128)(2,1)S(1)}, bf16[256,2,256]{2,1,0:T(2,128)(2,1)}, u32[]{:S(2)}) copy-start(bf16[256,2,256]{2,1,0:T(2,128)(2,1)} %out_gate_ref.1) | copy-start | bytes 786436
  77.2 1.0 %copy-start.7 = (bf16[256,2,256]{2,1,0:T(2,128)(2,1)S(1)}, bf16[256,2,256]{2,1,0:T(2,128)(2,1)}, u32[]{:S(2)}) copy-start(bf16[256,2,256]{2,1,0:T(2,128)(2,1)} %in_gate_ref.1) | copy-start | bytes 786436
  77.2 1.1 %copy-start.8 = (bf16[256,2,256]{2,1,0:T(2,128)(2,1)S(1)}, bf16[256,2,256]{2,1,0:T(2,128)(2,1)}, u32[]{:S(2)}) copy-start(bf16[256,2,256]{2,1,0:T(2,128)(2,1)} %values_ref.1) | copy-start | bytes 786436
  77.2 1.2 %copy-start.9 = (bf16[256,2,256]{2,1,0:T(2,128)(2,1)S(1)}, bf16[256,2,256]{2,1,0:T(2,128)(2,1)}, u32[]{:S(2)}) copy-start(bf16[256,2,256]{2,1,0:T(2,128)(2,1)} %cot_ref.1) | copy-start | bytes 786436

commit v3 on v2

--- a/solution.py
+++ b/solution.py
@@ -296,18 +296,24 @@
     return pl.pallas_call(
         gate_kernel,
         out_shape=jax.ShapeDtypeStruct((BLOCKS, SIGNALS, 5 * HALF), jnp.bfloat16),
-        in_specs=[pl.BlockSpec(memory_space=pl.ANY)] * 5,
+        in_specs=[pl.BlockSpec(memory_space=pltpu.HBM)] * 5,
         out_specs=pl.BlockSpec(memory_space=pltpu.VMEM),
         scratch_shapes=[
             pltpu.VMEM((4, ROWS, 2, ROWS), jnp.bfloat16),
             pltpu.VMEM((ROWS, ROWS), jnp.bfloat16),
             pltpu.SemaphoreType.DMA((5,)),
         ],
+        compiler_params=pltpu.CompilerParams(vmem_limit_bytes=16 * 1024 * 1024),
         cost_estimate=pl.CostEstimate(
             flops=400_000_000, bytes_accessed=2_000_000, transcendentals=0
         ),
         name="gates",
-    )(out_gate, in_gate, values_in, filter_taps, out_cotangent)
+    )(
+        *(
+            pltpu.with_memory_space_constraint(value, pltpu.HBM)
+            for value in (out_gate, in_gate, values_in, filter_taps, out_cotangent)
+        )
+    )
 
 
 def unchunks(received, member_count):
@@ -317,6 +323,10 @@
         .reshape(ROWS, member_count, BLOCKS * GROUPS_HERE)
         .astype(jnp.float32)
     )
+
+
+def rounded(value):
+    return lax.reduce_precision(value, exponent_bits=8, mantissa_bits=7)
 
 
 def exchange(value, axis):
@@ -337,16 +347,14 @@
         lag_sum.reshape(-1, 2, GROUPS_HERE, HALF).transpose(1, 3, 0, 2).reshape(row_count, -1)
         * norm_factor
     )
-    mixed_in = (in_gate.astype(jnp.float32) * values_in.astype(jnp.float32)).astype(jnp.bfloat16)
-    conv_cot = (out_cotangent.astype(jnp.float32) * out_gate.astype(jnp.float32)).astype(
-        jnp.bfloat16
-    )
+    mixed_in = rounded(in_gate.astype(jnp.float32) * values_in.astype(jnp.float32))
+    conv_cot = rounded(out_cotangent.astype(jnp.float32) * out_gate.astype(jnp.float32))
     conv_out = unchunks(returned[:, :, : 2 * HALF], member_count)
     back_conv = unchunks(returned[:, :, 2 * HALF : 4 * HALF], member_count)
-    before_gate = conv_out + skip_gain[None] * mixed_in.astype(jnp.float32)
+    before_gate = conv_out + skip_gain[None] * mixed_in
     mixed = (out_gate.astype(jnp.float32) * before_gate).astype(jnp.bfloat16)
     grad_out_gate = (out_cotangent.astype(jnp.float32) * before_gate).astype(jnp.bfloat16)
-    back_in = back_conv + skip_gain[None] * conv_cot.astype(jnp.float32)
+    back_in = back_conv + skip_gain[None] * conv_cot
     grad_in_gate = (back_in * values_in.astype(jnp.float32)).astype(jnp.bfloat16)
     grad_values = (back_in * in_gate.astype(jnp.float32)).astype(jnp.bfloat16)
     return (mixed, grad_out_gate, grad_in_gate, grad_values, grad_filter)

time: 86.3 us -> 85.2 us (0.987)
  transfers between devices with their start and end apart: 1 -> 1, of which waited for: 1 -> 1; matrix products, arithmetic and copies ran while one was open for 6% -> 7% of each run, Pallas kernels for 0% -> 0%
where the time goes in v3:
time: 85.2 us; the launch traced here: 84.8 us
  blocking collectives  56.9 us (67%)
  starting transfers between devices  10.3 us (12%)
  local copies, waits for them, and re-layouts  7.46 us (9%)
  Pallas kernels  6.28 us (7%)
  waiting for transfers between devices  2.47 us (3%)
    all_to_all x2, blocking collectives, exchange(): return lax.all_to_all(value, axis, split_axis=0, concat_axis=0, tiled=True)  56.9 us
    all_to_all x1, starting transfers between devices, exchange(): return lax.all_to_all(value, axis, split_axis=0, concat_axis=0, tiled=True)  10.3 us
    unnamed x27, local copies, waits for them, and re-layouts  5.49 us
    pallas_call x1, Pallas kernels, spectral(): pl.pallas_call(spectral_kernel, out_shape=jax.ShapeDtypeStruct((BLOCKS, S...  4 us
    all_to_all x1, waiting for transfers between devices, exchange(): return lax.all_to_all(value, axis, split_axis=0, concat_axis=0, tiled=True)  2.47 us
    pallas_call x1, Pallas kernels, gated_chunks(): pl.pallas_call(gate_kernel, out_shape=jax.ShapeDtypeStruct((BLOCKS, SIGNA...  2.28 us
  transfers between devices with their start and end apart: 1, of which 1 were waited for; matrix products, arithmetic and copies ran while one was open for 7% of the time, Pallas kernels for 0%

profile of v3, /device:TPU:6, one launch (start us, length us, event | category | flops | bytes accessed | tf_op | source)
XLA Modules:
  0.0 84.8 jit_solution(16523969502389430455)
XLA Ops:
  0.6 0.0 copy-start.1
  0.6 2.3 %gates.1 = bf16[64,8,640]{2,1,0:T(8,128)(2,1)S(1)} custom-call(bf16[256,2,256]{2,1,0:T(2,128)(2,1)} %out_gate_ref.1, bf16[256,2,256]{2,1,0:T(2,128)(2,1)} %in_gate_ref.1, bf16[256,2,256]{2,1,0:T(2,128)(2,1)} %values_ref.1, bf16[256,256]{1,0:T(8,128)(2,1)} %taps_ref.1, bf16[256,2,256]{2,1,0:T(2,128)(2,1)} %cot_ref.1), custom_call_target="tpu_custom_call" | custom-call | flops 400000000 | bytes 2000000 | tf_op jit(solution)/shard_map/gates/pallas_call | solution.py:296
  2.9 0.0 copy-start
  2.9 0.0 copy-start.2
  3.0 0.0 copy-start.3
  3.0 0.0 copy-start.4
  3.0 0.0 copy-start.5
  3.0 30.9 %all_to_all.15.recv_ref = bf16[64,8,640]{2,1,0:T(8,128)(2,1)S(1)} all-to-all(bf16[64,8,640]{2,1,0:T(8,128)(2,1)S(1)} %gates.1), channel_id=1, replica_groups=mesh['seq'=64,'chan'=8] {'seq'}, dimensions={0} | all-to-all | bytes 1310720 | tf_op jit(solution)/shard_map/all_to_all | solution.py:333
  34.0 4.0 %spectral.1 = bf16[64,8,640]{2,1,0:T(8,128)(2,1)S(1)} custom-call(bf16[64,8,640]{2,1,0:T(8,128)(2,1)S(1)} %all_to_all.15.recv_ref, bf16[128,128]{1,0:T(8,128)(2,1)S(1)} %copy-done.5, bf16[128,256]{1,0:T(8,128)(2,1)S(1)} %copy-done.4, f32[64,256]{1,0:T(8,128)S(1)} %copy-done.3, f32[64,256]{1,0:T(8,128)S(1)} %copy-done.2, bf16[2,768,256]{2,1,0:T(8,128)(2,1)S(1)} %copy-done.1, ...), custom_call_target="tpu_custom_call" | custom-call | flops 6000000000 | bytes 3000000 | tf_op jit(solution)/shard_map/spectral/pallas_call | solution.py:222
  38.0 26.0 %all_to_all.16 = bf16[64,8,640]{2,1,0:T(8,128)(2,1)S(1)} all-to-all(bf16[64,8,640]{2,1,0:T(8,128)(2,1)S(1)} %spectral.1), channel_id=1, replica_groups=mesh['seq'=64,'chan'=8] {'seq'}, dimensions={0} | all-to-all | bytes 1310720 | tf_op jit(solution)/shard_map/all_to_all | solution.py:333
  64.0 0.7 slice.14
  64.6 10.3 %all-to-all-start.2 = ((bf16[8,8,8,128]{3,2,1,0:T(8,128)(2,1)}), bf16[8,8,8,128]{3,2,1,0:T(8,128)(2,1)S(1)}, u32[]{:S(2)}, u32[]{:S(2)}) async-start(bf16[8,8,8,128]{3,2,1,0:T(8,128)(2,1)} %bitcast.4), calls=%async_computation.2 | async-start | bytes 262144 | tf_op jit(solution)/shard_map/all_to_all | solution.py:333
  75.0 0.1 slice_convert_fusion
  75.1 0.1 reshape.36
  75.2 0.3 copy.61
  75.5 0.2 copy.62
  75.7 0.1 reshape.35
  75.9 0.0 copy-start.10
  75.9 0.3 copy.56
  76.2 0.2 copy.59
  76.4 0.1 copy-done.10
  76.6 0.6 copy-done.6
  77.1 0.1 copy-done.7
  77.2 0.1 copy-done.8
  77.3 0.1 copy-done.9
  77.4 0.3 fusion.6
  77.7 1.0 %copy.66 = bf16[256,2,256]{2,1,0:T(2,128)(2,1)} copy(bf16[256,2,256]{2,0,1:T(8,128)(2,1)S(1)} %get-tuple-element.27) | data formatting | bytes 524288
  78.7 1.0 %copy.65 = bf16[256,2,256]{2,1,0:T(2,128)(2,1)} copy(bf16[256,2,256]{2,0,1:T(8,128)(2,1)S(1)} %get-tuple-element.28) | data formatting | bytes 524288
  79.6 1.0 %copy.67 = bf16[256,2,256]{2,1,0:T(2,128)(2,1)} copy(bf16[256,2,256]{2,0,1:T(8,128)(2,1)S(1)} %get-tuple-element.29) | data formatting | bytes 524288
  80.6 1.0 %copy.68 = bf16[256,2,256]{2,1,0:T(2,128)(2,1)} copy(bf16[256,2,256]{2,0,1:T(8,128)(2,1)S(1)} %get-tuple-element.30) | data formatting | bytes 524288
  81.6 2.5 %all-to-all-done.2 = bf16[8,8,8,128]{3,2,1,0:T(8,128)(2,1)S(1)} async-done(((bf16[8,8,8,128]{3,2,1,0:T(8,128)(2,1)}), bf16[8,8,8,128]{3,2,1,0:T(8,128)(2,1)S(1)}, u32[]{:S(2)}, u32[]{:S(2)}) %all-to-all-start.2) | async-done | bytes 131104 | tf_op jit(solution)/shard_map/all_to_all | solution.py:333
  84.1 0.6 copy.95
  (14 shorter events, 0.1 us)
Async XLA Ops:
  0.6 33.3 %copy-start.1 = (bf16[2,768,256]{2,1,0:T(8,128)(2,1)S(1)}, bf16[2,768,256]{2,1,0:T(8,128)(2,1)}, u32[]{:S(2)}) copy-start(bf16[2,768,256]{2,1,0:T(8,128)(2,1)} %constant.20.clone.forth_ref) | copy-start | bytes 2359300
  2.9 31.0 %copy-start = (bf16[2,768,256]{2,1,0:T(8,128)(2,1)S(1)}, bf16[2,768,256]{2,1,0:T(8,128)(2,1)}, u32[]{:S(2)}) copy-start(bf16[2,768,256]{2,1,0:T(8,128)(2,1)} %constant.21.clone.back_ref) | copy-start | bytes 2359300
  2.9 31.0 %copy-start.2 = (f32[64,256]{1,0:T(8,128)S(1)}, f32[64,256]{1,0:T(8,128)}, u32[]{:S(2)}) copy-start(f32[64,256]{1,0:T(8,128)} %constant.19.clone.sin_ref) | copy-start | bytes 196612
  3.0 31.0 %copy-start.3 = (f32[64,256]{1,0:T(8,128)S(1)}, f32[64,256]{1,0:T(8,128)}, u32[]{:S(2)}) copy-start(f32[64,256]{1,0:T(8,128)} %constant.18.clone.cos_ref) | copy-start | bytes 196612
  3.0 31.0 %copy-start.4 = (bf16[128,256]{1,0:T(8,128)(2,1)S(1)}, bf16[128,256]{1,0:T(8,128)(2,1)}, u32[]{:S(2)}) copy-start(bf16[128,256]{1,0:T(8,128)(2,1)} %constant.17.clone.leave_ref) | copy-start | bytes 196612
  3.0 31.0 %copy-start.5 = (bf16[128,128]{1,0:T(8,128)(2,1)S(1)}, bf16[128,128]{1,0:T(8,128)(2,1)}, u32[]{:S(2)}) copy-start(bf16[128,128]{1,0:T(8,128)(2,1)} %constant.16.clone.enter_ref) | copy-start | bytes 98308
  64.6 19.4 %all-to-all-start.2 = ((bf16[8,8,8,128]{3,2,1,0:T(8,128)(2,1)}), bf16[8,8,8,128]{3,2,1,0:T(8,128)(2,1)S(1)}, u32[]{:S(2)}, u32[]{:S(2)}) async-start(bf16[8,8,8,128]{3,2,1,0:T(8,128)(2,1)} %bitcast.4), calls=%async_computation.2 | async-start | bytes 262144 | tf_op jit(solution)/shard_map/all_to_all | solution.py:333
  75.9 0.7 copy-start.10
  76.2 1.0 %copy-start.6 = (bf16[256,2,256]{2,1,0:T(2,128)(2,1)S(1)}, bf16[256,2,256]{2,1,0:T(2,128)(2,1)}, u32[]{:S(2)}) copy-start(bf16[256,2,256]{2,1,0:T(2,128)(2,1)} %cot_ref.1) | copy-start | bytes 786436
  76.2 1.0 %copy-start.7 = (bf16[256,2,256]{2,1,0:T(2,128)(2,1)S(1)}, bf16[256,2,256]{2,1,0:T(2,128)(2,1)}, u32[]{:S(2)}) copy-start(bf16[256,2,256]{2,1,0:T(2,128)(2,1)} %out_gate_ref.1) | copy-start | bytes 786436
  76.2 1.1 %copy-start.8 = (bf16[256,2,256]{2,1,0:T(2,128)(2,1)S(1)}, bf16[256,2,256]{2,1,0:T(2,128)(2,1)}, u32[]{:S(2)}) copy-start(bf16[256,2,256]{2,1,0:T(2,128)(2,1)} %in_gate_ref.1) | copy-start | bytes 786436
  76.2 1.2 %copy-start.9 = (bf16[256,2,256]{2,1,0:T(2,128)(2,1)S(1)}, bf16[256,2,256]{2,1,0:T(2,128)(2,1)}, u32[]{:S(2)}) copy-start(bf16[256,2,256]{2,1,0:T(2,128)(2,1)} %values_ref.1) | copy-start | bytes 786436

commit v4 on v3

--- a/solution.py
+++ b/solution.py
@@ -15,6 +15,7 @@
 SIGNALS = 8
 GROUPS_HERE = 4
 KEPT = 64
+TILE = 16
 FULL = 2 * BLOCKS * ROWS
 
 
@@ -28,7 +29,8 @@
     kept = np.arange(KEPT)[:, None]
     block = np.arange(BLOCKS)[None, :]
     coarse = 2 * math.pi * (((2 * kept + 1) * block) % (4 * BLOCKS)) / (4 * BLOCKS)
-    enter_high, enter_low = split_table(np.concatenate([np.cos(coarse), -np.sin(coarse)], axis=0))
+    paired = np.stack([np.cos(coarse), -np.sin(coarse)]).reshape(2, -1, TILE, BLOCKS)
+    enter_high, enter_low = split_table(paired.swapaxes(0, 1).reshape(2 * KEPT, BLOCKS))
     enter = np.concatenate([enter_high, enter_low], axis=1)
     leave_high, leave_low = split_table(
         np.concatenate([np.cos(coarse.T), -np.sin(coarse.T)], axis=1) * (2.0 / FULL)
@@ -95,8 +97,6 @@
             recv_ref[:, :, lanes].astype(jnp.float32).reshape(BLOCKS * SIGNALS, HALF)
         )
     enter = enter_ref[...]
-    turn_cos = cos_ref[...]
-    turn_sin = sin_ref[...]
 
     def every(row):
         return pl.ds(row, BLOCKS, stride=SIGNALS)
@@ -135,17 +135,19 @@
                 [wide_ref[lane, every(row), :] for lane, row in places(group, item)], axis=1
             ).astype(jnp.bfloat16)
             first = mxu(enter, jnp.concatenate([taken, taken], axis=0))
-            real, imag = first[:KEPT], first[KEPT:]
-            turned_real = real * turn_cos + imag * turn_sin
-            turned_imag = imag * turn_cos - real * turn_sin
-            for odd in (0, 1):
-                sign = 1.0 - 2.0 * odd
-                put(
-                    odd,
-                    spot(group, item),
-                    turned_real[:, :HALF] + sign * turned_real[:, HALF:],
-                    turned_imag[:, :HALF] + sign * turned_imag[:, HALF:],
-                )
+            start = spot(group, item).start
+            for tile in range(0, KEPT, TILE):
+                real = first[2 * tile : 2 * tile + TILE]
+                imag = first[2 * tile + TILE : 2 * tile + 2 * TILE]
+                turn_cos = cos_ref[tile : tile + TILE, :]
+                turn_sin = sin_ref[tile : tile + TILE, :]
+                turned_real = real * turn_cos + imag * turn_sin
+                turned_imag = imag * turn_cos - real * turn_sin
+                rows = slice(start + tile, start + tile + TILE)
+                near_real, far_real = turned_real[:, :HALF], turned_real[:, HALF:]
+                near_imag, far_imag = turned_imag[:, :HALF], turned_imag[:, HALF:]
+                put(0, rows, near_real + far_real, near_imag + far_imag)
+                put(1, rows, near_real - far_real, near_imag - far_imag)
 
     def forth_group(group):
         rows = slice(group * count * KEPT, (group + 1) * count * KEPT)
@@ -154,52 +156,61 @@
 
     def multiply_group(group):
         for odd in (0, 1):
-
-            def spectrum(item):
-                rows = spot(group, item)
-                return spec_ref[odd, rows, :HALF], spec_ref[odd, rows, HALF:]
-
-            tap_real, tap_imag = spectrum(2 * members)
-            lag_real = lag_imag = None
-            for member in range(members):
-                in_real, in_imag = spectrum(member)
-                cot_real, cot_imag = spectrum(members + member)
-                put(
-                    odd,
-                    spot(group, member),
-                    in_real * tap_real - in_imag * tap_imag,
-                    in_real * tap_imag + in_imag * tap_real,
-                )
-                put(
-                    odd,
-                    spot(group, members + member),
-                    cot_real * tap_real + cot_imag * tap_imag,
-                    cot_imag * tap_real - cot_real * tap_imag,
-                )
-                more_real = cot_real * in_real + cot_imag * in_imag
-                more_imag = cot_imag * in_real - cot_real * in_imag
-                lag_real = more_real if member == 0 else lag_real + more_real
-                lag_imag = more_imag if member == 0 else lag_imag + more_imag
-            put(odd, spot(group, 2 * members), lag_real, lag_imag)
+            for tile in range(0, KEPT, TILE):
+
+                def tiled(item):
+                    start = spot(group, item).start + tile
+                    return slice(start, start + TILE)
+
+                def spectrum(item):
+                    rows = tiled(item)
+                    return spec_ref[odd, rows, :HALF], spec_ref[odd, rows, HALF:]
+
+                tap_real, tap_imag = spectrum(2 * members)
+                lag_real = lag_imag = None
+                for member in range(members):
+                    in_real, in_imag = spectrum(member)
+                    cot_real, cot_imag = spectrum(members + member)
+                    put(
+                        odd,
+                        tiled(member),
+                        in_real * tap_real - in_imag * tap_imag,
+                        in_real * tap_imag + in_imag * tap_real,
+                    )
+                    put(
+                        odd,
+                        tiled(members + member),
+                        cot_real * tap_real + cot_imag * tap_imag,
+                        cot_imag * tap_real - cot_real * tap_imag,
+                    )
+                    more_real = cot_real * in_real + cot_imag * in_imag
+                    more_imag = cot_imag * in_real - cot_real * in_imag
+                    lag_real = more_real if member == 0 else lag_real + more_real
+                    lag_imag = more_imag if member == 0 else lag_imag + more_imag
+                put(odd, tiled(2 * members), lag_real, lag_imag)
 
     def back_group(group):
         rows = slice(group * count * KEPT, (group + 1) * count * KEPT)
-        even_part = both(back_ref, 0, rows)
-        odd_part = both(back_ref, 1, rows)
-        turn_ref[0, rows, :] = even_part + odd_part
-        turn_ref[1, rows, :] = even_part - odd_part
+        for odd in (0, 1):
+            turn_ref[odd, rows, :] = both(back_ref, odd, rows)
 
     def leave_group(group):
         for item in range(count):
-            rows = spot(group, item)
-            real = jnp.concatenate([turn_ref[0, rows, :HALF], turn_ref[1, rows, :HALF]], axis=1)
-            imag = jnp.concatenate([turn_ref[0, rows, HALF:], turn_ref[1, rows, HALF:]], axis=1)
-            real_high, real_low = halves(real * turn_cos - imag * turn_sin)
-            imag_high, imag_low = halves(imag * turn_cos + real * turn_sin)
-            result = mxu(
-                leave,
-                jnp.concatenate([real_high, imag_high, real_low, imag_low], axis=0),
-            )
+            start = spot(group, item).start
+            pieces = [[], [], [], []]
+            for tile in range(0, KEPT, TILE):
+                rows = slice(start + tile, start + tile + TILE)
+                turn_cos = cos_ref[tile : tile + TILE, :]
+                turn_sin = sin_ref[tile : tile + TILE, :]
+                even, odd = turn_ref[0, rows, :], turn_ref[1, rows, :]
+                near, far = even + odd, even - odd
+                real = jnp.concatenate([near[:, :HALF], far[:, :HALF]], axis=1)
+                imag = jnp.concatenate([near[:, HALF:], far[:, HALF:]], axis=1)
+                real_high, real_low = halves(real * turn_cos - imag * turn_sin)
+                imag_high, imag_low = halves(imag * turn_cos + real * turn_sin)
+                for kept, piece in zip(pieces, (real_high, imag_high, real_low, imag_low)):
+                    kept.append(piece)
+            result = mxu(leave, jnp.concatenate(sum(pieces, []), axis=0))
             result = result[:BLOCKS] + result[BLOCKS:]
             for part, (lane, row) in enumerate(places(group, item)):
                 wide_ref[lane, every(row), :] = result[:, part * HALF : (part + 1) * HALF]
@@ -316,6 +327,24 @@
     )
 
 
+def lag_kernel(returned_ref, lag_ref, done):
+    copy = pltpu.make_async_copy(returned_ref.at[:, :, pl.ds(4 * HALF, HALF)], lag_ref, done)
+    copy.start()
+    copy.wait()
+
+
+def lag_chunks(returned):
+    return pl.pallas_call(
+        lag_kernel,
+        out_shape=jax.ShapeDtypeStruct((BLOCKS, SIGNALS, HALF), jnp.bfloat16),
+        in_specs=[pl.BlockSpec(memory_space=pltpu.VMEM)],
+        out_specs=pl.BlockSpec(memory_space=pl.ANY),
+        scratch_shapes=[pltpu.SemaphoreType.DMA],
+        compiler_params=pltpu.CompilerParams(vmem_limit_bytes=16 * 1024 * 1024),
+        name="lags",
+    )(returned)
+
+
 def unchunks(received, member_count):
     return (
         received.reshape(BLOCKS, member_count, GROUPS_HERE, ROWS)
@@ -338,9 +367,7 @@
     chan_count = lax.axis_size("chan")
     outgoing = gated_chunks(out_gate, in_gate, values_in, filter_taps, out_cotangent)
     returned = exchange(spectral(exchange(outgoing, "seq")), "seq")
-    lag_terms = exchange(
-        returned[:, :, 4 * HALF :].reshape(chan_count, -1, SIGNALS, HALF), "chan"
-    )
+    lag_terms = exchange(lag_chunks(returned).reshape(chan_count, -1, SIGNALS, HALF), "chan")
     norm_factor = 1.0 / math.sqrt(BLOCKS * row_count * member_count * chan_count)
     lag_sum = jnp.sum(lag_terms.astype(jnp.float32), axis=0)
     grad_filter = (

time: 85.2 us -> 85.1 us (level)
  no operation moved by 1% of the time
where the time goes in v4:
time: 85.1 us; the launch traced here: 84.7 us
  blocking collectives  56.9 us (67%)
  starting transfers between devices  10.3 us (12%)
  Pallas kernels  6.86 us (8%)
  local copies, waits for them, and re-layouts  6.8 us (8%)
  waiting for transfers between devices  2.47 us (3%)
  between operations  0.86 us (1%)
    all_to_all x2, blocking collectives, exchange(): return lax.all_to_all(value, axis, split_axis=0, concat_axis=0, tiled=True)  56.9 us
    all_to_all x1, starting transfers between devices, exchange(): return lax.all_to_all(value, axis, split_axis=0, concat_axis=0, tiled=True)  10.3 us
    unnamed x27, local copies, waits for them, and re-layouts  5.49 us
    pallas_call x1, Pallas kernels, spectral(): pl.pallas_call(spectral_kernel, out_shape=jax.ShapeDtypeStruct((BLOCKS, S...  3.93 us
    all_to_all x1, waiting for transfers between devices, exchange(): return lax.all_to_all(value, axis, split_axis=0, concat_axis=0, tiled=True)  2.47 us
    pallas_call x1, Pallas kernels, gated_chunks(): pl.pallas_call(gate_kernel, out_shape=jax.ShapeDtypeStruct((BLOCKS, SIGNA...  2.28 us
  transfers between devices with their start and end apart: 1, of which 1 were waited for; matrix products, arithmetic and copies ran while one was open for 7% of the time, Pallas kernels for 0%

profile of v4, /device:TPU:6, one launch (start us, length us, event | category | flops | bytes accessed | tf_op | source)
XLA Modules:
  0.0 84.7 jit_solution(2561736167745592254)
XLA Ops:
  0.6 0.0 copy-start.1
  0.6 2.3 %gates.1 = bf16[64,8,640]{2,1,0:T(8,128)(2,1)S(1)} custom-call(bf16[256,2,256]{2,1,0:T(2,128)(2,1)} %out_gate_ref.1, bf16[256,2,256]{2,1,0:T(2,128)(2,1)} %in_gate_ref.1, bf16[256,2,256]{2,1,0:T(2,128)(2,1)} %values_ref.1, bf16[256,256]{1,0:T(8,128)(2,1)} %taps_ref.1, bf16[256,2,256]{2,1,0:T(2,128)(2,1)} %cot_ref.1), custom_call_target="tpu_custom_call" | custom-call | flops 400000000 | bytes 2000000 | tf_op jit(solution)/shard_map/gates/pallas_call | solution.py:307
  2.9 0.0 copy-start
  2.9 0.0 copy-start.2
  3.0 0.0 copy-start.3
  3.0 0.0 copy-start.4
  3.0 0.0 copy-start.5
  3.0 30.9 %all_to_all.15.recv_ref = bf16[64,8,640]{2,1,0:T(8,128)(2,1)S(1)} all-to-all(bf16[64,8,640]{2,1,0:T(8,128)(2,1)S(1)} %gates.1), channel_id=1, replica_groups=mesh['seq'=64,'chan'=8] {'seq'}, dimensions={0} | all-to-all | bytes 1310720 | tf_op jit(solution)/shard_map/all_to_all | solution.py:362
  34.0 3.9 %spectral.1 = bf16[64,8,640]{2,1,0:T(8,128)(2,1)S(1)} custom-call(bf16[64,8,640]{2,1,0:T(8,128)(2,1)S(1)} %all_to_all.15.recv_ref, bf16[128,128]{1,0:T(8,128)(2,1)S(1)} %copy-done.5, bf16[128,256]{1,0:T(8,128)(2,1)S(1)} %copy-done.4, f32[64,256]{1,0:T(8,128)S(1)} %copy-done.3, f32[64,256]{1,0:T(8,128)S(1)} %copy-done.2, bf16[2,768,256]{2,1,0:T(8,128)(2,1)S(1)} %copy-done.1, ...), custom_call_target="tpu_custom_call" | custom-call | flops 6000000000 | bytes 3000000 | tf_op jit(solution)/shard_map/spectral/pallas_call | solution.py:233
  37.9 26.0 %all_to_all.16.returned_ref = bf16[64,8,640]{2,1,0:T(8,128)(2,1)S(1)} all-to-all(bf16[64,8,640]{2,1,0:T(8,128)(2,1)S(1)} %spectral.1), channel_id=1, replica_groups=mesh['seq'=64,'chan'=8] {'seq'}, dimensions={0} | all-to-all | bytes 1310720 | tf_op jit(solution)/shard_map/all_to_all | solution.py:362
  63.9 0.7 lags.1
  64.6 10.3 %all-to-all-start.2 = ((bf16[8,8,8,128]{3,2,1,0:T(8,128)(2,1)}), bf16[8,8,8,128]{3,2,1,0:T(8,128)(2,1)S(1)}, u32[]{:S(2)}, u32[]{:S(2)}) async-start(bf16[8,8,8,128]{3,2,1,0:T(8,128)(2,1)} %bitcast.4), calls=%async_computation.2 | async-start | bytes 262144 | tf_op jit(solution)/shard_map/all_to_all | solution.py:362
  74.9 0.1 slice_convert_fusion
  75.0 0.1 reshape.36
  75.2 0.3 copy.61
  75.4 0.2 copy.62
  75.7 0.1 reshape.35
  75.8 0.0 copy-start.10
  75.8 0.3 copy.56
  76.2 0.2 copy.59
  76.4 0.1 copy-done.10
  76.5 0.6 copy-done.6
  77.1 0.1 copy-done.7
  77.1 0.1 copy-done.8
  77.2 0.1 copy-done.9
  77.3 0.3 fusion.6
  77.6 1.0 %copy.66 = bf16[256,2,256]{2,1,0:T(2,128)(2,1)} copy(bf16[256,2,256]{2,0,1:T(8,128)(2,1)S(1)} %get-tuple-element.27) | data formatting | bytes 524288
  78.6 1.0 %copy.65 = bf16[256,2,256]{2,1,0:T(2,128)(2,1)} copy(bf16[256,2,256]{2,0,1:T(8,128)(2,1)S(1)} %get-tuple-element.28) | data formatting | bytes 524288
  79.6 1.0 %copy.67 = bf16[256,2,256]{2,1,0:T(2,128)(2,1)} copy(bf16[256,2,256]{2,0,1:T(8,128)(2,1)S(1)} %get-tuple-element.29) | data formatting | bytes 524288
  80.6 1.0 %copy.68 = bf16[256,2,256]{2,1,0:T(2,128)(2,1)} copy(bf16[256,2,256]{2,0,1:T(8,128)(2,1)S(1)} %get-tuple-element.30) | data formatting | bytes 524288
  81.5 2.5 %all-to-all-done.2 = bf16[8,8,8,128]{3,2,1,0:T(8,128)(2,1)S(1)} async-done(((bf16[8,8,8,128]{3,2,1,0:T(8,128)(2,1)}), bf16[8,8,8,128]{3,2,1,0:T(8,128)(2,1)S(1)}, u32[]{:S(2)}, u32[]{:S(2)}) %all-to-all-start.2) | async-done | bytes 131104 | tf_op jit(solution)/shard_map/all_to_all | solution.py:362
  84.1 0.6 copy.95
  (14 shorter events, 0.1 us)
Async XLA Ops:
  0.6 33.3 %copy-start.1 = (bf16[2,768,256]{2,1,0:T(8,128)(2,1)S(1)}, bf16[2,768,256]{2,1,0:T(8,128)(2,1)}, u32[]{:S(2)}) copy-start(bf16[2,768,256]{2,1,0:T(8,128)(2,1)} %constant.20.clone.forth_ref) | copy-start | bytes 2359300
  2.9 31.0 %copy-start = (bf16[2,768,256]{2,1,0:T(8,128)(2,1)S(1)}, bf16[2,768,256]{2,1,0:T(8,128)(2,1)}, u32[]{:S(2)}) copy-start(bf16[2,768,256]{2,1,0:T(8,128)(2,1)} %constant.21.clone.back_ref) | copy-start | bytes 2359300
  2.9 31.0 %copy-start.2 = (f32[64,256]{1,0:T(8,128)S(1)}, f32[64,256]{1,0:T(8,128)}, u32[]{:S(2)}) copy-start(f32[64,256]{1,0:T(8,128)} %constant.19.clone.sin_ref) | copy-start | bytes 196612
  3.0 31.0 %copy-start.3 = (f32[64,256]{1,0:T(8,128)S(1)}, f32[64,256]{1,0:T(8,128)}, u32[]{:S(2)}) copy-start(f32[64,256]{1,0:T(8,128)} %constant.18.clone.cos_ref) | copy-start | bytes 196612
  3.0 31.0 %copy-start.4 = (bf16[128,256]{1,0:T(8,128)(2,1)S(1)}, bf16[128,256]{1,0:T(8,128)(2,1)}, u32[]{:S(2)}) copy-start(bf16[128,256]{1,0:T(8,128)(2,1)} %constant.17.clone.leave_ref) | copy-start | bytes 196612
  3.0 31.0 %copy-start.5 = (bf16[128,128]{1,0:T(8,128)(2,1)S(1)}, bf16[128,128]{1,0:T(8,128)(2,1)}, u32[]{:S(2)}) copy-start(bf16[128,128]{1,0:T(8,128)(2,1)} %constant.16.clone.enter_ref) | copy-start | bytes 98308
  64.6 19.4 %all-to-all-start.2 = ((bf16[8,8,8,128]{3,2,1,0:T(8,128)(2,1)}), bf16[8,8,8,128]{3,2,1,0:T(8,128)(2,1)S(1)}, u32[]{:S(2)}, u32[]{:S(2)}) async-start(bf16[8,8,8,128]{3,2,1,0:T(8,128)(2,1)} %bitcast.4), calls=%async_computation.2 | async-start | bytes 262144 | tf_op jit(solution)/shard_map/all_to_all | solution.py:362
  75.8 0.7 copy-start.10
  76.1 1.0 %copy-start.6 = (bf16[256,2,256]{2,1,0:T(2,128)(2,1)S(1)}, bf16[256,2,256]{2,1,0:T(2,128)(2,1)}, u32[]{:S(2)}) copy-start(bf16[256,2,256]{2,1,0:T(2,128)(2,1)} %cot_ref.1) | copy-start | bytes 786436
  76.1 1.0 %copy-start.7 = (bf16[256,2,256]{2,1,0:T(2,128)(2,1)S(1)}, bf16[256,2,256]{2,1,0:T(2,128)(2,1)}, u32[]{:S(2)}) copy-start(bf16[256,2,256]{2,1,0:T(2,128)(2,1)} %out_gate_ref.1) | copy-start | bytes 786436
  76.1 1.1 %copy-start.8 = (bf16[256,2,256]{2,1,0:T(2,128)(2,1)S(1)}, bf16[256,2,256]{2,1,0:T(2,128)(2,1)}, u32[]{:S(2)}) copy-start(bf16[256,2,256]{2,1,0:T(2,128)(2,1)} %in_gate_ref.1) | copy-start | bytes 786436
  76.1 1.2 %copy-start.9 = (bf16[256,2,256]{2,1,0:T(2,128)(2,1)S(1)}, bf16[256,2,256]{2,1,0:T(2,128)(2,1)}, u32[]{:S(2)}) copy-start(bf16[256,2,256]{2,1,0:T(2,128)(2,1)} %values_ref.1) | copy-start | bytes 786436

commit v5 on v3

v5 whole, which is shorter than its diff:
```python
import functools
import math

import jax
import jax.numpy as jnp
import ml_dtypes
import numpy as np
from jax import lax
from jax.experimental import pallas as pl
from jax.experimental.pallas import tpu as pltpu
from jax.sharding import PartitionSpec as P

BLOCKS = 64
ROWS = 256
HALF = ROWS // 2
SIGNALS = 8
GROUPS_HERE = 4
KEPT = 64
TILE = 16
FULL = 2 * BLOCKS * ROWS


def split_table(table):
    high = table.astype(ml_dtypes.bfloat16)
    low = (table - high.astype(np.float64)).astype(ml_dtypes.bfloat16)
    return high, low


def tables():
    kept = np.arange(KEPT)[:, None]
    block = np.arange(BLOCKS)[None, :]
    coarse = 2 * math.pi * (((2 * kept + 1) * block) % (4 * BLOCKS)) / (4 * BLOCKS)
    paired = np.stack([np.cos(coarse), -np.sin(coarse)]).reshape(2, -1, TILE, BLOCKS)
    enter_high, enter_low = split_table(paired.swapaxes(0, 1).reshape(2 * KEPT, BLOCKS))
    enter = np.concatenate([enter_high, enter_low], axis=1)
    leave_high, leave_low = split_table(
        np.concatenate([np.cos(coarse.T), -np.sin(coarse.T)], axis=1) * (2.0 / FULL)
    )
    leave = np.concatenate(
        [
            np.concatenate([leave_high, leave_high], axis=1),
            np.concatenate([leave_low, np.zeros_like(leave_low)], axis=1),
        ]
    )
    row = np.arange(ROWS)[None, :]
    twist = 2 * math.pi * (kept + 0.5) * row / FULL
    turn_cos = np.cos(twist).astype(np.float32)
    turn_sin = np.sin(twist).astype(np.float32)
    fine = []
    for odd in (0, 1):
        angle = (
            2
            * math.pi
            * ((np.arange(HALF)[:, None] * (2 * np.arange(HALF)[None, :] + odd)) % ROWS)
            / ROWS
        )
        cos, sin = np.cos(angle), np.sin(angle)
        forth = np.concatenate(
            [np.concatenate([cos, -sin], axis=1), np.concatenate([sin, cos], axis=1)], axis=0
        )
        fine.append((split_table(forth), split_table(forth.T)))
    forth, back = (
        np.stack([np.concatenate([high, low, high]) for high, low in (pair[way] for pair in fine)])
        for way in (0, 1)
    )
    return enter, leave, turn_cos, turn_sin, forth, back


def mxu(left, right):
    return jnp.dot(left, right, preferred_element_type=jnp.float32)


def halves(value):
    high = value.astype(jnp.bfloat16)
    low = (value - high.astype(jnp.float32)).astype(jnp.bfloat16)
    return high, low


class Stages:
    def __init__(self, cos_ref, sin_ref, enter_ref, leave_ref, forth_ref, back_ref):
        self.cos_ref = cos_ref
        self.sin_ref = sin_ref
        self.enter_ref = enter_ref
        self.leave_ref = leave_ref
        self.forth_ref = forth_ref
        self.back_ref = back_ref

    def put(self, pair, odd, rows, real, imag):
        for part, value in enumerate((real, imag)):
            lanes = slice(part * HALF, (part + 1) * HALF)
            for ref, piece in zip(pair, halves(value)):
                ref[odd, rows, lanes] = piece

    def both(self, pair, matrix_ref, odd, rows):
        high = pair[0][odd, rows, :]
        return mxu(jnp.concatenate([pair[1][odd, rows, :], high, high], axis=1), matrix_ref[odd])

    def turns(self, tile):
        return self.cos_ref[tile : tile + TILE, :], self.sin_ref[tile : tile + TILE, :]

    def enter(self, taken, pair, start):
        first = mxu(self.enter_ref[...], jnp.concatenate([taken, taken], axis=0))
        for tile in range(0, KEPT, TILE):
            real = first[2 * tile : 2 * tile + TILE]
            imag = first[2 * tile + TILE : 2 * tile + 2 * TILE]
            turn_cos, turn_sin = self.turns(tile)
            turned_real = real * turn_cos + imag * turn_sin
            turned_imag = imag * turn_cos - real * turn_sin
            rows = slice(start + tile, start + tile + TILE)
            near_real, far_real = turned_real[:, :HALF], turned_real[:, HALF:]
            near_imag, far_imag = turned_imag[:, :HALF], turned_imag[:, HALF:]
            self.put(pair, 0, rows, near_real + far_real, near_imag + far_imag)
            self.put(pair, 1, rows, near_real - far_real, near_imag - far_imag)

    def forth(self, pair, spec_ref, rows):
        for odd in (0, 1):
            spec_ref[odd, rows, :] = self.both(pair, self.forth_ref, odd, rows)

    def back(self, pair, turn_ref, rows):
        for odd in (0, 1):
            turn_ref[odd, rows, :] = self.both(pair, self.back_ref, odd, rows)

    def leave(self, turn_ref, start):
        pieces = [[], [], [], []]
        for tile in range(0, KEPT, TILE):
            rows = slice(start + tile, start + tile + TILE)
            turn_cos, turn_sin = self.turns(tile)
            even, odd = turn_ref[0, rows, :], turn_ref[1, rows, :]
            near, far = even + odd, even - odd
            real = jnp.concatenate([near[:, :HALF], far[:, :HALF]], axis=1)
            imag = jnp.concatenate([near[:, HALF:], far[:, HALF:]], axis=1)
            real_high, real_low = halves(real * turn_cos - imag * turn_sin)
            imag_high, imag_low = halves(imag * turn_cos + real * turn_sin)
            for kept, piece in zip(pieces, (real_high, imag_high, real_low, imag_low)):
                kept.append(piece)
        result = mxu(self.leave_ref[...], jnp.concatenate(sum(pieces, []), axis=0))
        return result[:BLOCKS] + result[BLOCKS:]


MEMBERS = SIGNALS // GROUPS_HERE
PAIRS = 2 * MEMBERS
GROUP_ROWS = PAIRS * KEPT


def every(row):
    return pl.ds(row, BLOCKS, stride=SIGNALS)


def spread(wide_ref, lane, received):
    wide_ref[lane] = received.astype(jnp.float32).reshape(BLOCKS * SIGNALS, HALF)


def gather(wide_ref, lane):
    return wide_ref[lane].reshape(BLOCKS, SIGNALS, HALF).astype(jnp.bfloat16)


def places(group, item):
    which, member = divmod(item, MEMBERS)
    row = member * GROUPS_HERE + group
    return ((2 * which, row), (2 * which + 1, row))


def spot(group, item, offset=0, size=KEPT):
    start = (group * PAIRS + item) * KEPT + offset
    return slice(start, start + size)


def lag_kernel(
    recv_ref,
    enter_ref,
    leave_ref,
    cos_ref,
    sin_ref,
    forth_ref,
    back_ref,
    lag_ref,
    spec_ref,
    wide_ref,
    high_ref,
    low_ref,
    high_lag_ref,
    low_lag_ref,
    turn_ref,
    wide_lag_ref,
):
    stages = Stages(cos_ref, sin_ref, enter_ref, leave_ref, forth_ref, back_ref)
    pair, joined = (high_ref, low_ref), (high_lag_ref, low_lag_ref)
    for lane in range(4):
        spread(wide_ref, lane, recv_ref[:, :, lane * HALF : (lane + 1) * HALF])
    for group in range(GROUPS_HERE):
        for item in range(PAIRS):
            taken = jnp.concatenate(
                [wide_ref[lane, every(row), :] for lane, row in places(group, item)], axis=1
            ).astype(jnp.bfloat16)
            stages.enter(taken, pair, spot(group, item).start)
    for group in range(GROUPS_HERE):
        stages.forth(pair, spec_ref, slice(group * GROUP_ROWS, (group + 1) * GROUP_ROWS))
    for group in range(GROUPS_HERE):
        for odd in (0, 1):
            for tile in range(0, KEPT, TILE):
                real = imag = None
                for member in range(MEMBERS):
                    rows = spot(group, member, tile, TILE)
                    in_real, in_imag = spec_ref[odd, rows, :HALF], spec_ref[odd, rows, HALF:]
                    rows = spot(group, MEMBERS + member, tile, TILE)
                    cot_real, cot_imag = spec_ref[odd, rows, :HALF], spec_ref[odd, rows, HALF:]
                    more_real = cot_real * in_real + cot_imag * in_imag
                    more_imag = cot_imag * in_real - cot_real * in_imag
                    real = more_real if member == 0 else real + more_real
                    imag = more_imag if member == 0 else imag + more_imag
                start = group * KEPT + tile
                stages.put(joined, odd, slice(start, start + TILE), real, imag)
    stages.back(joined, turn_ref, slice(0, GROUPS_HERE * KEPT))
    for group in range(GROUPS_HERE):
        result = stages.leave(turn_ref, group * KEPT)
        wide_lag_ref[0, every(group), :] = result[:, :HALF]
        wide_lag_ref[0, every(group + GROUPS_HERE), :] = result[:, HALF:]
    lag_ref[...] = gather(wide_lag_ref, 0)


def signal_kernel(
    plane_ref,
    skip_ref,
    recv_ref,
    spec_ref,
    wide_ref,
    enter_ref,
    leave_ref,
    cos_ref,
    sin_ref,
    forth_ref,
    back_ref,
    send_ref,
    wide_taps_ref,
    high_taps_ref,
    low_taps_ref,
    spec_taps_ref,
    high_ref,
    low_ref,
    turn_ref,
    wide_out_ref,
):
    stages = Stages(cos_ref, sin_ref, enter_ref, leave_ref, forth_ref, back_ref)
    taps_pair, pair = (high_taps_ref, low_taps_ref), (high_ref, low_ref)
    first_group = plane_ref[1] * GROUPS_HERE
    spread(wide_taps_ref, 0, recv_ref[:, :, 4 * HALF :])
    for group in range(GROUPS_HERE):
        taken = jnp.concatenate(
            [
                wide_taps_ref[0, every(group), :],
                wide_taps_ref[0, every(group + GROUPS_HERE), :],
            ],
            axis=1,
        ).astype(jnp.bfloat16)
        stages.enter(taken, taps_pair, group * KEPT)
    stages.forth(taps_pair, spec_taps_ref, slice(0, GROUPS_HERE * KEPT))

    def multiply(group):
        for odd in (0, 1):
            for tile in range(0, KEPT, TILE):
                rows = slice(group * KEPT + tile, group * KEPT + tile + TILE)
                tap_real, tap_imag = spec_taps_ref[odd, rows, :HALF], spec_taps_ref[odd, rows, HALF:]
                for item in range(PAIRS):
                    rows = spot(group, item, tile, TILE)
                    real, imag = spec_ref[odd, rows, :HALF], spec_ref[odd, rows, HALF:]
                    turn = tap_imag if item < MEMBERS else -tap_imag
                    stages.put(
                        pair,
                        odd,
                        rows,
                        real * tap_real - imag * turn,
                        real * turn + imag * tap_real,
                    )

    def back(group):
        stages.back(pair, turn_ref, slice(group * GROUP_ROWS, (group + 1) * GROUP_ROWS))

    def leave(group):
        for item in range(PAIRS):
            result = stages.leave(turn_ref, spot(group, item).start)
            gain = skip_ref[item % MEMBERS, first_group + group]
            for part, (lane, row) in enumerate(places(group, item)):
                direct = wide_ref[lane, every(row), :] * gain
                wide_out_ref[lane, every(row), :] = (
                    result[:, part * HALF : (part + 1) * HALF] + direct
                )

    for step in range(GROUPS_HERE + 2):
        for lag, stage in enumerate((multiply, back, leave)):
            if 0 <= step - lag < GROUPS_HERE:
                stage(step - lag)
    for lane in range(4):
        send_ref[:, :, lane * HALF : (lane + 1) * HALF] = gather(wide_out_ref, lane)


def spectral(received, plane, skip_gain, send_lag):
    constants = [jnp.asarray(table) for table in tables()]
    signal_rows, group_rows = GROUPS_HERE * GROUP_ROWS, GROUPS_HERE * KEPT
    whole = pl.BlockSpec(memory_space=pltpu.VMEM)
    scalar = pl.BlockSpec(memory_space=pltpu.SMEM)
    params = pltpu.CompilerParams(vmem_limit_bytes=24 * 1024 * 1024)
    lag, spec, wide = pl.pallas_call(
        lag_kernel,
        out_shape=(
            jax.ShapeDtypeStruct((BLOCKS, SIGNALS, HALF), jnp.bfloat16),
            jax.ShapeDtypeStruct((2, signal_rows, ROWS), jnp.float32),
            jax.ShapeDtypeStruct((4, BLOCKS * SIGNALS, HALF), jnp.float32),
        ),
        in_specs=[whole] * 7,
        out_specs=(whole,) * 3,
        scratch_shapes=[
            pltpu.VMEM((2, signal_rows, ROWS), jnp.bfloat16),
            pltpu.VMEM((2, signal_rows, ROWS), jnp.bfloat16),
            pltpu.VMEM((2, group_rows, ROWS), jnp.bfloat16),
            pltpu.VMEM((2, group_rows, ROWS), jnp.bfloat16),
            pltpu.VMEM((2, group_rows, ROWS), jnp.float32),
            pltpu.VMEM((1, BLOCKS * SIGNALS, HALF), jnp.float32),
        ],
        compiler_params=params,
        cost_estimate=pl.CostEstimate(
            flops=3_000_000_000, bytes_accessed=5_000_000, transcendentals=0
        ),
        name="lags",
    )(received, *constants)
    moved = send_lag(lag)
    signals = pl.pallas_call(
        signal_kernel,
        out_shape=jax.ShapeDtypeStruct((BLOCKS, SIGNALS, 4 * HALF), jnp.bfloat16),
        in_specs=[scalar] * 2 + [whole] * 9,
        out_specs=whole,
        scratch_shapes=[
            pltpu.VMEM((1, BLOCKS * SIGNALS, HALF), jnp.float32),
            pltpu.VMEM((2, group_rows, ROWS), jnp.bfloat16),
            pltpu.VMEM((2, group_rows, ROWS), jnp.bfloat16),
            pltpu.VMEM((2, group_rows, ROWS), jnp.float32),
            pltpu.VMEM((2, signal_rows, ROWS), jnp.bfloat16),
            pltpu.VMEM((2, signal_rows, ROWS), jnp.bfloat16),
            pltpu.VMEM((2, signal_rows, ROWS), jnp.float32),
            pltpu.VMEM((4, BLOCKS * SIGNALS, HALF), jnp.float32),
        ],
        compiler_params=params,
        cost_estimate=pl.CostEstimate(
            flops=3_000_000_000, bytes_accessed=5_000_000, transcendentals=0
        ),
        name="signals",
    )(plane, skip_gain, received, spec, wide, *constants)
    return jnp.concatenate([signals, moved], axis=2)


RING = 8


def shift(row, column):
    return (row + RING // 2 * (column % 2)) % RING


def holders(plane):
    return [
        [lax.rem(first - RING // 2 * odd + 2 * RING - plane, RING) for odd in (0, 1)]
        for first in range(RING)
    ]


def gate_kernel(
    plane_ref,
    out_gate_ref,
    in_gate_ref,
    values_ref,
    taps_ref,
    cot_ref,
    send_ref,
    gates_ref,
    held_taps_ref,
    arrived,
):
    sources = (in_gate_ref, values_ref, cot_ref, out_gate_ref)
    copies = [
        pltpu.make_async_copy(source, gates_ref.at[slot], arrived.at[slot])
        for slot, source in enumerate(sources)
    ]
    copies.append(pltpu.make_async_copy(taps_ref, held_taps_ref, arrived.at[len(sources)]))
    for copy in copies:
        copy.start()

    row = lax.broadcasted_iota(jnp.int32, (2 * ROWS, 2 * ROWS), 0)
    column = lax.broadcasted_iota(jnp.int32, (2 * ROWS, 2 * ROWS), 1)
    parted = (row == column % ROWS * 2 + column // ROWS).astype(jnp.float32)
    parted = parted.astype(jnp.bfloat16)
    plain = (row == column)[:ROWS, :ROWS].astype(jnp.float32).astype(jnp.bfloat16)

    def turned(value, order):
        return lax.dot_general(
            value, order, (((0,), (0,)), ((), ())), preferred_element_type=jnp.float32
        ).astype(jnp.bfloat16)

    owners = holders(plane_ref[0])

    def send(part, lanes, value):
        rows = slice(part * GROUPS_HERE, (part + 1) * GROUPS_HERE)
        value = value.reshape(BLOCKS, GROUPS_HERE, -1)
        for first in range(RING):
            for second in range(RING):
                send_ref[owners[first][second % 2], second, rows, lanes] = value[
                    first * RING + second
                ]

    for which in range(2):
        left, right = 2 * which, 2 * which + 1
        copies[left].wait()
        copies[right].wait()
        product = gates_ref[left].reshape(2 * ROWS, ROWS).astype(jnp.float32) * gates_ref[
            right
        ].reshape(2 * ROWS, ROWS).astype(jnp.float32)
        signal = turned(product.astype(jnp.bfloat16), parted)
        for member in range(2):
            send(
                member,
                slice(which * ROWS, (which + 1) * ROWS),
                signal[:, member * ROWS : (member + 1) * ROWS],
            )
    copies[-1].wait()
    taps = turned(held_taps_ref[...], plain)
    for half in range(2):
        send(half, slice(2 * ROWS, None), taps[:, half * HALF : (half + 1) * HALF])


def gated_chunks(plane, out_gate, in_gate, values_in, filter_taps, out_cotangent):
    return pl.pallas_call(
        gate_kernel,
        out_shape=jax.ShapeDtypeStruct((RING, RING, SIGNALS, 5 * HALF), jnp.bfloat16),
        in_specs=[pl.BlockSpec(memory_space=pltpu.SMEM)]
        + [pl.BlockSpec(memory_space=pltpu.HBM)] * 5,
        out_specs=pl.BlockSpec(memory_space=pltpu.VMEM),
        scratch_shapes=[
            pltpu.VMEM((4, ROWS, 2, ROWS), jnp.bfloat16),
            pltpu.VMEM((ROWS, ROWS), jnp.bfloat16),
            pltpu.SemaphoreType.DMA((5,)),
        ],
        compiler_params=pltpu.CompilerParams(vmem_limit_bytes=16 * 1024 * 1024),
        cost_estimate=pl.CostEstimate(
            flops=400_000_000, bytes_accessed=2_000_000, transcendentals=0
        ),
        name="gates",
    )(
        plane,
        *(
            pltpu.with_memory_space_constraint(value, pltpu.HBM)
            for value in (out_gate, in_gate, values_in, filter_taps, out_cotangent)
        )
    )


def outcome_kernel(
    scale,
    plane_ref,
    returned_ref,
    out_gate_ref,
    in_gate_ref,
    values_ref,
    cot_ref,
    mixed_ref,
    grad_out_gate_ref,
    grad_in_gate_ref,
    grad_values_ref,
    grad_filter_ref,
    ordered_ref,
    results_ref,
    sums_ref,
    left,
):
    owners = holders(plane_ref[0])
    for first in range(RING):
        for second in range(RING):
            ordered_ref[first * RING + second] = returned_ref[
                owners[first][second % 2], second, :, : 2 * ROWS
            ]
    row = lax.broadcasted_iota(jnp.int32, (2 * ROWS, 2 * ROWS), 0)
    column = lax.broadcasted_iota(jnp.int32, (2 * ROWS, 2 * ROWS), 1)
    parted = (column == row % 2 * ROWS + row // 2).astype(jnp.float32).astype(jnp.bfloat16)
    copies = []
    results = (
        (mixed_ref, out_gate_ref),
        (grad_out_gate_ref, cot_ref),
        (grad_in_gate_ref, values_ref),
        (grad_values_ref, in_gate_ref),
    )
    for which in range(2):
        lanes = slice(which * ROWS, (which + 1) * ROWS)
        turned = jnp.concatenate(
            [
                ordered_ref[:, part * GROUPS_HERE : (part + 1) * GROUPS_HERE, lanes].reshape(
                    ROWS, ROWS
                )
                for part in range(2)
            ],
            axis=1,
        )
        signal = lax.dot_general(
            parted, turned, (((1,), (1,)), ((), ())), preferred_element_type=jnp.float32
        )
        for slot in (2 * which, 2 * which + 1):
            result_ref, gate_ref = results[slot]
            gate = gate_ref[...].reshape(2 * ROWS, ROWS).astype(jnp.float32)
            results_ref[slot] = (signal * gate).astype(jnp.bfloat16).reshape(ROWS, 2, ROWS)
            copies.append(
                pltpu.make_async_copy(results_ref.at[slot], result_ref, left.at[slot])
            )
            copies[-1].start()
    for second in range(RING):
        total = returned_ref[0, second, :, 2 * ROWS :].astype(jnp.float32)
        for first in range(1, RING):
            total += returned_ref[first, second, :, 2 * ROWS :].astype(jnp.float32)
        total = total * scale
        rows = slice(second * GROUPS_HERE, (second + 1) * GROUPS_HERE)
        sums_ref[rows, :HALF] = total[:GROUPS_HERE]
        sums_ref[rows, HALF:] = total[GROUPS_HERE:]
    copies.append(pltpu.make_async_copy(sums_ref, grad_filter_ref, left.at[len(results)]))
    copies[-1].start()
    for copy in copies:
        copy.wait()


def outcomes(scale, plane, returned, out_gate, in_gate, values_in, out_cotangent):
    whole = pl.BlockSpec(memory_space=pltpu.VMEM)
    signal = jax.ShapeDtypeStruct((ROWS, 2, ROWS), jnp.bfloat16)
    return pl.pallas_call(
        functools.partial(outcome_kernel, scale),
        out_shape=(signal,) * 4
        + (jax.ShapeDtypeStruct((RING * GROUPS_HERE, ROWS), jnp.float32),),
        in_specs=[pl.BlockSpec(memory_space=pltpu.SMEM)] + [whole] * 5,
        out_specs=(pl.BlockSpec(memory_space=pl.ANY),) * 5,
        scratch_shapes=[
            pltpu.VMEM((BLOCKS, SIGNALS, 2 * ROWS), jnp.bfloat16),
            pltpu.VMEM((4, ROWS, 2, ROWS), jnp.bfloat16),
            pltpu.VMEM((RING * GROUPS_HERE, ROWS), jnp.float32),
            pltpu.SemaphoreType.DMA((5,)),
        ],
        compiler_params=pltpu.CompilerParams(vmem_limit_bytes=16 * 1024 * 1024),
        cost_estimate=pl.CostEstimate(
            flops=400_000_000, bytes_accessed=3_000_000, transcendentals=0
        ),
        name="outcomes",
    )(plane, returned, out_gate, in_gate, values_in, out_cotangent)


def exchange(value, axis):
    return lax.all_to_all(value, axis, split_axis=0, concat_axis=0, tiled=True)


def local(out_gate, in_gate, values_in, filter_taps, skip_gain, out_cotangent):
    row_count, member_count, group_count = out_gate.shape
    chan_count = lax.axis_size("chan")
    plane = lax.axis_index("chan")
    row, column = jnp.divmod(lax.axis_index("seq"), RING)
    owned = (plane + shift(row, column)) % RING * RING + column
    plane = jnp.stack([plane, owned]).astype(jnp.int32)

    def send_lag(lag):
        pairs = [
            (
                (first * RING + second) * RING + level,
                (first * RING + second) * RING + (level + shift(first, second)) % RING,
            )
            for first in range(RING)
            for second in range(RING)
            for level in range(RING)
        ]
        return lax.ppermute(lag, ("seq", "chan"), pairs)

    outgoing = gated_chunks(plane, out_gate, in_gate, values_in, filter_taps, out_cotangent)
    received = exchange(outgoing.reshape(BLOCKS, SIGNALS, 5 * HALF), "seq")
    returned = exchange(spectral(received, plane, skip_gain, send_lag), "seq")
    norm_factor = 1.0 / math.sqrt(BLOCKS * row_count * member_count * chan_count)
    *gradients, filter_sum = outcomes(
        norm_factor,
        plane,
        returned.reshape(RING, RING, SIGNALS, 5 * HALF),
        out_gate,
        in_gate,
        values_in,
        out_cotangent,
    )
    return (*gradients, filter_sum.T)


def solution(mesh):
    in_specs = (
        P("seq", "chan", None),
        P("seq", "chan", None),
        P("seq", "chan", None),
        P("seq", None),
        P("chan", None),
        P("seq", "chan", None),
    )
    out_specs = (
        P("seq", "chan", None),
        P("seq", "chan", None),
        P("seq", "chan", None),
        P("seq", "chan", None),
        P("seq", "chan"),
    )
    return jax.shard_map(local, mesh=mesh, in_specs=in_specs, out_specs=out_specs, check_vma=False)
```

time: 85.2 us -> 82.2 us (0.965)
  blocking collectives: 56.9 us -> 68.2 us
  starting transfers between devices: 10.3 us -> 0.67 us
  local copies, waits for them, and re-layouts: 7.46 us -> 0.06 us
  Pallas kernels: 6.28 us -> 11.1 us
  waiting for transfers between devices: 2.47 us -> 0.01 us
    all_to_all x2, blocking collectives: 56.9 us -> 68.2 us  [exchange(): return lax.all_to_all(value, axis, split_axis=0, concat_axis=0, tiled=True)]
    all_to_all x1 -> x0, starting transfers between devices: 10.3 us -> none  [exchange(): return lax.all_to_all(value, axis, split_axis=0, concat_axis=0, tiled=True)]
    unnamed x27 -> x22, local copies, waits for them, and re-layouts: 5.49 us -> 0.06 us
    pallas_call x2 -> x4, Pallas kernels: 6.28 us -> 11.1 us  [the longest x1 3.4 us: spectral(): pl.pallas_call(signal_kernel, out_shape=jax.ShapeDtypeStruct((BLOCKS, SIG...]
    all_to_all x1 -> x0, waiting for transfers between devices: 2.47 us -> none  [exchange(): return lax.all_to_all(value, axis, split_axis=0, concat_axis=0, tiled=True)]
    convert_element_type x6 -> x0, local copies, waits for them, and re-layouts: 1.27 us -> none  [unchunks(): return received.reshape(BLOCKS, member_count, GROUPS_HERE, ROWS).transpos...]
  transfers between devices with their start and end apart: 1 -> 1, of which waited for: 1 -> 0; matrix products, arithmetic and copies ran while one was open for 7% -> 0% of each run, Pallas kernels for 0% -> 4%
where the time goes in v5:
time: 82.2 us; the launch traced here: 81 us
  blocking collectives  68.2 us (83%)
  Pallas kernels  11.1 us (14%)
  between operations  0.85 us (1%)
    all_to_all x2, blocking collectives, exchange(): return lax.all_to_all(value, axis, split_axis=0, concat_axis=0, tiled=True)  68.2 us
    pallas_call x1, Pallas kernels, spectral(): pl.pallas_call(signal_kernel, out_shape=jax.ShapeDtypeStruct((BLOCKS, SIG...  3.4 us
    pallas_call x1, Pallas kernels, gated_chunks(): pl.pallas_call(gate_kernel, out_shape=jax.ShapeDtypeStruct((RING, RING, S...  2.82 us
    pallas_call x1, Pallas kernels, outcomes(): pl.pallas_call(functools.partial(outcome_kernel, scale), out_shape=(signa...  2.52 us
    pallas_call x1, Pallas kernels, spectral(): pl.pallas_call(lag_kernel, out_shape=(jax.ShapeDtypeStruct((BLOCKS, SIGNA...  2.4 us
  transfers between devices with their start and end apart: 1, of which 0 were waited for; matrix products, arithmetic and copies ran while one was open for 0% of the time, Pallas kernels for 4%

profile of v5, /device:TPU:6, one launch (start us, length us, event | category | flops | bytes accessed | tf_op | source)
XLA Modules:
  0.0 81.0 jit_solution(18358841081942037240)
XLA Ops:
  0.7 0.1 pad_add_fusion.plane_ref
  0.8 0.0 copy-start.5
  0.8 0.0 copy-start.6
  0.8 0.0 copy-start.7
  0.8 0.0 copy-start.8
  0.8 0.0 copy-start.9
  0.8 0.0 copy-start.10
  0.8 2.8 %gates.1 = bf16[8,8,8,640]{3,2,1,0:T(8,128)(2,1)S(1)} custom-call(s32[2]{0:T(128)S(1)} %pad_add_fusion.plane_ref, bf16[256,2,256]{2,1,0:T(2,128)(2,1)} %out_gate_ref.3, bf16[256,2,256]{2,1,0:T(2,128)(2,1)} %in_gate_ref.3, bf16[256,2,256]{2,1,0:T(2,128)(2,1)} %values_ref.3, bf16[256,256]{1,0:T(8,128)(2,1)} %taps_ref.1, bf16[256,2,256]{2,1,0:T(2,128)(2,1)} %cot_ref.3), custom_call_target="tpu_custom_call" | custom-call | flops 400000000 | bytes 2000000 | tf_op jit(solution)/shard_map/gates/pallas_call | solution.py:428
  3.6 30.8 %all_to_all.10.recv_ref = bf16[64,8,640]{2,1,0:T(8,128)(2,1)S(1)} all-to-all(bf16[64,8,640]{2,1,0:T(8,128)(2,1)S(1)} %bitcast.6), channel_id=1, replica_groups=mesh['seq'=64,'chan'=8] {'seq'}, dimensions={0} | all-to-all | bytes 1310720 | tf_op jit(solution)/shard_map/all_to_all | solution.py:547
  34.4 0.0 copy-done.5
  34.4 0.0 copy-done.6
  34.4 0.0 copy-done.7
  34.4 0.0 copy-done.8
  34.4 0.0 copy-done.9
  34.5 0.0 copy-done.10
  34.5 0.0 copy-start.4
  34.5 2.4 %lags.1 = (bf16[64,8,128]{2,1,0:T(8,128)(2,1)S(1)}, f32[2,1024,256]{2,1,0:T(8,128)S(1)}, f32[4,512,128]{2,1,0:T(8,128)S(1)}) custom-call(bf16[64,8,640]{2,1,0:T(8,128)(2,1)S(1)} %all_to_all.10.recv_ref, bf16[128,128]{1,0:T(8,128)(2,1)S(1)} %copy-done.10, bf16[128,256]{1,0:T(8,128)(2,1)S(1)} %copy-done.9, f32[64,256]{1,0:T(8,128)S(1)} %copy-done.8, ...), custom_call_target="tpu_custom_call" | custom-call | flops 3000000000 | bytes 5000000 | tf_op jit(solution)/shard_map/lags/pallas_call | solution.py:302
  36.9 0.7 collective-permute-start
  37.6 0.0 copy-done.4
  37.6 3.4 %signals.1 = bf16[64,8,512]{2,1,0:T(8,128)(2,1)S(1)} custom-call(s32[2]{0:T(128)S(1)} %pad_add_fusion.plane_ref, f32[2,256]{1,0:T(2,128)S(1)} %copy-done.4, bf16[64,8,640]{2,1,0:T(8,128)(2,1)S(1)} %all_to_all.10.recv_ref, f32[2,1024,256]{2,1,0:T(8,128)S(1)} %get-tuple-element.13.spec_ref, f32[4,512,128]{2,1,0:T(8,128)S(1)} %get-tuple-element.14.wide_ref, ...), custom_call_target="tpu_custom_call" | custom-call | flops 3000000000 | bytes 5000000 | tf_op jit(solution)/shard_map/signals/pallas_call | solution.py:326
  41.0 0.0 copy-start
  41.0 0.0 copy-start.1
  41.0 0.0 copy-start.2
  41.0 0.0 copy-start.3
  41.0 0.0 collective-permute-done
  41.0 0.1 pad_maximum_fusion
  41.1 37.4 %all_to_all.11 = bf16[64,8,640]{2,1,0:T(8,128)(2,1)S(1)} all-to-all(bf16[64,8,640]{2,1,0:T(8,128)(2,1)S(1)} %pad_maximum_fusion), channel_id=1, replica_groups=mesh['seq'=64,'chan'=8] {'seq'}, dimensions={0} | all-to-all | bytes 1310720 | tf_op jit(solution)/shard_map/all_to_all | solution.py:547
  78.5 0.0 copy-done
  78.5 0.0 copy-done.1
  78.5 0.0 copy-done.2
  78.5 0.0 copy-done.3
  78.5 2.5 %outcomes.1 = (bf16[256,2,256]{2,1,0:T(2,128)(2,1)}, bf16[256,2,256]{2,1,0:T(2,128)(2,1)}, bf16[256,2,256]{2,1,0:T(2,128)(2,1)}, bf16[256,2,256]{2,1,0:T(2,128)(2,1)}, f32[32,256]{1,0:T(8,128)}) custom-call(s32[2]{0:T(128)S(1)} %pad_add_fusion.plane_ref, bf16[8,8,8,640]{3,2,1,0:T(8,128)(2,1)S(1)} %bitcast.5, bf16[256,2,256]{2,1,0:T(2,128)(2,1)S(1)} %copy-done, ...), custom_call_target="tpu_custom_call" | custom-call | flops 400000000 | bytes 3000000 | tf_op jit(solution)/shard_map/outcomes/pallas_call | solution.py:526
Async XLA Ops:
  0.8 33.7 %copy-start.5 = (bf16[2,768,256]{2,1,0:T(8,128)(2,1)S(1)}, bf16[2,768,256]{2,1,0:T(8,128)(2,1)}, u32[]{:S(2)}) copy-start(bf16[2,768,256]{2,1,0:T(8,128)(2,1)} %constant.77.clone.back_ref) | copy-start | bytes 2359300
  0.8 33.7 %copy-start.6 = (bf16[2,768,256]{2,1,0:T(8,128)(2,1)S(1)}, bf16[2,768,256]{2,1,0:T(8,128)(2,1)}, u32[]{:S(2)}) copy-start(bf16[2,768,256]{2,1,0:T(8,128)(2,1)} %constant.76.clone.forth_ref) | copy-start | bytes 2359300
  0.8 33.7 %copy-start.7 = (f32[64,256]{1,0:T(8,128)S(1)}, f32[64,256]{1,0:T(8,128)}, u32[]{:S(2)}) copy-start(f32[64,256]{1,0:T(8,128)} %constant.75.clone.sin_ref) | copy-start | bytes 196612
  0.8 33.7 %copy-start.8 = (f32[64,256]{1,0:T(8,128)S(1)}, f32[64,256]{1,0:T(8,128)}, u32[]{:S(2)}) copy-start(f32[64,256]{1,0:T(8,128)} %constant.74.clone.cos_ref) | copy-start | bytes 196612
  0.8 33.7 %copy-start.9 = (bf16[128,256]{1,0:T(8,128)(2,1)S(1)}, bf16[128,256]{1,0:T(8,128)(2,1)}, u32[]{:S(2)}) copy-start(bf16[128,256]{1,0:T(8,128)(2,1)} %constant.73.clone.leave_ref) | copy-start | bytes 196612
  0.8 33.7 %copy-start.10 = (bf16[128,128]{1,0:T(8,128)(2,1)S(1)}, bf16[128,128]{1,0:T(8,128)(2,1)}, u32[]{:S(2)}) copy-start(bf16[128,128]{1,0:T(8,128)(2,1)} %constant.72.clone.enter_ref) | copy-start | bytes 98308
  34.5 3.1 %copy-start.4 = (f32[2,256]{1,0:T(2,128)S(1)}, f32[2,256]{1,0:T(2,128)}, u32[]{:S(2)}) copy-start(f32[2,256]{1,0:T(2,128)} %skip_ref.1) | copy-start | bytes 6148
  36.9 4.1 %collective-permute-start = (bf16[64,8,128]{2,1,0:T(8,128)(2,1)S(1)}, bf16[64,8,128]{2,1,0:T(8,128)(2,1)S(1)}, u32[]{:S(2)}, u32[]{:S(2)}) collective-permute-start(bf16[64,8,128]{2,1,0:T(8,128)(2,1)S(1)} %get-tuple-element.15), channel_id=1, source_target_pairs={{0,0},{1,1},{2,2},{3,3},{4,4},{5,5},{6,6},{7,7},{8,12},{9,13},{10,... | collective-permute-start | bytes 393224 | tf_op jit(solution)/shard_map/ppermute | solution.py:568
  41.0 37.5 %copy-start = (bf16[256,2,256]{2,1,0:T(2,128)(2,1)S(1)}, bf16[256,2,256]{2,1,0:T(2,128)(2,1)}, u32[]{:S(2)}) copy-start(bf16[256,2,256]{2,1,0:T(2,128)(2,1)} %out_gate_ref.3) | copy-start | bytes 786436
  41.0 37.5 %copy-start.1 = (bf16[256,2,256]{2,1,0:T(2,128)(2,1)S(1)}, bf16[256,2,256]{2,1,0:T(2,128)(2,1)}, u32[]{:S(2)}) copy-start(bf16[256,2,256]{2,1,0:T(2,128)(2,1)} %in_gate_ref.3) | copy-start | bytes 786436
  41.0 37.5 %copy-start.2 = (bf16[256,2,256]{2,1,0:T(2,128)(2,1)S(1)}, bf16[256,2,256]{2,1,0:T(2,128)(2,1)}, u32[]{:S(2)}) copy-start(bf16[256,2,256]{2,1,0:T(2,128)(2,1)} %values_ref.3) | copy-start | bytes 786436
  41.0 37.5 %copy-start.3 = (bf16[256,2,256]{2,1,0:T(2,128)(2,1)S(1)}, bf16[256,2,256]{2,1,0:T(2,128)(2,1)}, u32[]{:S(2)}) copy-start(bf16[256,2,256]{2,1,0:T(2,128)(2,1)} %cot_ref.3) | copy-start | bytes 786436

commit v6 on v5

--- a/solution.py
+++ b/solution.py
@@ -219,7 +219,6 @@
 
 
 def signal_kernel(
-    plane_ref,
     skip_ref,
     recv_ref,
     spec_ref,
@@ -242,7 +241,8 @@
 ):
     stages = Stages(cos_ref, sin_ref, enter_ref, leave_ref, forth_ref, back_ref)
     taps_pair, pair = (high_taps_ref, low_taps_ref), (high_ref, low_ref)
-    first_group = plane_ref[1] * GROUPS_HERE
+    skip = jnp.concatenate([skip_ref[...], jnp.zeros((6, ROWS), jnp.float32)], axis=0)
+    gains = pltpu.roll(skip, lax.rem(ROWS - position()[1] * GROUPS_HERE, ROWS), 1)
     spread(wide_taps_ref, 0, recv_ref[:, :, 4 * HALF :])
     for group in range(GROUPS_HERE):
         taken = jnp.concatenate(
@@ -278,7 +278,8 @@
     def leave(group):
         for item in range(PAIRS):
             result = stages.leave(turn_ref, spot(group, item).start)
-            gain = skip_ref[item % MEMBERS, first_group + group]
+            member = item % MEMBERS
+            gain = gains[member : member + 1, group : group + 1]
             for part, (lane, row) in enumerate(places(group, item)):
                 direct = wide_ref[lane, every(row), :] * gain
                 wide_out_ref[lane, every(row), :] = (
@@ -293,11 +294,10 @@
         send_ref[:, :, lane * HALF : (lane + 1) * HALF] = gather(wide_out_ref, lane)
 
 
-def spectral(received, plane, skip_gain, send_lag):
+def spectral(received, skip_gain, send_lag):
     constants = [jnp.asarray(table) for table in tables()]
     signal_rows, group_rows = GROUPS_HERE * GROUP_ROWS, GROUPS_HERE * KEPT
     whole = pl.BlockSpec(memory_space=pltpu.VMEM)
-    scalar = pl.BlockSpec(memory_space=pltpu.SMEM)
     params = pltpu.CompilerParams(vmem_limit_bytes=24 * 1024 * 1024)
     lag, spec, wide = pl.pallas_call(
         lag_kernel,
@@ -326,7 +326,7 @@
     signals = pl.pallas_call(
         signal_kernel,
         out_shape=jax.ShapeDtypeStruct((BLOCKS, SIGNALS, 4 * HALF), jnp.bfloat16),
-        in_specs=[scalar] * 2 + [whole] * 9,
+        in_specs=[whole] * 10,
         out_specs=whole,
         scratch_shapes=[
             pltpu.VMEM((1, BLOCKS * SIGNALS, HALF), jnp.float32),
@@ -343,7 +343,7 @@
             flops=3_000_000_000, bytes_accessed=5_000_000, transcendentals=0
         ),
         name="signals",
-    )(plane, skip_gain, received, spec, wide, *constants)
+    )(skip_gain, received, spec, wide, *constants)
     return jnp.concatenate([signals, moved], axis=2)
 
 
@@ -352,6 +352,13 @@
 
 def shift(row, column):
     return (row + RING // 2 * (column % 2)) % RING
+
+
+def position():
+    seat, plane = lax.axis_index("seq"), lax.axis_index("chan")
+    row, column = lax.div(seat, RING), lax.rem(seat, RING)
+    held = lax.rem(plane + row + RING // 2 * lax.rem(column, 2), RING) * RING + column
+    return plane, held
 
 
 def holders(plane):
@@ -362,7 +369,6 @@
 
 
 def gate_kernel(
-    plane_ref,
     out_gate_ref,
     in_gate_ref,
     values_ref,
@@ -393,7 +399,7 @@
             value, order, (((0,), (0,)), ((), ())), preferred_element_type=jnp.float32
         ).astype(jnp.bfloat16)
 
-    owners = holders(plane_ref[0])
+    owners = holders(position()[0])
 
     def send(part, lanes, value):
         rows = slice(part * GROUPS_HERE, (part + 1) * GROUPS_HERE)
@@ -424,12 +430,11 @@
         send(half, slice(2 * ROWS, None), taps[:, half * HALF : (half + 1) * HALF])
 
 
-def gated_chunks(plane, out_gate, in_gate, values_in, filter_taps, out_cotangent):
+def gated_chunks(out_gate, in_gate, values_in, filter_taps, out_cotangent):
     return pl.pallas_call(
         gate_kernel,
         out_shape=jax.ShapeDtypeStruct((RING, RING, SIGNALS, 5 * HALF), jnp.bfloat16),
-        in_specs=[pl.BlockSpec(memory_space=pltpu.SMEM)]
-        + [pl.BlockSpec(memory_space=pltpu.HBM)] * 5,
+        in_specs=[pl.BlockSpec(memory_space=pltpu.HBM)] * 5,
         out_specs=pl.BlockSpec(memory_space=pltpu.VMEM),
         scratch_shapes=[
             pltpu.VMEM((4, ROWS, 2, ROWS), jnp.bfloat16),
@@ -442,7 +447,6 @@
         ),
         name="gates",
     )(
-        plane,
         *(
             pltpu.with_memory_space_constraint(value, pltpu.HBM)
             for value in (out_gate, in_gate, values_in, filter_taps, out_cotangent)
@@ -452,7 +456,6 @@
 
 def outcome_kernel(
     scale,
-    plane_ref,
     returned_ref,
     out_gate_ref,
     in_gate_ref,
@@ -468,7 +471,7 @@
     sums_ref,
     left,
 ):
-    owners = holders(plane_ref[0])
+    owners = holders(position()[0])
     for first in range(RING):
         for second in range(RING):
             ordered_ref[first * RING + second] = returned_ref[
@@ -520,14 +523,14 @@
         copy.wait()
 
 
-def outcomes(scale, plane, returned, out_gate, in_gate, values_in, out_cotangent):
+def outcomes(scale, returned, out_gate, in_gate, values_in, out_cotangent):
     whole = pl.BlockSpec(memory_space=pltpu.VMEM)
     signal = jax.ShapeDtypeStruct((ROWS, 2, ROWS), jnp.bfloat16)
     return pl.pallas_call(
         functools.partial(outcome_kernel, scale),
         out_shape=(signal,) * 4
         + (jax.ShapeDtypeStruct((RING * GROUPS_HERE, ROWS), jnp.float32),),
-        in_specs=[pl.BlockSpec(memory_space=pltpu.SMEM)] + [whole] * 5,
+        in_specs=[whole] * 5,
         out_specs=(pl.BlockSpec(memory_space=pl.ANY),) * 5,
         scratch_shapes=[
             pltpu.VMEM((BLOCKS, SIGNALS, 2 * ROWS), jnp.bfloat16),
@@ -540,7 +543,7 @@
             flops=400_000_000, bytes_accessed=3_000_000, transcendentals=0
         ),
         name="outcomes",
-    )(plane, returned, out_gate, in_gate, values_in, out_cotangent)
+    )(returned, out_gate, in_gate, values_in, out_cotangent)
 
 
 def exchange(value, axis):
@@ -550,10 +553,6 @@
 def local(out_gate, in_gate, values_in, filter_taps, skip_gain, out_cotangent):
     row_count, member_count, group_count = out_gate.shape
     chan_count = lax.axis_size("chan")
-    plane = lax.axis_index("chan")
-    row, column = jnp.divmod(lax.axis_index("seq"), RING)
-    owned = (plane + shift(row, column)) % RING * RING + column
-    plane = jnp.stack([plane, owned]).astype(jnp.int32)
 
     def send_lag(lag):
         pairs = [
@@ -567,13 +566,12 @@
         ]
         return lax.ppermute(lag, ("seq", "chan"), pairs)
 
-    outgoing = gated_chunks(plane, out_gate, in_gate, values_in, filter_taps, out_cotangent)
+    outgoing = gated_chunks(out_gate, in_gate, values_in, filter_taps, out_cotangent)
     received = exchange(outgoing.reshape(BLOCKS, SIGNALS, 5 * HALF), "seq")
-    returned = exchange(spectral(received, plane, skip_gain, send_lag), "seq")
+    returned = exchange(spectral(received, skip_gain, send_lag), "seq")
     norm_factor = 1.0 / math.sqrt(BLOCKS * row_count * member_count * chan_count)
     *gradients, filter_sum = outcomes(
         norm_factor,
-        plane,
         returned.reshape(RING, RING, SIGNALS, 5 * HALF),
         out_gate,
         in_gate,

time: 82.2 us -> 81.1 us (0.987)
  Pallas kernels: 11.1 us -> 9.51 us
where the time goes in v6:
time: 81.1 us; the launch traced here: 79.9 us
  blocking collectives  68.8 us (85%)
  Pallas kernels  9.51 us (12%)
    all_to_all x2, blocking collectives, exchange(): return lax.all_to_all(value, axis, split_axis=0, concat_axis=0, tiled=True)  68.8 us
    pallas_call x1, Pallas kernels, spectral(): pl.pallas_call(signal_kernel, out_shape=jax.ShapeDtypeStruct((BLOCKS, SIG...  2.82 us
    pallas_call x1, Pallas kernels, gated_chunks(): pl.pallas_call(gate_kernel, out_shape=jax.ShapeDtypeStruct((RING, RING, S...  2.4 us
    pallas_call x1, Pallas kernels, spectral(): pl.pallas_call(lag_kernel, out_shape=(jax.ShapeDtypeStruct((BLOCKS, SIGNA...  2.33 us
    pallas_call x1, Pallas kernels, outcomes(): pl.pallas_call(functools.partial(outcome_kernel, scale), out_shape=(signa...  1.96 us
  transfers between devices with their start and end apart: 1, of which 0 were waited for; matrix products, arithmetic and copies ran while one was open for 0% of the time, Pallas kernels for 4%

profile of v6, /device:TPU:6, one launch (start us, length us, event | category | flops | bytes accessed | tf_op | source)
XLA Modules:
  0.0 79.9 jit_solution(386062606431318376)
XLA Ops:
  0.6 0.0 copy-start.5
  0.6 0.0 copy-start.6
  0.7 0.0 copy-start.7
  0.7 0.0 copy-start.8
  0.7 0.0 copy-start.9
  0.7 0.0 copy-start.10
  0.7 2.4 %gates.1 = bf16[8,8,8,640]{3,2,1,0:T(8,128)(2,1)S(1)} custom-call(bf16[256,2,256]{2,1,0:T(2,128)(2,1)} %out_gate_ref.3, bf16[256,2,256]{2,1,0:T(2,128)(2,1)} %in_gate_ref.3, bf16[256,2,256]{2,1,0:T(2,128)(2,1)} %values_ref.3, bf16[256,256]{1,0:T(8,128)(2,1)} %taps_ref.1, bf16[256,2,256]{2,1,0:T(2,128)(2,1)} %cot_ref.3), custom_call_target="tpu_custom_call" | custom-call | flops 400000000 | bytes 2000000 | tf_op jit(solution)/shard_map/gates/pallas_call | solution.py:434
  3.1 30.8 %all_to_all.10.recv_ref = bf16[64,8,640]{2,1,0:T(8,128)(2,1)S(1)} all-to-all(bf16[64,8,640]{2,1,0:T(8,128)(2,1)S(1)} %bitcast.3), channel_id=1, replica_groups=mesh['seq'=64,'chan'=8] {'seq'}, dimensions={0} | all-to-all | bytes 1310720 | tf_op jit(solution)/shard_map/all_to_all | solution.py:550
  33.9 0.0 copy-done.5
  33.9 0.0 copy-done.6
  33.9 0.0 copy-done.7
  33.9 0.0 copy-done.8
  33.9 0.0 copy-done.9
  33.9 0.0 copy-done.10
  33.9 0.0 copy-start.4
  34.0 2.3 %lags.1 = (bf16[64,8,128]{2,1,0:T(8,128)(2,1)S(1)}, f32[2,1024,256]{2,1,0:T(8,128)S(1)}, f32[4,512,128]{2,1,0:T(8,128)S(1)}) custom-call(bf16[64,8,640]{2,1,0:T(8,128)(2,1)S(1)} %all_to_all.10.recv_ref, bf16[128,128]{1,0:T(8,128)(2,1)S(1)} %copy-done.10, bf16[128,256]{1,0:T(8,128)(2,1)S(1)} %copy-done.9, f32[64,256]{1,0:T(8,128)S(1)} %copy-done.8, ...), custom_call_target="tpu_custom_call" | custom-call | flops 3000000000 | bytes 5000000 | tf_op jit(solution)/shard_map/lags/pallas_call | solution.py:302
  36.3 0.7 collective-permute-start
  37.0 0.0 copy-done.4
  37.0 2.8 %signals.1 = bf16[64,8,512]{2,1,0:T(8,128)(2,1)S(1)} custom-call(f32[2,256]{1,0:T(2,128)S(1)} %copy-done.4, bf16[64,8,640]{2,1,0:T(8,128)(2,1)S(1)} %all_to_all.10.recv_ref, f32[2,1024,256]{2,1,0:T(8,128)S(1)} %get-tuple-element.13.spec_ref, f32[4,512,128]{2,1,0:T(8,128)S(1)} %get-tuple-element.14.wide_ref, bf16[128,128]{1,0:T(8,128)(2,1)S(1)} %copy-done.10, ...), custom_call_target="tpu_custom_call" | custom-call | flops 3000000000 | bytes 5000000 | tf_op jit(solution)/shard_map/signals/pallas_call | solution.py:326
  39.8 0.0 copy-start
  39.8 0.0 copy-start.1
  39.8 0.0 copy-start.2
  39.8 0.0 copy-start.3
  39.9 0.0 collective-permute-done
  39.9 0.1 pad_maximum_fusion
  39.9 38.0 %all_to_all.11 = bf16[64,8,640]{2,1,0:T(8,128)(2,1)S(1)} all-to-all(bf16[64,8,640]{2,1,0:T(8,128)(2,1)S(1)} %pad_maximum_fusion), channel_id=1, replica_groups=mesh['seq'=64,'chan'=8] {'seq'}, dimensions={0} | all-to-all | bytes 1310720 | tf_op jit(solution)/shard_map/all_to_all | solution.py:550
  77.9 0.0 copy-done
  77.9 0.0 copy-done.1
  77.9 0.0 copy-done.2
  77.9 0.0 copy-done.3
  77.9 2.0 %outcomes.1 = (bf16[256,2,256]{2,1,0:T(2,128)(2,1)}, bf16[256,2,256]{2,1,0:T(2,128)(2,1)}, bf16[256,2,256]{2,1,0:T(2,128)(2,1)}, bf16[256,2,256]{2,1,0:T(2,128)(2,1)}, f32[32,256]{1,0:T(8,128)}) custom-call(bf16[8,8,8,640]{3,2,1,0:T(8,128)(2,1)S(1)} %bitcast.4, bf16[256,2,256]{2,1,0:T(2,128)(2,1)S(1)} %copy-done, bf16[256,2,256]{2,1,0:T(2,128)(2,1)S(1)} %copy-done.1, ...), custom_call_target="tpu_custom_call" | custom-call | flops 400000000 | bytes 3000000 | tf_op jit(solution)/shard_map/outcomes/pallas_call | solution.py:529
Async XLA Ops:
  0.6 33.3 %copy-start.5 = (bf16[2,768,256]{2,1,0:T(8,128)(2,1)S(1)}, bf16[2,768,256]{2,1,0:T(8,128)(2,1)}, u32[]{:S(2)}) copy-start(bf16[2,768,256]{2,1,0:T(8,128)(2,1)} %constant.17.clone.back_ref) | copy-start | bytes 2359300
  0.6 33.3 %copy-start.6 = (bf16[2,768,256]{2,1,0:T(8,128)(2,1)S(1)}, bf16[2,768,256]{2,1,0:T(8,128)(2,1)}, u32[]{:S(2)}) copy-start(bf16[2,768,256]{2,1,0:T(8,128)(2,1)} %constant.16.clone.forth_ref) | copy-start | bytes 2359300
  0.7 33.3 %copy-start.7 = (f32[64,256]{1,0:T(8,128)S(1)}, f32[64,256]{1,0:T(8,128)}, u32[]{:S(2)}) copy-start(f32[64,256]{1,0:T(8,128)} %constant.15.clone.sin_ref) | copy-start | bytes 196612
  0.7 33.2 %copy-start.8 = (f32[64,256]{1,0:T(8,128)S(1)}, f32[64,256]{1,0:T(8,128)}, u32[]{:S(2)}) copy-start(f32[64,256]{1,0:T(8,128)} %constant.14.clone.cos_ref) | copy-start | bytes 196612
  0.7 33.2 %copy-start.9 = (bf16[128,256]{1,0:T(8,128)(2,1)S(1)}, bf16[128,256]{1,0:T(8,128)(2,1)}, u32[]{:S(2)}) copy-start(bf16[128,256]{1,0:T(8,128)(2,1)} %constant.13.clone.leave_ref) | copy-start | bytes 196612
  0.7 33.2 %copy-start.10 = (bf16[128,128]{1,0:T(8,128)(2,1)S(1)}, bf16[128,128]{1,0:T(8,128)(2,1)}, u32[]{:S(2)}) copy-start(bf16[128,128]{1,0:T(8,128)(2,1)} %constant.12.clone.enter_ref) | copy-start | bytes 98308
  33.9 3.0 %copy-start.4 = (f32[2,256]{1,0:T(2,128)S(1)}, f32[2,256]{1,0:T(2,128)}, u32[]{:S(2)}) copy-start(f32[2,256]{1,0:T(2,128)} %skip_ref.1) | copy-start | bytes 6148
  36.3 3.6 %collective-permute-start = (bf16[64,8,128]{2,1,0:T(8,128)(2,1)S(1)}, bf16[64,8,128]{2,1,0:T(8,128)(2,1)S(1)}, u32[]{:S(2)}, u32[]{:S(2)}) collective-permute-start(bf16[64,8,128]{2,1,0:T(8,128)(2,1)S(1)} %get-tuple-element.15), channel_id=1, source_target_pairs={{0,0},{1,1},{2,2},{3,3},{4,4},{5,5},{6,6},{7,7},{8,12},{9,13},{10,... | collective-permute-start | bytes 393224 | tf_op jit(solution)/shard_map/ppermute | solution.py:567
  39.8 38.1 %copy-start = (bf16[256,2,256]{2,1,0:T(2,128)(2,1)S(1)}, bf16[256,2,256]{2,1,0:T(2,128)(2,1)}, u32[]{:S(2)}) copy-start(bf16[256,2,256]{2,1,0:T(2,128)(2,1)} %out_gate_ref.3) | copy-start | bytes 786436
  39.8 38.1 %copy-start.1 = (bf16[256,2,256]{2,1,0:T(2,128)(2,1)S(1)}, bf16[256,2,256]{2,1,0:T(2,128)(2,1)}, u32[]{:S(2)}) copy-start(bf16[256,2,256]{2,1,0:T(2,128)(2,1)} %in_gate_ref.3) | copy-start | bytes 786436
  39.8 38.1 %copy-start.2 = (bf16[256,2,256]{2,1,0:T(2,128)(2,1)S(1)}, bf16[256,2,256]{2,1,0:T(2,128)(2,1)}, u32[]{:S(2)}) copy-start(bf16[256,2,256]{2,1,0:T(2,128)(2,1)} %values_ref.3) | copy-start | bytes 786436
  39.8 38.1 %copy-start.3 = (bf16[256,2,256]{2,1,0:T(2,128)(2,1)S(1)}, bf16[256,2,256]{2,1,0:T(2,128)(2,1)}, u32[]{:S(2)}) copy-start(bf16[256,2,256]{2,1,0:T(2,128)(2,1)} %cot_ref.3) | copy-start | bytes 786436

commit v7 on v6

--- a/solution.py
+++ b/solution.py
@@ -187,13 +187,17 @@
     pair, joined = (high_ref, low_ref), (high_lag_ref, low_lag_ref)
     for lane in range(4):
         spread(wide_ref, lane, recv_ref[:, :, lane * HALF : (lane + 1) * HALF])
-    for group in range(GROUPS_HERE):
+    def enter(group):
         for item in range(PAIRS):
             taken = jnp.concatenate(
                 [wide_ref[lane, every(row), :] for lane, row in places(group, item)], axis=1
             ).astype(jnp.bfloat16)
             stages.enter(taken, pair, spot(group, item).start)
+
+    enter(0)
     for group in range(GROUPS_HERE):
+        if group + 1 < GROUPS_HERE:
+            enter(group + 1)
         stages.forth(pair, spec_ref, slice(group * GROUP_ROWS, (group + 1) * GROUP_ROWS))
     for group in range(GROUPS_HERE):
         for odd in (0, 1):
@@ -210,7 +214,8 @@
                     imag = more_imag if member == 0 else imag + more_imag
                 start = group * KEPT + tile
                 stages.put(joined, odd, slice(start, start + TILE), real, imag)
-    stages.back(joined, turn_ref, slice(0, GROUPS_HERE * KEPT))
+    for half in range(2):
+        stages.back(joined, turn_ref, slice(half * 2 * KEPT, (half + 1) * 2 * KEPT))
     for group in range(GROUPS_HERE):
         result = stages.leave(turn_ref, group * KEPT)
         wide_lag_ref[0, every(group), :] = result[:, :HALF]
@@ -253,7 +258,9 @@
             axis=1,
         ).astype(jnp.bfloat16)
         stages.enter(taken, taps_pair, group * KEPT)
-    stages.forth(taps_pair, spec_taps_ref, slice(0, GROUPS_HERE * KEPT))
+    size = GROUPS_HERE * KEPT // 2
+    for part in range(2):
+        stages.forth(taps_pair, spec_taps_ref, slice(part * size, (part + 1) * size))
 
     def multiply(group):
         for odd in (0, 1):
@@ -273,7 +280,10 @@
                     )
 
     def back(group):
-        stages.back(pair, turn_ref, slice(group * GROUP_ROWS, (group + 1) * GROUP_ROWS))
+        size = GROUP_ROWS // 1
+        for part in range(1):
+            start = group * GROUP_ROWS + part * size
+            stages.back(pair, turn_ref, slice(start, start + size))
 
     def leave(group):
         for item in range(PAIRS):
@@ -286,10 +296,9 @@
                     result[:, part * HALF : (part + 1) * HALF] + direct
                 )
 
-    for step in range(GROUPS_HERE + 2):
-        for lag, stage in enumerate((multiply, back, leave)):
-            if 0 <= step - lag < GROUPS_HERE:
-                stage(step - lag)
+    for stage in (multiply, back, leave):
+        for group in range(GROUPS_HERE):
+            stage(group)
     for lane in range(4):
         send_ref[:, :, lane * HALF : (lane + 1) * HALF] = gather(wide_out_ref, lane)
 

time: 81.1 us -> 80.8 us (level)
  transfers between devices with their start and end apart: 1 -> 1, of which waited for: 0 -> 0; matrix products, arithmetic and copies ran while one was open for 0% -> 0% of each run, Pallas kernels for 4% -> 3%
where the time goes in v7:
time: 80.8 us; the launch traced here: 79.6 us
  blocking collectives  69 us (85%)
  Pallas kernels  9.02 us (11%)
  between operations  0.81 us (1%)
    all_to_all x2, blocking collectives, exchange(): return lax.all_to_all(value, axis, split_axis=0, concat_axis=0, tiled=True)  69 us
    pallas_call x1, Pallas kernels, spectral(): pl.pallas_call(signal_kernel, out_shape=jax.ShapeDtypeStruct((BLOCKS, SIG...  2.61 us
    pallas_call x1, Pallas kernels, gated_chunks(): pl.pallas_call(gate_kernel, out_shape=jax.ShapeDtypeStruct((RING, RING, S...  2.4 us
    pallas_call x1, Pallas kernels, spectral(): pl.pallas_call(lag_kernel, out_shape=(jax.ShapeDtypeStruct((BLOCKS, SIGNA...  2.05 us
    pallas_call x1, Pallas kernels, outcomes(): pl.pallas_call(functools.partial(outcome_kernel, scale), out_shape=(signa...  1.96 us
  transfers between devices with their start and end apart: 1, of which 0 were waited for; matrix products, arithmetic and copies ran while one was open for 0% of the time, Pallas kernels for 3%

profile of v7, /device:TPU:6, one launch (start us, length us, event | category | flops | bytes accessed | tf_op | source)
XLA Modules:
  0.0 79.6 jit_solution(9002969807023812347)
XLA Ops:
  0.6 0.0 copy-start.5
  0.6 0.0 copy-start.6
  0.7 0.0 copy-start.7
  0.7 0.0 copy-start.8
  0.7 0.0 copy-start.9
  0.7 0.0 copy-start.10
  0.7 2.4 %gates.1 = bf16[8,8,8,640]{3,2,1,0:T(8,128)(2,1)S(1)} custom-call(bf16[256,2,256]{2,1,0:T(2,128)(2,1)} %out_gate_ref.3, bf16[256,2,256]{2,1,0:T(2,128)(2,1)} %in_gate_ref.3, bf16[256,2,256]{2,1,0:T(2,128)(2,1)} %values_ref.3, bf16[256,256]{1,0:T(8,128)(2,1)} %taps_ref.1, bf16[256,2,256]{2,1,0:T(2,128)(2,1)} %cot_ref.3), custom_call_target="tpu_custom_call" | custom-call | flops 400000000 | bytes 2000000 | tf_op jit(solution)/shard_map/gates/pallas_call | solution.py:443
  3.1 30.8 %all_to_all.10.recv_ref = bf16[64,8,640]{2,1,0:T(8,128)(2,1)S(1)} all-to-all(bf16[64,8,640]{2,1,0:T(8,128)(2,1)S(1)} %bitcast.3), channel_id=1, replica_groups=mesh['seq'=64,'chan'=8] {'seq'}, dimensions={0} | all-to-all | bytes 1310720 | tf_op jit(solution)/shard_map/all_to_all | solution.py:559
  33.9 0.0 copy-done.5
  33.9 0.0 copy-done.6
  33.9 0.0 copy-done.7
  33.9 0.0 copy-done.8
  33.9 0.0 copy-done.9
  33.9 0.0 copy-done.10
  33.9 0.0 copy-start.4
  34.0 2.1 %lags.1 = (bf16[64,8,128]{2,1,0:T(8,128)(2,1)S(1)}, f32[2,1024,256]{2,1,0:T(8,128)S(1)}, f32[4,512,128]{2,1,0:T(8,128)S(1)}) custom-call(bf16[64,8,640]{2,1,0:T(8,128)(2,1)S(1)} %all_to_all.10.recv_ref, bf16[128,128]{1,0:T(8,128)(2,1)S(1)} %copy-done.10, bf16[128,256]{1,0:T(8,128)(2,1)S(1)} %copy-done.9, f32[64,256]{1,0:T(8,128)S(1)} %copy-done.8, ...), custom_call_target="tpu_custom_call" | custom-call | flops 3000000000 | bytes 5000000 | tf_op jit(solution)/shard_map/lags/pallas_call | solution.py:311
  36.0 0.7 collective-permute-start
  36.7 0.0 copy-done.4
  36.7 2.6 %signals.1 = bf16[64,8,512]{2,1,0:T(8,128)(2,1)S(1)} custom-call(f32[2,256]{1,0:T(2,128)S(1)} %copy-done.4, bf16[64,8,640]{2,1,0:T(8,128)(2,1)S(1)} %all_to_all.10.recv_ref, f32[2,1024,256]{2,1,0:T(8,128)S(1)} %get-tuple-element.13.spec_ref, f32[4,512,128]{2,1,0:T(8,128)S(1)} %get-tuple-element.14.wide_ref, bf16[128,128]{1,0:T(8,128)(2,1)S(1)} %copy-done.10, ...), custom_call_target="tpu_custom_call" | custom-call | flops 3000000000 | bytes 5000000 | tf_op jit(solution)/shard_map/signals/pallas_call | solution.py:335
  39.3 0.0 copy-start
  39.3 0.0 copy-start.1
  39.3 0.0 copy-start.2
  39.4 0.0 copy-start.3
  39.4 0.0 collective-permute-done
  39.4 0.1 pad_maximum_fusion
  39.4 38.2 %all_to_all.11 = bf16[64,8,640]{2,1,0:T(8,128)(2,1)S(1)} all-to-all(bf16[64,8,640]{2,1,0:T(8,128)(2,1)S(1)} %pad_maximum_fusion), channel_id=1, replica_groups=mesh['seq'=64,'chan'=8] {'seq'}, dimensions={0} | all-to-all | bytes 1310720 | tf_op jit(solution)/shard_map/all_to_all | solution.py:559
  77.6 0.0 copy-done
  77.6 0.0 copy-done.1
  77.6 0.0 copy-done.2
  77.6 0.0 copy-done.3
  77.6 2.0 %outcomes.1 = (bf16[256,2,256]{2,1,0:T(2,128)(2,1)}, bf16[256,2,256]{2,1,0:T(2,128)(2,1)}, bf16[256,2,256]{2,1,0:T(2,128)(2,1)}, bf16[256,2,256]{2,1,0:T(2,128)(2,1)}, f32[32,256]{1,0:T(8,128)}) custom-call(bf16[8,8,8,640]{3,2,1,0:T(8,128)(2,1)S(1)} %bitcast.4, bf16[256,2,256]{2,1,0:T(2,128)(2,1)S(1)} %copy-done, bf16[256,2,256]{2,1,0:T(2,128)(2,1)S(1)} %copy-done.1, ...), custom_call_target="tpu_custom_call" | custom-call | flops 400000000 | bytes 3000000 | tf_op jit(solution)/shard_map/outcomes/pallas_call | solution.py:538
Async XLA Ops:
  0.6 33.3 %copy-start.5 = (bf16[2,768,256]{2,1,0:T(8,128)(2,1)S(1)}, bf16[2,768,256]{2,1,0:T(8,128)(2,1)}, u32[]{:S(2)}) copy-start(bf16[2,768,256]{2,1,0:T(8,128)(2,1)} %constant.17.clone.back_ref) | copy-start | bytes 2359300
  0.6 33.3 %copy-start.6 = (bf16[2,768,256]{2,1,0:T(8,128)(2,1)S(1)}, bf16[2,768,256]{2,1,0:T(8,128)(2,1)}, u32[]{:S(2)}) copy-start(bf16[2,768,256]{2,1,0:T(8,128)(2,1)} %constant.16.clone.forth_ref) | copy-start | bytes 2359300
  0.7 33.3 %copy-start.7 = (f32[64,256]{1,0:T(8,128)S(1)}, f32[64,256]{1,0:T(8,128)}, u32[]{:S(2)}) copy-start(f32[64,256]{1,0:T(8,128)} %constant.15.clone.sin_ref) | copy-start | bytes 196612
  0.7 33.2 %copy-start.8 = (f32[64,256]{1,0:T(8,128)S(1)}, f32[64,256]{1,0:T(8,128)}, u32[]{:S(2)}) copy-start(f32[64,256]{1,0:T(8,128)} %constant.14.clone.cos_ref) | copy-start | bytes 196612
  0.7 33.2 %copy-start.9 = (bf16[128,256]{1,0:T(8,128)(2,1)S(1)}, bf16[128,256]{1,0:T(8,128)(2,1)}, u32[]{:S(2)}) copy-start(bf16[128,256]{1,0:T(8,128)(2,1)} %constant.13.clone.leave_ref) | copy-start | bytes 196612
  0.7 33.2 %copy-start.10 = (bf16[128,128]{1,0:T(8,128)(2,1)S(1)}, bf16[128,128]{1,0:T(8,128)(2,1)}, u32[]{:S(2)}) copy-start(bf16[128,128]{1,0:T(8,128)(2,1)} %constant.12.clone.enter_ref) | copy-start | bytes 98308
  33.9 2.8 %copy-start.4 = (f32[2,256]{1,0:T(2,128)S(1)}, f32[2,256]{1,0:T(2,128)}, u32[]{:S(2)}) copy-start(f32[2,256]{1,0:T(2,128)} %skip_ref.1) | copy-start | bytes 6148
  36.0 3.4 %collective-permute-start = (bf16[64,8,128]{2,1,0:T(8,128)(2,1)S(1)}, bf16[64,8,128]{2,1,0:T(8,128)(2,1)S(1)}, u32[]{:S(2)}, u32[]{:S(2)}) collective-permute-start(bf16[64,8,128]{2,1,0:T(8,128)(2,1)S(1)} %get-tuple-element.15), channel_id=1, source_target_pairs={{0,0},{1,1},{2,2},{3,3},{4,4},{5,5},{6,6},{7,7},{8,12},{9,13},{10,... | collective-permute-start | bytes 393224 | tf_op jit(solution)/shard_map/ppermute | solution.py:576
  39.3 38.3 %copy-start = (bf16[256,2,256]{2,1,0:T(2,128)(2,1)S(1)}, bf16[256,2,256]{2,1,0:T(2,128)(2,1)}, u32[]{:S(2)}) copy-start(bf16[256,2,256]{2,1,0:T(2,128)(2,1)} %out_gate_ref.3) | copy-start | bytes 786436
  39.3 38.3 %copy-start.1 = (bf16[256,2,256]{2,1,0:T(2,128)(2,1)S(1)}, bf16[256,2,256]{2,1,0:T(2,128)(2,1)}, u32[]{:S(2)}) copy-start(bf16[256,2,256]{2,1,0:T(2,128)(2,1)} %in_gate_ref.3) | copy-start | bytes 786436
  39.3 38.3 %copy-start.2 = (bf16[256,2,256]{2,1,0:T(2,128)(2,1)S(1)}, bf16[256,2,256]{2,1,0:T(2,128)(2,1)}, u32[]{:S(2)}) copy-start(bf16[256,2,256]{2,1,0:T(2,128)(2,1)} %values_ref.3) | copy-start | bytes 786436
  39.4 38.3 %copy-start.3 = (bf16[256,2,256]{2,1,0:T(2,128)(2,1)S(1)}, bf16[256,2,256]{2,1,0:T(2,128)(2,1)}, u32[]{:S(2)}) copy-start(bf16[256,2,256]{2,1,0:T(2,128)(2,1)} %cot_ref.3) | copy-start | bytes 786436

commit v8 on v7

--- a/solution.py
+++ b/solution.py
@@ -366,13 +366,13 @@
 def position():
     seat, plane = lax.axis_index("seq"), lax.axis_index("chan")
     row, column = lax.div(seat, RING), lax.rem(seat, RING)
-    held = lax.rem(plane + row + RING // 2 * lax.rem(column, 2), RING) * RING + column
+    held = lax.rem(RING - plane + row + RING // 2 * lax.rem(column, 2), RING) * RING + column
     return plane, held
 
 
 def holders(plane):
     return [
-        [lax.rem(first - RING // 2 * odd + 2 * RING - plane, RING) for odd in (0, 1)]
+        [lax.rem(first - RING // 2 * odd + RING + plane, RING) for odd in (0, 1)]
         for first in range(RING)
     ]
 
@@ -567,7 +567,7 @@
         pairs = [
             (
                 (first * RING + second) * RING + level,
-                (first * RING + second) * RING + (level + shift(first, second)) % RING,
+                (first * RING + second) * RING + (shift(first, second) - level) % RING,
             )
             for first in range(RING)
             for second in range(RING)

time: 80.8 us -> 80.9 us (level)
  no operation moved by 1% of the time
where the time goes in v8:
time: 80.9 us; the launch traced here: 79.7 us
  blocking collectives  69.1 us (85%)
  Pallas kernels  9.02 us (11%)
  between operations  0.81 us (1%)
    all_to_all x2, blocking collectives, exchange(): return lax.all_to_all(value, axis, split_axis=0, concat_axis=0, tiled=True)  69.1 us
    pallas_call x1, Pallas kernels, spectral(): pl.pallas_call(signal_kernel, out_shape=jax.ShapeDtypeStruct((BLOCKS, SIG...  2.61 us
    pallas_call x1, Pallas kernels, gated_chunks(): pl.pallas_call(gate_kernel, out_shape=jax.ShapeDtypeStruct((RING, RING, S...  2.4 us
    pallas_call x1, Pallas kernels, spectral(): pl.pallas_call(lag_kernel, out_shape=(jax.ShapeDtypeStruct((BLOCKS, SIGNA...  2.05 us
    pallas_call x1, Pallas kernels, outcomes(): pl.pallas_call(functools.partial(outcome_kernel, scale), out_shape=(signa...  1.96 us
  transfers between devices with their start and end apart: 1, of which 0 were waited for; matrix products, arithmetic and copies ran while one was open for 0% of the time, Pallas kernels for 3%

profile of v8, /device:TPU:6, one launch (start us, length us, event | category | flops | bytes accessed | tf_op | source)
XLA Modules:
  0.0 79.7 jit_solution(177547549357405935)
XLA Ops:
  0.6 0.0 copy-start.5
  0.6 0.0 copy-start.6
  0.7 0.0 copy-start.7
  0.7 0.0 copy-start.8
  0.7 0.0 copy-start.9
  0.7 0.0 copy-start.10
  0.7 2.4 %gates.1 = bf16[8,8,8,640]{3,2,1,0:T(8,128)(2,1)S(1)} custom-call(bf16[256,2,256]{2,1,0:T(2,128)(2,1)} %out_gate_ref.3, bf16[256,2,256]{2,1,0:T(2,128)(2,1)} %in_gate_ref.3, bf16[256,2,256]{2,1,0:T(2,128)(2,1)} %values_ref.3, bf16[256,256]{1,0:T(8,128)(2,1)} %taps_ref.1, bf16[256,2,256]{2,1,0:T(2,128)(2,1)} %cot_ref.3), custom_call_target="tpu_custom_call" | custom-call | flops 400000000 | bytes 2000000 | tf_op jit(solution)/shard_map/gates/pallas_call | solution.py:443
  3.1 30.8 %all_to_all.10.recv_ref = bf16[64,8,640]{2,1,0:T(8,128)(2,1)S(1)} all-to-all(bf16[64,8,640]{2,1,0:T(8,128)(2,1)S(1)} %bitcast.3), channel_id=1, replica_groups=mesh['seq'=64,'chan'=8] {'seq'}, dimensions={0} | all-to-all | bytes 1310720 | tf_op jit(solution)/shard_map/all_to_all | solution.py:559
  33.9 0.0 copy-done.5
  33.9 0.0 copy-done.6
  33.9 0.0 copy-done.7
  33.9 0.0 copy-done.8
  33.9 0.0 copy-done.9
  33.9 0.0 copy-done.10
  33.9 0.0 copy-start.4
  34.0 2.1 %lags.1 = (bf16[64,8,128]{2,1,0:T(8,128)(2,1)S(1)}, f32[2,1024,256]{2,1,0:T(8,128)S(1)}, f32[4,512,128]{2,1,0:T(8,128)S(1)}) custom-call(bf16[64,8,640]{2,1,0:T(8,128)(2,1)S(1)} %all_to_all.10.recv_ref, bf16[128,128]{1,0:T(8,128)(2,1)S(1)} %copy-done.10, bf16[128,256]{1,0:T(8,128)(2,1)S(1)} %copy-done.9, f32[64,256]{1,0:T(8,128)S(1)} %copy-done.8, ...), custom_call_target="tpu_custom_call" | custom-call | flops 3000000000 | bytes 5000000 | tf_op jit(solution)/shard_map/lags/pallas_call | solution.py:311
  36.0 0.7 collective-permute-start
  36.7 0.0 copy-done.4
  36.7 2.6 %signals.1 = bf16[64,8,512]{2,1,0:T(8,128)(2,1)S(1)} custom-call(f32[2,256]{1,0:T(2,128)S(1)} %copy-done.4, bf16[64,8,640]{2,1,0:T(8,128)(2,1)S(1)} %all_to_all.10.recv_ref, f32[2,1024,256]{2,1,0:T(8,128)S(1)} %get-tuple-element.13.spec_ref, f32[4,512,128]{2,1,0:T(8,128)S(1)} %get-tuple-element.14.wide_ref, bf16[128,128]{1,0:T(8,128)(2,1)S(1)} %copy-done.10, ...), custom_call_target="tpu_custom_call" | custom-call | flops 3000000000 | bytes 5000000 | tf_op jit(solution)/shard_map/signals/pallas_call | solution.py:335
  39.3 0.0 copy-start
  39.3 0.0 copy-start.1
  39.3 0.0 copy-start.2
  39.4 0.0 copy-start.3
  39.4 0.0 collective-permute-done
  39.4 0.1 pad_maximum_fusion
  39.4 38.3 %all_to_all.11 = bf16[64,8,640]{2,1,0:T(8,128)(2,1)S(1)} all-to-all(bf16[64,8,640]{2,1,0:T(8,128)(2,1)S(1)} %pad_maximum_fusion), channel_id=1, replica_groups=mesh['seq'=64,'chan'=8] {'seq'}, dimensions={0} | all-to-all | bytes 1310720 | tf_op jit(solution)/shard_map/all_to_all | solution.py:559
  77.8 0.0 copy-done
  77.8 0.0 copy-done.1
  77.8 0.0 copy-done.2
  77.8 0.0 copy-done.3
  77.8 2.0 %outcomes.1 = (bf16[256,2,256]{2,1,0:T(2,128)(2,1)}, bf16[256,2,256]{2,1,0:T(2,128)(2,1)}, bf16[256,2,256]{2,1,0:T(2,128)(2,1)}, bf16[256,2,256]{2,1,0:T(2,128)(2,1)}, f32[32,256]{1,0:T(8,128)}) custom-call(bf16[8,8,8,640]{3,2,1,0:T(8,128)(2,1)S(1)} %bitcast.4, bf16[256,2,256]{2,1,0:T(2,128)(2,1)S(1)} %copy-done, bf16[256,2,256]{2,1,0:T(2,128)(2,1)S(1)} %copy-done.1, ...), custom_call_target="tpu_custom_call" | custom-call | flops 400000000 | bytes 3000000 | tf_op jit(solution)/shard_map/outcomes/pallas_call | solution.py:538
Async XLA Ops:
  0.6 33.3 %copy-start.5 = (bf16[2,768,256]{2,1,0:T(8,128)(2,1)S(1)}, bf16[2,768,256]{2,1,0:T(8,128)(2,1)}, u32[]{:S(2)}) copy-start(bf16[2,768,256]{2,1,0:T(8,128)(2,1)} %constant.17.clone.back_ref) | copy-start | bytes 2359300
  0.6 33.3 %copy-start.6 = (bf16[2,768,256]{2,1,0:T(8,128)(2,1)S(1)}, bf16[2,768,256]{2,1,0:T(8,128)(2,1)}, u32[]{:S(2)}) copy-start(bf16[2,768,256]{2,1,0:T(8,128)(2,1)} %constant.16.clone.forth_ref) | copy-start | bytes 2359300
  0.7 33.3 %copy-start.7 = (f32[64,256]{1,0:T(8,128)S(1)}, f32[64,256]{1,0:T(8,128)}, u32[]{:S(2)}) copy-start(f32[64,256]{1,0:T(8,128)} %constant.15.clone.sin_ref) | copy-start | bytes 196612
  0.7 33.2 %copy-start.8 = (f32[64,256]{1,0:T(8,128)S(1)}, f32[64,256]{1,0:T(8,128)}, u32[]{:S(2)}) copy-start(f32[64,256]{1,0:T(8,128)} %constant.14.clone.cos_ref) | copy-start | bytes 196612
  0.7 33.2 %copy-start.9 = (bf16[128,256]{1,0:T(8,128)(2,1)S(1)}, bf16[128,256]{1,0:T(8,128)(2,1)}, u32[]{:S(2)}) copy-start(bf16[128,256]{1,0:T(8,128)(2,1)} %constant.13.clone.leave_ref) | copy-start | bytes 196612
  0.7 33.2 %copy-start.10 = (bf16[128,128]{1,0:T(8,128)(2,1)S(1)}, bf16[128,128]{1,0:T(8,128)(2,1)}, u32[]{:S(2)}) copy-start(bf16[128,128]{1,0:T(8,128)(2,1)} %constant.12.clone.enter_ref) | copy-start | bytes 98308
  33.9 2.8 %copy-start.4 = (f32[2,256]{1,0:T(2,128)S(1)}, f32[2,256]{1,0:T(2,128)}, u32[]{:S(2)}) copy-start(f32[2,256]{1,0:T(2,128)} %skip_ref.1) | copy-start | bytes 6148
  36.0 3.4 %collective-permute-start = (bf16[64,8,128]{2,1,0:T(8,128)(2,1)S(1)}, bf16[64,8,128]{2,1,0:T(8,128)(2,1)S(1)}, u32[]{:S(2)}, u32[]{:S(2)}) collective-permute-start(bf16[64,8,128]{2,1,0:T(8,128)(2,1)S(1)} %get-tuple-element.15), channel_id=1, source_target_pairs={{0,0},{1,7},{2,6},{3,5},{4,4},{5,3},{6,2},{7,1},{8,12},{9,11},{10,... | collective-permute-start | bytes 393224 | tf_op jit(solution)/shard_map/ppermute | solution.py:576
  39.3 38.5 %copy-start = (bf16[256,2,256]{2,1,0:T(2,128)(2,1)S(1)}, bf16[256,2,256]{2,1,0:T(2,128)(2,1)}, u32[]{:S(2)}) copy-start(bf16[256,2,256]{2,1,0:T(2,128)(2,1)} %out_gate_ref.3) | copy-start | bytes 786436
  39.3 38.4 %copy-start.1 = (bf16[256,2,256]{2,1,0:T(2,128)(2,1)S(1)}, bf16[256,2,256]{2,1,0:T(2,128)(2,1)}, u32[]{:S(2)}) copy-start(bf16[256,2,256]{2,1,0:T(2,128)(2,1)} %in_gate_ref.3) | copy-start | bytes 786436
  39.3 38.4 %copy-start.2 = (bf16[256,2,256]{2,1,0:T(2,128)(2,1)S(1)}, bf16[256,2,256]{2,1,0:T(2,128)(2,1)}, u32[]{:S(2)}) copy-start(bf16[256,2,256]{2,1,0:T(2,128)(2,1)} %values_ref.3) | copy-start | bytes 786436
  39.4 38.4 %copy-start.3 = (bf16[256,2,256]{2,1,0:T(2,128)(2,1)S(1)}, bf16[256,2,256]{2,1,0:T(2,128)(2,1)}, u32[]{:S(2)}) copy-start(bf16[256,2,256]{2,1,0:T(2,128)(2,1)} %cot_ref.3) | copy-start | bytes 786436

commit v9 on v8

--- a/solution.py
+++ b/solution.py
@@ -280,8 +280,8 @@
                     )
 
     def back(group):
-        size = GROUP_ROWS // 1
-        for part in range(1):
+        size = GROUP_ROWS // 2
+        for part in range(2):
             start = group * GROUP_ROWS + part * size
             stages.back(pair, turn_ref, slice(start, start + size))
 

time: 80.9 us -> 80.9 us (level)
  no operation moved by 1% of the time
where the time goes in v9:
time: 80.9 us; the launch traced here: 79.7 us
  blocking collectives  69 us (85%)
  Pallas kernels  9.08 us (11%)
  between operations  0.81 us (1%)
    all_to_all x2, blocking collectives, exchange(): return lax.all_to_all(value, axis, split_axis=0, concat_axis=0, tiled=True)  69 us
    pallas_call x1, Pallas kernels, spectral(): pl.pallas_call(signal_kernel, out_shape=jax.ShapeDtypeStruct((BLOCKS, SIG...  2.67 us
    pallas_call x1, Pallas kernels, gated_chunks(): pl.pallas_call(gate_kernel, out_shape=jax.ShapeDtypeStruct((RING, RING, S...  2.4 us
    pallas_call x1, Pallas kernels, spectral(): pl.pallas_call(lag_kernel, out_shape=(jax.ShapeDtypeStruct((BLOCKS, SIGNA...  2.05 us
    pallas_call x1, Pallas kernels, outcomes(): pl.pallas_call(functools.partial(outcome_kernel, scale), out_shape=(signa...  1.96 us
  transfers between devices with their start and end apart: 1, of which 0 were waited for; matrix products, arithmetic and copies ran while one was open for 0% of the time, Pallas kernels for 3%

profile of v9, /device:TPU:6, one launch (start us, length us, event | category | flops | bytes accessed | tf_op | source)
XLA Modules:
  0.0 79.7 jit_solution(16273582031136153331)
XLA Ops:
  0.6 0.0 copy-start.5
  0.6 0.0 copy-start.6
  0.7 0.0 copy-start.7
  0.7 0.0 copy-start.8
  0.7 0.0 copy-start.9
  0.7 0.0 copy-start.10
  0.7 2.4 %gates.1 = bf16[8,8,8,640]{3,2,1,0:T(8,128)(2,1)S(1)} custom-call(bf16[256,2,256]{2,1,0:T(2,128)(2,1)} %out_gate_ref.3, bf16[256,2,256]{2,1,0:T(2,128)(2,1)} %in_gate_ref.3, bf16[256,2,256]{2,1,0:T(2,128)(2,1)} %values_ref.3, bf16[256,256]{1,0:T(8,128)(2,1)} %taps_ref.1, bf16[256,2,256]{2,1,0:T(2,128)(2,1)} %cot_ref.3), custom_call_target="tpu_custom_call" | custom-call | flops 400000000 | bytes 2000000 | tf_op jit(solution)/shard_map/gates/pallas_call | solution.py:443
  3.1 30.8 %all_to_all.10.recv_ref = bf16[64,8,640]{2,1,0:T(8,128)(2,1)S(1)} all-to-all(bf16[64,8,640]{2,1,0:T(8,128)(2,1)S(1)} %bitcast.3), channel_id=1, replica_groups=mesh['seq'=64,'chan'=8] {'seq'}, dimensions={0} | all-to-all | bytes 1310720 | tf_op jit(solution)/shard_map/all_to_all | solution.py:559
  33.9 0.0 copy-done.5
  33.9 0.0 copy-done.6
  33.9 0.0 copy-done.7
  33.9 0.0 copy-done.8
  33.9 0.0 copy-done.9
  33.9 0.0 copy-done.10
  33.9 0.0 copy-start.4
  34.0 2.1 %lags.1 = (bf16[64,8,128]{2,1,0:T(8,128)(2,1)S(1)}, f32[2,1024,256]{2,1,0:T(8,128)S(1)}, f32[4,512,128]{2,1,0:T(8,128)S(1)}) custom-call(bf16[64,8,640]{2,1,0:T(8,128)(2,1)S(1)} %all_to_all.10.recv_ref, bf16[128,128]{1,0:T(8,128)(2,1)S(1)} %copy-done.10, bf16[128,256]{1,0:T(8,128)(2,1)S(1)} %copy-done.9, f32[64,256]{1,0:T(8,128)S(1)} %copy-done.8, ...), custom_call_target="tpu_custom_call" | custom-call | flops 3000000000 | bytes 5000000 | tf_op jit(solution)/shard_map/lags/pallas_call | solution.py:311
  36.0 0.7 collective-permute-start
  36.7 0.0 copy-done.4
  36.7 2.7 %signals.1 = bf16[64,8,512]{2,1,0:T(8,128)(2,1)S(1)} custom-call(f32[2,256]{1,0:T(2,128)S(1)} %copy-done.4, bf16[64,8,640]{2,1,0:T(8,128)(2,1)S(1)} %all_to_all.10.recv_ref, f32[2,1024,256]{2,1,0:T(8,128)S(1)} %get-tuple-element.13.spec_ref, f32[4,512,128]{2,1,0:T(8,128)S(1)} %get-tuple-element.14.wide_ref, bf16[128,128]{1,0:T(8,128)(2,1)S(1)} %copy-done.10, ...), custom_call_target="tpu_custom_call" | custom-call | flops 3000000000 | bytes 5000000 | tf_op jit(solution)/shard_map/signals/pallas_call | solution.py:335
  39.4 0.0 copy-start
  39.4 0.0 copy-start.1
  39.4 0.0 copy-start.2
  39.4 0.0 copy-start.3
  39.4 0.0 collective-permute-done
  39.4 0.1 pad_maximum_fusion
  39.5 38.3 %all_to_all.11 = bf16[64,8,640]{2,1,0:T(8,128)(2,1)S(1)} all-to-all(bf16[64,8,640]{2,1,0:T(8,128)(2,1)S(1)} %pad_maximum_fusion), channel_id=1, replica_groups=mesh['seq'=64,'chan'=8] {'seq'}, dimensions={0} | all-to-all | bytes 1310720 | tf_op jit(solution)/shard_map/all_to_all | solution.py:559
  77.8 0.0 copy-done
  77.8 0.0 copy-done.1
  77.8 0.0 copy-done.2
  77.8 0.0 copy-done.3
  77.8 2.0 %outcomes.1 = (bf16[256,2,256]{2,1,0:T(2,128)(2,1)}, bf16[256,2,256]{2,1,0:T(2,128)(2,1)}, bf16[256,2,256]{2,1,0:T(2,128)(2,1)}, bf16[256,2,256]{2,1,0:T(2,128)(2,1)}, f32[32,256]{1,0:T(8,128)}) custom-call(bf16[8,8,8,640]{3,2,1,0:T(8,128)(2,1)S(1)} %bitcast.4, bf16[256,2,256]{2,1,0:T(2,128)(2,1)S(1)} %copy-done, bf16[256,2,256]{2,1,0:T(2,128)(2,1)S(1)} %copy-done.1, ...), custom_call_target="tpu_custom_call" | custom-call | flops 400000000 | bytes 3000000 | tf_op jit(solution)/shard_map/outcomes/pallas_call | solution.py:538
Async XLA Ops:
  0.6 33.3 %copy-start.5 = (bf16[2,768,256]{2,1,0:T(8,128)(2,1)S(1)}, bf16[2,768,256]{2,1,0:T(8,128)(2,1)}, u32[]{:S(2)}) copy-start(bf16[2,768,256]{2,1,0:T(8,128)(2,1)} %constant.17.clone.back_ref) | copy-start | bytes 2359300
  0.6 33.3 %copy-start.6 = (bf16[2,768,256]{2,1,0:T(8,128)(2,1)S(1)}, bf16[2,768,256]{2,1,0:T(8,128)(2,1)}, u32[]{:S(2)}) copy-start(bf16[2,768,256]{2,1,0:T(8,128)(2,1)} %constant.16.clone.forth_ref) | copy-start | bytes 2359300
  0.7 33.3 %copy-start.7 = (f32[64,256]{1,0:T(8,128)S(1)}, f32[64,256]{1,0:T(8,128)}, u32[]{:S(2)}) copy-start(f32[64,256]{1,0:T(8,128)} %constant.15.clone.sin_ref) | copy-start | bytes 196612
  0.7 33.2 %copy-start.8 = (f32[64,256]{1,0:T(8,128)S(1)}, f32[64,256]{1,0:T(8,128)}, u32[]{:S(2)}) copy-start(f32[64,256]{1,0:T(8,128)} %constant.14.clone.cos_ref) | copy-start | bytes 196612
  0.7 33.2 %copy-start.9 = (bf16[128,256]{1,0:T(8,128)(2,1)S(1)}, bf16[128,256]{1,0:T(8,128)(2,1)}, u32[]{:S(2)}) copy-start(bf16[128,256]{1,0:T(8,128)(2,1)} %constant.13.clone.leave_ref) | copy-start | bytes 196612
  0.7 33.2 %copy-start.10 = (bf16[128,128]{1,0:T(8,128)(2,1)S(1)}, bf16[128,128]{1,0:T(8,128)(2,1)}, u32[]{:S(2)}) copy-start(bf16[128,128]{1,0:T(8,128)(2,1)} %constant.12.clone.enter_ref) | copy-start | bytes 98308
  33.9 2.8 %copy-start.4 = (f32[2,256]{1,0:T(2,128)S(1)}, f32[2,256]{1,0:T(2,128)}, u32[]{:S(2)}) copy-start(f32[2,256]{1,0:T(2,128)} %skip_ref.1) | copy-start | bytes 6148
  36.0 3.4 %collective-permute-start = (bf16[64,8,128]{2,1,0:T(8,128)(2,1)S(1)}, bf16[64,8,128]{2,1,0:T(8,128)(2,1)S(1)}, u32[]{:S(2)}, u32[]{:S(2)}) collective-permute-start(bf16[64,8,128]{2,1,0:T(8,128)(2,1)S(1)} %get-tuple-element.15), channel_id=1, source_target_pairs={{0,0},{1,7},{2,6},{3,5},{4,4},{5,3},{6,2},{7,1},{8,12},{9,11},{10,... | collective-permute-start | bytes 393224 | tf_op jit(solution)/shard_map/ppermute | solution.py:576
  39.4 38.4 %copy-start = (bf16[256,2,256]{2,1,0:T(2,128)(2,1)S(1)}, bf16[256,2,256]{2,1,0:T(2,128)(2,1)}, u32[]{:S(2)}) copy-start(bf16[256,2,256]{2,1,0:T(2,128)(2,1)} %out_gate_ref.3) | copy-start | bytes 786436
  39.4 38.4 %copy-start.1 = (bf16[256,2,256]{2,1,0:T(2,128)(2,1)S(1)}, bf16[256,2,256]{2,1,0:T(2,128)(2,1)}, u32[]{:S(2)}) copy-start(bf16[256,2,256]{2,1,0:T(2,128)(2,1)} %in_gate_ref.3) | copy-start | bytes 786436
  39.4 38.4 %copy-start.2 = (bf16[256,2,256]{2,1,0:T(2,128)(2,1)S(1)}, bf16[256,2,256]{2,1,0:T(2,128)(2,1)}, u32[]{:S(2)}) copy-start(bf16[256,2,256]{2,1,0:T(2,128)(2,1)} %values_ref.3) | copy-start | bytes 786436
  39.4 38.4 %copy-start.3 = (bf16[256,2,256]{2,1,0:T(2,128)(2,1)S(1)}, bf16[256,2,256]{2,1,0:T(2,128)(2,1)}, u32[]{:S(2)}) copy-start(bf16[256,2,256]{2,1,0:T(2,128)(2,1)} %cot_ref.3) | copy-start | bytes 786436
